TPU v7x, 32 devices: a whole 2x2x4 slice. The times are simulated.
32 devices in a mesh: ctx: 16 (over z, y, x), head: 2 (over core).
Axes of the slice: x: 2, y: 2, z: 4, core: 2. Of those that a mesh axis runs over, the one named last changes fastest.
Arguments:
- query_proj: bfloat16 [2048, 2048], P('ctx', 'head'), may hold values from -6 to 6
- key_proj: bfloat16 [2048, 2048], P('ctx', 'head'), may hold values from -6 to 6
- value_proj: bfloat16 [2048, 4096], P('ctx', 'head'), may hold values from -6 to 6
- gate_proj: bfloat16 [2048, 4096], P('ctx', 'head'), may hold values from -6 to 6
- write_strength: float32 [2048, 32], P('ctx', 'head'), may hold values from 0 to 1
- log_decay: float32 [2048, 32], P('ctx', 'head'), may hold values from -1 to 0
- norm_gain: float32 [128], replicated, may hold values from 0.1 to 1.9
- out_weight: bfloat16 [4096, 2048], P('head'), may hold values from -0.125 to 0.125
Outputs:
- layer_out: bfloat16 [2048, 2048], P('ctx', 'head')
All inputs are finite; a program needn't handle non-finite values.
Results may differ from a plain program's by a relative error of at most 0.017.
Values may be sent and summed in bfloat16 or wider, within the bound.
No kernel may reach another device: no remote copies, remote signals or barrier semaphores. Data moves between devices by JAX's collectives and lax.ppermute only.
A program may use at most 128 MiB of HBM per device.

v0:
```python
import jax
import jax.numpy as jnp
from jax import lax
from jax.sharding import PartitionSpec as P

HV = 32
HK = 16
DK = 128
DV = 128
SPAN = 64


exact_matmul_mode = lax.Precision.HIGHEST
EPSILON = 1e-06


def carried_in(part, axis, combine, identity):
    place = lax.axis_index(axis)
    gathered = jax.tree.map(lambda a: lax.all_gather(a, axis), part)
    state = jax.tree.map(lambda a, e: jnp.zeros_like(a) + jnp.asarray(e, a.dtype), part, identity)

    def one(turn, state):
        return combine(
            state, jax.tree.map(lambda a: lax.dynamic_index_in_dim(a, turn, 0, False), gathered)
        )

    return lax.fori_loop(0, place, one, state)


def unit_rows(vectors):
    return vectors * lax.rsqrt(jnp.sum(vectors * vectors, axis=-1, keepdims=True) + EPSILON)


def span_terms(queries, keys, values, strength, decays):
    span_len = decays.shape[-1]
    value_width = values.shape[-1]
    key_width = keys.shape[-1]
    cumulative = jnp.cumsum(decays, axis=-1)
    row_index = jnp.arange(span_len)[:, None]
    col_index = jnp.arange(span_len)[None, :]
    strict = col_index < row_index
    inclusive = col_index <= row_index
    log_gaps = cumulative[..., :, None] - cumulative[..., None, :]
    factors = jnp.where(inclusive, jnp.exp(jnp.where(inclusive, log_gaps, 0.0)), 0.0)
    key_products = jnp.einsum("htk,hsk->hts", keys, keys, precision=exact_matmul_mode)
    lower_part = jnp.where(strict, strength[..., :, None] * factors * key_products, 0.0)
    system = jnp.eye(span_len, dtype=jnp.float32) + lower_part
    growth = jnp.exp(cumulative)
    right_side = jnp.concatenate(
        [strength[..., None] * values, (strength * growth)[..., None] * keys], axis=-1
    )
    solved = jax.scipy.linalg.solve_triangular(system, right_side, lower=True, unit_diagonal=True)
    value_slice = solved[..., :value_width]
    key_part = solved[..., value_width:]
    tail_decay = jnp.exp(cumulative[..., -1:] - cumulative)
    trailing_keys = keys * tail_decay[..., None]
    identity_k = jnp.eye(key_width, dtype=jnp.float32)
    state_transfer = growth[..., -1, None, None] * identity_k - jnp.einsum(
        "hsk,hsj->hkj", trailing_keys, key_part, precision=exact_matmul_mode
    )
    start_position = jnp.einsum(
        "nil,nim->nlm", trailing_keys, value_slice, precision=exact_matmul_mode
    )
    scores = jnp.einsum("htk,hsk->hts", queries, keys, precision=exact_matmul_mode) * factors
    within_block_output = jnp.einsum(
        "hts,hsv->htv", scores, value_slice, precision=exact_matmul_mode
    )
    window_rows = growth[..., None] * queries - jnp.einsum(
        "hts,hsk->htk", scores, key_part, precision=exact_matmul_mode
    )
    return (state_transfer, start_position, within_block_output, window_rows)


def gate_norm(output_rows, gate_rows, norm_gain):
    mean_square = jnp.mean(output_rows * output_rows, axis=-1, keepdims=True)
    return output_rows * lax.rsqrt(mean_square + EPSILON) * norm_gain * jax.nn.silu(gate_rows)


def apply_map(per_step_function, desired_value):
    return jnp.einsum("epn,eni->epi", per_step_function, desired_value, precision=exact_matmul_mode)


def combine(earlier, later):
    return (apply_map(later[0], earlier[0]), apply_map(later[0], earlier[1]) + later[1])


def carry_over(device_pair, identity_k, zero_state):
    return carried_in(device_pair, "ctx", combine, (identity_k, zero_state))


def local(
    query_proj, key_proj, value_proj, gate_proj, write_strength, log_decay, norm_gain, out_weight
):
    rows_here = query_proj.shape[0]
    value_heads = value_proj.shape[1] // DV
    key_heads = query_proj.shape[1] // DK
    spans_here = rows_here // SPAN

    def heads_first(array, heads, width):
        shaped = array.reshape(spans_here, SPAN, heads, width).transpose(0, 2, 1, 3)
        return shaped.reshape(spans_here * heads, SPAN, width)

    def small_first(array):
        return (
            array.reshape(spans_here, SPAN, value_heads)
            .transpose(0, 2, 1)
            .reshape(spans_here * value_heads, SPAN)
        )

    queries = unit_rows(query_proj.astype(jnp.float32).reshape(rows_here, key_heads, DK)) * DK ** (
        -0.5
    )
    keys = unit_rows(key_proj.astype(jnp.float32).reshape(rows_here, key_heads, DK))
    queries = heads_first(jnp.repeat(queries, HV // HK, axis=1), value_heads, DK)
    keys = heads_first(jnp.repeat(keys, HV // HK, axis=1), value_heads, DK)
    values = heads_first(value_proj.astype(jnp.float32), value_heads, DV)
    state_transfer, start_position, within_block_output, window_rows = span_terms(
        queries, keys, values, small_first(write_strength), small_first(log_decay)
    )
    state_transfer = state_transfer.reshape(spans_here, value_heads, DK, DK)
    start_position = start_position.reshape(spans_here, value_heads, DK, DV)
    within_block_output = within_block_output.reshape(spans_here, value_heads, SPAN, DV)
    window_rows = window_rows.reshape(spans_here, value_heads, SPAN, DK)
    identity_k = jnp.broadcast_to(jnp.eye(DK, dtype=jnp.float32), (value_heads, DK, DK))
    zero_state = jnp.zeros((value_heads, DK, DV), jnp.float32)

    def compose_only(carry, pieces):
        return ((apply_map(pieces[0], carry[0]), apply_map(pieces[0], carry[1]) + pieces[1]), None)

    device_pair, unused = lax.scan(
        compose_only, (identity_k, zero_state), (state_transfer, start_position)
    )
    carried = carry_over(device_pair, identity_k, zero_state)
    state_in = carried[1]

    def advance(running_state, pieces):
        per_step_function, step_shift, window_extent = pieces
        spare_window = jnp.einsum(
            "lye,lei->lyi", window_extent, running_state, precision=exact_matmul_mode
        )
        return (apply_map(per_step_function, running_state) + step_shift, spare_window)

    final_state, extra = lax.scan(advance, state_in, (state_transfer, start_position, window_rows))
    output_rows = (
        (within_block_output + extra).transpose(0, 2, 1, 3).reshape(rows_here, value_heads, DV)
    )
    gate_rows = gate_proj.astype(jnp.float32).reshape(rows_here, value_heads, DV)
    mixed = (
        gate_norm(output_rows, gate_rows, norm_gain)
        .reshape(rows_here, value_heads * DV)
        .astype(jnp.bfloat16)
    )
    summed = lax.psum_scatter(
        jnp.einsum("fd,tf->dt", out_weight, mixed, preferred_element_type=jnp.float32).astype(
            jnp.bfloat16
        ),
        "head",
        scatter_dimension=0,
        tiled=True,
    ).astype(jnp.float32)
    return summed.T.astype(jnp.bfloat16)


def solution(mesh):
    return jax.shard_map(
        local,
        mesh=mesh,
        in_specs=(
            P("ctx", "head"),
            P("ctx", "head"),
            P("ctx", "head"),
            P("ctx", "head"),
            P("ctx", "head"),
            P("ctx", "head"),
            P(),
            P("head", None),
        ),
        out_specs=P("ctx", "head"),
        check_vma=False,
    )
```

profile of v0, /device:TPU:0, one launch (start us, length us, event | category | flops | bytes accessed | tf_op | source)
XLA Modules:
  0.0 584.8 jit_solution(7867411062587982998)
XLA Ops:
  12.6 1.8 fusion.52
  14.4 2.1 copy.80
  16.5 2.8 fusion.51
  19.3 3.3 copy.77
  22.7 7.4 %add_bitcast_fusion = (f32[32,1,64,64]{0,3,2,1:T(8,128)}, f32[32,64,64]{0,2,1:T(8,128)}) fusion(f32[32,64,64]{0,2,1:T(8,128)S(1)} %copy-done.11, f32[64,64]{1,0:T(8,128)S(1)} %fusion.48, f32[32,64]{0,1:T(8,128)S(1)} %copy.79, f32[64,64]{1,0:T(8,128)S(1)} %get-tuple-element.173, f32[32,64]{0,1:T(8,128)S(1)} %copy.75, ...), kind=kLoop, calls=%fused_computation.32 | loop fusion | flops 1310720 | bytes 2158592 | tf_op jit(solution)/shard_map/jit(_solve_triangular)/vmap()/triangular_solve | solution.py:52
  30.0 68.7 %custom-call.4 = f32[32,1,64,64]{0,2,3,1:T(8,128)} custom-call(f32[32,1,64,64]{0,3,2,1:T(8,128)} %get-tuple-element.165), custom_call_target="InvertDiagBlocksLowerTriangular" | custom-call | tf_op jit(solution)/shard_map/jit(_solve_triangular)/vmap()/triangular_solve | solution.py:52
  98.8 2.9 copy.82
  103.0 1.9 fusion.22
  104.9 5.1 fusion.35
  110.0 4.2 multiply_subtract_fusion
  114.3 10.5 %while.39 = (s32[]{:T(128)}, f32[16,128,128]{2,1,0:T(8,128)S(1)}, f32[16,128,128]{2,1,0:T(8,128)}, f32[2,16,128,128]{3,2,1,0:T(8,128)S(1)}, f32[2,16,128,128]{3,2,1,0:T(8,128)}, /*index=5*/s32[]{:T(128)}, s32[]{:T(128)}) while((s32[]{:T(128)}, f32[16,128,128]{2,1,0:T(8,128)S(1)}, f32[16,128,128]{2,1,0:T(8,128)}, ...), condition=%wide.region_4.5_spmd.clone, body=%wide.region_3.4_spmd.clone.sunk | while | flops 805830656 | bytes 24118936 | solution.py:130
  114.4 1.1 copy-done.5
  116.3 2.1 convolution_add_fusion.8
  118.4 1.2 fusion.88
  119.7 1.1 copy-done.5
  121.5 2.1 convolution_add_fusion.8
  123.6 1.2 fusion.88
  126.0 2.5 copy.83
  128.5 3.5 fusion.37
  132.0 2.3 convolution_subtract_fusion
  134.3 185.0 %all-gather.7.cloned.1.call-done = f32[256,128,128]{2,1,0:T(8,128)} async-done(((f32[16,128,128]{2,1,0:T(8,128)}), f32[256,128,128]{2,1,0:T(8,128)}) %all-gather.7.cloned.1.call-update) | async-done | bytes 16777232 | tf_op jit(solution)/shard_map/all_gather | solution.py:19
  319.3 192.6 %all-gather.5.cloned.1.call-done = f32[256,128,128]{2,1,0:T(8,128)} async-done(((f32[16,128,128]{2,1,0:T(8,128)}), f32[256,128,128]{2,1,0:T(8,128)}) %all-gather.5.cloned.1.call-update) | async-done | bytes 16777232 | tf_op jit(solution)/shard_map/all_gather | solution.py:19
  512.0 7.9 %while.38 = (s32[]{:T(128)}, f32[16,128,128]{2,1,0:T(8,128)S(1)}, f32[2,16,64,128]{3,2,1,0:T(8,128)}, f32[2,16,128,128]{3,2,1,0:T(8,128)S(1)}, f32[2,16,128,128]...) while((s32[]{:T(128)}, f32[16,128,128]{2,1,0:T(8,128)S(1)}, f32[2,16,64,128]{3,2,1,0:T(8,128)}, ...), condition=%wide.region_8.9_spmd, body=%wide.region_7.8_spmd.sunk | while | flops 604241920 | bytes 29362372 | solution.py:143
  512.4 1.1 copy-done.8
  513.9 1.1 fusion.83
  514.9 1.2 convolution_add_fusion.7
  516.2 1.1 copy-done.8
  517.7 1.1 fusion.83
  518.8 1.2 convolution_add_fusion.7
  519.9 1.9 multiply_reduce_fusion
  522.9 6.1 %fusion.21 = bf16[2048,128]{0,1:T(8,128)(2,1)} fusion(bf16[2048,2048]{1,0:T(8,128)(2,1)} %param.21, bf16[128,2048]{1,0:T(8,128)(2,1)S(1)} %copy-done.16, f32[16,8,16,128]{3,2,1,0:T(8,128)S(1)} %bitcast.151, f32[16,8,16,128]{3,2,1,0:T(8,128)S(1)} %bitcast.150, f32[2048]{0:T(1024)S(1)} %broadcast_bitcast_fusion), kind=kOutput, calls=%fused_computation.26 | convolution fusion | flops 1076363264 | bytes 11542528 | tf_op jit(solution)/shard_map/fd,tf->dt/dot_general | solution.py:154
  529.1 49.2 %reduce-scatter.2.cloned.1.call-done = bf16[1024,128]{0,1:T(8,128)(2,1)} async-done(((bf16[2048,128]{0,1:T(8,128)(2,1)}), bf16[1024,128]{0,1:T(8,128)(2,1)}) %reduce-scatter.2.cloned.1.call-update) | async-done | bytes 262160 | tf_op jit(solution)/shard_map/reduce_scatter | solution.py:153
  (99 shorter events, 11.8 us)
Async XLA Ops:
  6.5 122.0 %copy-start = (f32[128]{0:T(128)S(1)}, f32[128]{0:T(128)}, u32[]{:S(2)}) copy-start(f32[128]{0:T(128)} %param.20) | copy-start | bytes 1540
  6.5 312.8 %all-gather.7.cloned.1.call-start = ((), (), s32[]{:S(2)}) async-start(), calls=%async_computation.3 | async-start | bytes 17825792 | tf_op jit(solution)/shard_map/all_gather | solution.py:19
  10.8 1.0 copy-start.15
  11.7 4.8 copy-start.9
  19.3 3.3 copy-start.11
  30.0 71.7 %copy-start.14 = (bf16[128,2048]{1,0:T(8,128)(2,1)S(1)}, bf16[128,2048]{1,0:T(8,128)(2,1)}, u32[]{:S(2)}) copy-start(bf16[128,2048]{1,0:T(8,128)(2,1)} %param.16) | copy-start | bytes 1572868
  104.9 5.1 copy-start.6
  114.3 1.2 copy-start.5
  114.3 1.9 copy-start.2
  119.6 1.2 copy-start.5
  119.6 1.9 copy-start.2
  124.8 1.1 copy-start.4
  124.8 387.1 %all-gather.5.cloned.1.call-start = ((), (), s32[]{:S(2)}) async-start(), calls=%async_computation.2 | async-start | bytes 17825792 | tf_op jit(solution)/shard_map/all_gather | solution.py:19
  125.9 452.4 %reduce-scatter.2.cloned.1.call-start = ((), (), s32[]{:S(2)}) async-start(), calls=%async_computation.1 | async-start | bytes 786432 | tf_op jit(solution)/shard_map/reduce_scatter | solution.py:153
  128.5 3.5 copy-start.7
  128.5 3.5 copy-start.10
  512.3 1.2 copy-start.8
  512.3 1.5 copy-start.12
  512.3 2.6 copy-start.3
  514.9 1.2 copy-start.13
  516.1 1.2 copy-start.8
  516.1 1.5 copy-start.12
  516.2 2.6 copy-start.3
  518.7 1.2 copy-start.13
  521.8 1.1 copy-start.16
  522.9 55.3 %copy-start.1 = (f32[128]{0:T(128)S(1)}, f32[128]{0:T(128)}, u32[]{:S(2)}) copy-start(f32[128]{0:T(128)} %param.20) | copy-start | bytes 1540
Sparse Core Ops, SparseCore 0:
  125.0 194.3 all-gather.6
  322.1 189.7 all-gather.4
  529.2 48.9 reduce-scatter.1
where the time goes:
time: 586 us; the launch traced here: 585 us
  waiting for transfers between devices  427 us (73%)
  other arithmetic  81 us (14%)
  matrix products  38.8 us (7%)
  local copies, waits for them, and re-layouts  24.1 us (4%)
  between operations  13.5 us (2%)
    all_gather x2, waiting for transfers between devices, carried_in(): gathered = jax.tree.map(lambda a: lax.all_gather(a, axis), part)  378 us
    another operation x4, other arithmetic, span_terms(): jax.scipy.linalg.solve_triangular(system, right_side, lower=True, unit_di...  76.1 us
    reduce_scatter x1, waiting for transfers between devices, local(): lax.psum_scatter(jnp.einsum('fd,tf->dt', out_weight, mixed, preferred_ele...  49.2 us
  transfers between devices with their start and end apart: 3, of which 3 were waited for; matrix products, arithmetic and copies ran while one was open for 1% of the time, Pallas kernels for 0%

commit v1 on v0

v1 whole, which is shorter than its diff:
```python
import functools

import jax
import jax.numpy as jnp
from jax import lax
from jax.experimental import pallas as pl
from jax.experimental.pallas import tpu as pltpu
from jax.sharding import PartitionSpec as P

HV = 32
HK = 16
DK = 128
DV = 128
REP = HV // HK
SMALL_BITS = 4
SMALL_ROWS = 1 << SMALL_BITS
CHUNKS = 8
BASE_BITS = 3
BASE = 1 << BASE_BITS
PIECE_ROWS = 8
EPSILON = 1e-06
BF16 = jnp.bfloat16
F32 = jnp.float32


def nn(a, b):
    return lax.dot_general(a, b, (((1,), (0,)), ((), ())), preferred_element_type=F32)


def nt(a, b):
    return lax.dot_general(a, b, (((1,), (1,)), ((), ())), preferred_element_type=F32)


def two_pieces(x):
    high = x.astype(BF16)
    return high, (x - high.astype(F32)).astype(BF16)


def iotas(shape):
    return lax.broadcasted_iota(jnp.int32, shape, 0), lax.broadcasted_iota(jnp.int32, shape, 1)


def triangles(size):
    row, col = iotas((size, size))
    return row, col, (col <= row).astype(BF16), (row <= col).astype(BF16), (row == col).astype(BF16)


def solved(lowers, rights, size):
    count = len(lowers)
    row, col = iotas((size, size))
    place, lane = iotas((BASE, size))
    packed = []
    for low in lowers:
        held = low[0:BASE]
        for b in range(1, size // BASE):
            held = jnp.where(lane >> BASE_BITS == b, low[b * BASE : (b + 1) * BASE], held)
        packed.append(held)
    packed = jnp.concatenate(packed, axis=0).astype(BF16)
    found = [jnp.where(place == (lane & (BASE - 1)), 1.0, 0.0)] * count
    first_col = col & ~(BASE - 1)
    for k in range(BASE - 1):
        spread = jnp.where(row == first_col + k, 1.0, 0.0).astype(BF16)
        column = nn(packed, spread)
        found = [
            x - column[h * BASE : (h + 1) * BASE] * x[k : k + 1] for h, x in enumerate(found)
        ]
    rounded = [low.astype(BF16) for low in lowers]
    step, apart = BASE, row ^ col
    while True:
        pair = 2 * step
        below = jnp.where((apart >= step) & (apart < pair) & (col < row), 1.0, 0.0).astype(BF16)
        diagonal = jnp.where(apart < step, 1.0, 0.0)
        lane = lax.broadcasted_iota(jnp.int32, (step, size), 1)
        even = (lane & step) == 0
        first = [nn(x.astype(BF16), low * below).astype(BF16) for x, low in zip(found, rounded)]
        whole = [
            (jnp.concatenate([x] * (size // step), axis=0) * diagonal).astype(BF16) for x in found
        ]
        if pair == size:
            ends = [nn(w, right) for w, right in zip(whole, rights)]
            fixes = [nn(f, end.astype(BF16)) for f, end in zip(first, ends)]
            return [
                jnp.concatenate([end[:step], end[step:] - fix], axis=0)
                for end, fix in zip(ends, fixes)
            ]
        second = [nn(f, w) for f, w in zip(first, whole)]
        found = [
            jnp.concatenate([jnp.where(even, x, 0.0), jnp.where(even, -y, x)], axis=0)
            for x, y in zip(found, second)
        ]
        step = pair


def decay_gaps(cum_col, cum_row, row, col):
    return jnp.exp(jnp.where(col <= row, cum_col - cum_row, -1e30))


def inverse_norms(gram, row, col):
    diagonal = jnp.where(row == col, gram, 0.0)
    return (
        lax.rsqrt(jnp.sum(diagonal, axis=1, keepdims=True) + EPSILON),
        lax.rsqrt(jnp.sum(diagonal, axis=0, keepdims=True) + EPSILON),
    )


def place_in_group(group):
    return lax.rem(lax.axis_index("ctx"), group)


def pack_kernel(key_hbm, value_hbm, strength_hbm, decay_hbm, *refs):
    group = len(refs) - 6
    out_refs, (rows_ref, held, scalars, small, in_sems, out_sems) = refs[:group], refs[group:]
    tokens = key_hbm.shape[0]
    heads = strength_hbm.shape[0]
    place = place_in_group(group)
    base = (1 + REP) * tokens
    scalar_copies = [
        pltpu.make_async_copy(ref, scalars.at[kind], in_sems.at[group, kind])
        for kind, ref in enumerate((strength_hbm, decay_hbm))
    ]
    arrivals = []
    for s in range(group):
        j = place ^ s
        sources = [key_hbm.at[:, pl.ds(pl.multiple_of(j * DK, DK), DK)]] + [
            value_hbm.at[:, pl.ds(pl.multiple_of((j * REP + r) * DV, DV), DV)] for r in range(REP)
        ]
        arrivals.append(
            [
                pltpu.make_async_copy(
                    source, held.at[s, pl.ds(n * tokens, tokens), :], in_sems.at[s, n]
                )
                for n, source in enumerate(sources)
            ]
        )
    for copy in scalar_copies + sum(arrivals, []):
        copy.start()
    row, col = iotas((SMALL_ROWS * group, 4 * heads))
    slot, target = row & (SMALL_ROWS - 1), row >> SMALL_BITS

    def picked(target):
        pick = jnp.zeros(row.shape, F32)
        for kind in range(2):
            for piece in range(2):
                at = slot - piece * PIECE_ROWS - kind * REP
                wanted = (2 * kind + piece) * heads + target * REP + at
                pick = pick + jnp.where((at >= 0) & (at < REP) & (col == wanted), 1.0, 0.0)
        return pick.astype(BF16)

    picks = picked(target ^ place), picked(target)
    for copy in scalar_copies:
        copy.wait()
    pieces = jnp.concatenate(two_pieces(scalars[0]) + two_pieces(scalars[1]), axis=0)
    sent, natural = [nn(pick, pieces).astype(BF16) for pick in picks]
    if tokens < DK:
        fill = jnp.zeros((sent.shape[0], DK - tokens), BF16)
        sent, natural = [jnp.concatenate([x, fill], axis=1) for x in (sent, natural)]
    small[...] = natural
    departures = [pltpu.make_async_copy(small, rows_ref, out_sems.at[group])]
    departures[0].start()
    for s, out_ref in enumerate(out_refs):
        held[s, base : base + SMALL_ROWS, :] = sent[s * SMALL_ROWS : (s + 1) * SMALL_ROWS, :]
        for copy in arrivals[s]:
            copy.wait()
        departures.append(pltpu.make_async_copy(held.at[s], out_ref, out_sems.at[s]))
        departures[-1].start()
    for copy in departures:
        copy.wait()


def solved_blocks(blocks, small, tokens):
    row, col, lower_ones, upper_ones, eye = triangles(tokens)
    small = small.astype(F32)
    pieces = [
        jnp.concatenate(
            [
                small[b * SMALL_ROWS + start : b * SMALL_ROWS + start + PIECE_ROWS]
                for b in range(len(blocks))
            ],
            axis=0,
        ).astype(BF16)
        for start in (0, PIECE_ROWS)
    ]
    cum_rows = sum(nn(p, upper_ones) for p in pieces)
    plain_cols = sum(nt(eye, p) for p in pieces)
    cum_cols = sum(nt(lower_ones, p) for p in pieces)

    def spread(array, at):
        return jnp.broadcast_to(array[:, at : at + 1], (tokens, DK))

    lowers, rights, works = [], [], []
    for b, (keys, values) in enumerate(blocks):
        gram = nt(keys, keys)
        key_col, key_row = inverse_norms(gram, row, col)
        key_col = jnp.broadcast_to(key_col, (tokens, DK))
        gram = gram * key_row * key_col[:, :tokens]
        unit_keys = keys.astype(F32) * key_col
        for r in range(REP):
            at = b * PIECE_ROWS + r
            strength = spread(plain_cols, at)
            cum_row, cum_col = cum_rows[at + REP : at + REP + 1, :], spread(cum_cols, at + REP)
            factors = decay_gaps(cum_col[:, :tokens], cum_row, row, col)
            lowers.append(jnp.where(col < row, strength[:, :tokens] * factors * gram, 0.0))
            rights.append(
                jnp.concatenate(
                    [
                        (strength * values[r].astype(F32)).astype(BF16),
                        (strength * jnp.exp(cum_col) * unit_keys).astype(BF16),
                    ],
                    axis=1,
                )
            )
            works.append((keys, cum_col, key_col, key_row, factors))
    return solved(lowers, rights, tokens), works


def inside_kernel(query_ref, key_ref, value_ref, rows_ref, *refs, first, shifts=0):
    copies = []
    if shifts:
        weight_hbm, inside_ref, window_ref, early_ref, sems = refs
        target = lax.rem(lax.axis_index("head") + 1, shifts)
        copies = weight_copies(weight_hbm, target, 0, early_ref, sems)
    else:
        inside_ref, window_ref = refs
    tokens = query_ref.shape[0]
    blocks = inside_ref.shape[0] // REP

    def columns(ref, start, size):
        return ref[:, start * size : (start + 1) * size]

    sides, works = solved_blocks(
        [
            (
                columns(key_ref, j, DK),
                [columns(value_ref, j * REP + r, DV) for r in range(REP)],
            )
            for j in range(first, first + blocks)
        ],
        rows_ref[first * SMALL_ROWS : (first + blocks) * SMALL_ROWS, :][:, :tokens],
        tokens,
    )
    for b in range(blocks):
        queries = columns(query_ref, first + b, DK)
        products = nt(queries, works[b * REP][0])
        queries = queries.astype(F32)
        query_col = lax.rsqrt(
            jnp.sum(queries * queries, axis=1, keepdims=True) + EPSILON
        ) * DK**-0.5
        query_col = jnp.broadcast_to(query_col, (tokens, DK))
        queries = queries * query_col
        products = products * works[b * REP][3] * query_col[:, :tokens]
        for r in range(REP):
            at = b * REP + r
            _, cum_col, _, _, factors = works[at]
            scores = (products * factors).astype(BF16)
            both = nn(scores, sides[at].astype(BF16))
            inside_ref[at] = both[:, :DV].astype(BF16)
            window_ref[at] = (jnp.exp(cum_col) * queries - both[:, DV:]).astype(BF16)
    for copy in copies:
        copy.wait()


def in_order(own_half, own, other):
    return jnp.where(own_half == 0, own, other), jnp.where(own_half == 0, other, own)


def half_kernel(*refs, blocks, group, tokens, own, with_map):
    taken, refs = refs[:blocks], refs[blocks:]
    if not own:
        (own_end, own_map), refs = refs[:2], refs[2:]
    before_ref, map_ref, end_ref, end_map_ref, *refs = refs
    if not own:
        group_ref, *refs = refs
        if with_map:
            group_map_ref, *refs = refs
    offsets, removals, decays = refs
    place = place_in_group(group)
    low = lax.rem(place, blocks)
    base = (1 + REP) * tokens
    sides, works = solved_blocks(
        [
            (t[0:tokens, :], [t[(1 + r) * tokens : (2 + r) * tokens, :] for r in range(REP)])
            for t in taken
        ],
        jnp.concatenate([t[base : base + SMALL_ROWS, :][:, :tokens] for t in taken], axis=0),
        tokens,
    )
    for b in range(blocks):
        keys_turned = works[b * REP][0].T
        for r in range(REP):
            at = b * REP + r
            _, cum_col, key_col, _, _ = works[at]
            last = cum_col[tokens - 1 : tokens, :]
            decays[at] = jnp.broadcast_to(jnp.exp(last), (PIECE_ROWS, DK))
            tail = key_col * jnp.exp(last - cum_col)
            tail = jnp.concatenate([tail, tail], axis=1)
            both = nn(keys_turned, (sides[at] * tail).astype(BF16))
            offsets[at] = both[:, :DV]
            removals[at] = both[:, DV:].astype(BF16)

    key_row, key_col = iotas((DK, DK))
    eye = (key_row == key_col).astype(F32)
    states = [None] * REP
    for i in range(blocks):
        following = []
        for r in range(REP):
            at = (low ^ i) * REP + r
            decay = decays[at][0:1, :]
            if i == 0:
                map_ref[at] = eye.astype(BF16)
                before_ref[at] = jnp.zeros((DK, DV), F32)
                following.append(
                    jnp.concatenate(
                        [eye * decay - removals[at].astype(F32), offsets[at]], axis=1
                    )
                )
                continue
            held = states[r].astype(BF16)
            map_ref[at] = held[:, :DK]
            before_ref[at] = states[r][:, DK:]
            moved = nn(removals[at], held)
            following.append(
                jnp.concatenate(
                    [
                        states[r][:, :DK] * decay - moved[:, :DK],
                        states[r][:, DK:] * decay - moved[:, DK:] + offsets[at],
                    ],
                    axis=1,
                )
            )
        states = following
    own_half = place // blocks
    for r in range(REP):
        end_map, end = states[r][:, :DK], states[r][:, DK:]
        end_map_ref[r] = end_map
        end_ref[r] = end
        if not own:
            first_end, second_end = in_order(own_half, own_end[r], end)
            first_map, second_map = in_order(own_half, own_map[r], end_map)
            second_map = second_map.astype(BF16)
            group_ref[r] = (nn(second_map, first_end.astype(BF16)) + second_end).astype(BF16)
            if with_map:
                group_map_ref[r] = nn(second_map, first_map.astype(BF16))


def carry_kernel(
    own_before, own_maps, own_end, own_map, other_before, other_maps, other_end, other_map,
    carried_ref, out_ref, held, sems,
):
    group = held.shape[0]
    half = group // 2
    place = place_in_group(group)
    own_half = place // half
    later_group = lax.axis_index("ctx") >= group
    starts = []
    for r in range(REP):
        carried = jnp.where(later_group, carried_ref[r].astype(F32), 0.0)
        first_end, _ = in_order(own_half, own_end[r], other_end[r])
        first_map, _ = in_order(own_half, own_map[r], other_map[r])
        middle = first_end + nn(first_map.astype(BF16), carried.astype(BF16))
        starts.append([x.astype(BF16) for x in in_order(own_half, carried, middle)])
    copies = []
    for s in range(group):
        before, maps = (own_before, own_maps) if s < half else (other_before, other_maps)
        for r in range(REP):
            at = (s % half) * REP + r
            start = starts[r][0] if s < half else starts[r][1]
            held[s, r * DK : (r + 1) * DK, :] = (before[at] + nn(maps[at], start)).astype(BF16)
        copies.append(pltpu.make_async_copy(held.at[s], out_ref.at[place ^ s], sems.at[s]))
        copies[-1].start()
    for copy in copies:
        copy.wait()


def weight_copies(weight_hbm, target, first, held, sems):
    count, depth, width = held.shape
    columns = pl.ds(pl.multiple_of(target * width, width), width)
    copies = [
        pltpu.make_async_copy(
            weight_hbm.at[pl.ds((first + c) * depth, depth), columns], held.at[c], sems.at[c]
        )
        for c in range(count)
    ]
    for copy in copies:
        copy.start()
    return copies


def project(chunk_of, targets):
    totals = [None] * len(targets)
    for c in range(len(targets[0])):
        rows = chunk_of(c)
        for n, chunks in enumerate(targets):
            chunk, copy = chunks[c]
            if copy is not None:
                copy.wait()
            part = nn(rows, chunk[...])
            totals[n] = part if totals[n] is None else totals[n] + part
    return [total.astype(BF16) for total in totals]


def mixed_kernel(
    state_ref, first_inside, first_window, second_inside, second_window, gate_ref, gain_ref,
    early_ref, weight_hbm, mixed_ref, own_early_ref, *refs, shifts,
):
    out_refs, (held, sems, own_sems) = refs[:-3], refs[-3:]
    me = lax.axis_index("head")
    early, depth, _ = early_ref.shape
    chunks = held.shape[0] // (shifts - 1)
    targets = []
    for n in range(shifts - 1):
        known = early if n == 0 else 0
        slots = pl.ds(n * chunks, chunks - known)
        copies = weight_copies(
            weight_hbm, lax.rem(me + 1 + n, shifts), known, held.at[slots], sems.at[slots]
        )
        targets.append(
            [(early_ref.at[c], None) for c in range(known)]
            + [(held.at[n * chunks + c], copy) for c, copy in enumerate(copies)]
        )
    own_copies = weight_copies(weight_hbm, me, 0, own_early_ref, own_sems)
    gain = gain_ref[...]
    split = first_inside.shape[0]

    def head(h):
        inside, window, at = (
            (first_inside, first_window, h) if h < split
            else (second_inside, second_window, h - split)
        )
        j, r = h // REP, h % REP
        columns = pl.ds(h * DV, DV)
        rows = inside[at].astype(F32) + nn(window[at], state_ref[j, r * DK : (r + 1) * DK, :])
        scale = lax.rsqrt(jnp.mean(rows * rows, axis=1, keepdims=True) + EPSILON)
        gate = gate_ref[:, columns].astype(F32)
        mixed = (rows * scale * gain * (gate / (1.0 + jnp.exp(-gate)))).astype(BF16)
        mixed_ref[:, columns] = mixed
        return mixed

    def chunk_of(c):
        return jnp.concatenate(
            [head(h) for h in range(c * depth // DV, (c + 1) * depth // DV)], axis=1
        )

    for out_ref, total in zip(out_refs, project(chunk_of, targets)):
        out_ref[...] = total
    for copy in own_copies:
        copy.wait()


def own_columns_kernel(mixed_ref, early_ref, weight_hbm, out_ref, held, sems):
    early, depth, _ = early_ref.shape
    copies = weight_copies(weight_hbm, lax.axis_index("head"), early, held, sems)
    chunks = [(early_ref.at[c], None) for c in range(early)]
    chunks += [(held.at[c], copy) for c, copy in enumerate(copies)]
    (out_ref[...],) = project(lambda c: mixed_ref[:, c * depth : (c + 1) * depth], [chunks])


def local(
    query_proj, key_proj, value_proj, gate_proj, write_strength, log_decay, norm_gain, out_weight,
    *, n_ctx, n_head,
):
    tokens = query_proj.shape[0]
    heads = value_proj.shape[1] // DV
    group = query_proj.shape[1] // DK
    half = group // 2
    width = out_weight.shape[1] // n_head
    n_groups = n_ctx // group
    groups = [list(range(g, g + group)) for g in range(0, n_ctx, group)]
    packed_rows = (1 + REP) * tokens + SMALL_ROWS
    mib = 1024 * 1024

    def kernel(body, out, name, limit, micros, scratch=(), specs=None, out_specs=None):
        return pl.pallas_call(
            body,
            out_shape=out,
            scratch_shapes=scratch,
            compiler_params=pltpu.CompilerParams(
                vmem_limit_bytes=None if limit is None else limit * mib
            ),
            cost_estimate=pl.CostEstimate(
                flops=int(micros * 1e9), bytes_accessed=mib, transcendentals=0
            ),
            name=name,
            **({} if specs is None else {"in_specs": specs}),
            **({} if out_specs is None else {"out_specs": out_specs}),
        )

    def shape(dims, kind):
        return jax.ShapeDtypeStruct(dims, kind)

    def shifted(array, distance):
        return lax.ppermute(array, "ctx", [(i, i + distance) for i in range(n_ctx - distance)])

    def swapped(array, distance):
        return lax.ppermute(array, "ctx", [(i, i ^ distance) for i in range(n_ctx)])

    any_space = pl.BlockSpec(memory_space=pl.ANY)
    vmem = pl.BlockSpec(memory_space=pltpu.VMEM)
    *packed, rows = kernel(
        pack_kernel,
        (shape((packed_rows, DK), BF16),) * group + (shape((group * SMALL_ROWS, DK), BF16),),
        "pack",
        None,
        2,
        scratch=[
            pltpu.VMEM((group, packed_rows, DK), BF16),
            pltpu.VMEM((2, heads, tokens), F32),
            pltpu.VMEM((group * SMALL_ROWS, DK), BF16),
            pltpu.SemaphoreType.DMA((group + 1, 1 + REP)),
            pltpu.SemaphoreType.DMA((group + 1,)),
        ],
        specs=[any_space] * 4,
        out_specs=(any_space,) * (group + 1),
    )(key_proj, value_proj, write_strength.T, log_decay.T)
    taken = [packed[0]] + [swapped(packed[s], s) for s in range(1, group)]

    def half_states(blocks, more, name):
        own, with_map = not more, n_groups > 2
        return kernel(
            functools.partial(half_kernel, blocks=half, group=group, tokens=tokens, own=own, with_map=with_map),
            (
                shape((half * REP, DK, DV), F32),
                shape((half * REP, DK, DK), BF16),
                shape((REP, DK, DV), F32),
                shape((REP, DK, DK), F32),
            )
            + (() if own else (shape((REP, DK, DV), BF16),))
            + ((shape((REP, DK, DK), F32),) if with_map and not own else ()),
            name,
            16,
            3.5,
            scratch=[
                pltpu.VMEM((half * REP, DK, DV), F32),
                pltpu.VMEM((half * REP, DK, DK), BF16),
                pltpu.VMEM((half * REP, PIECE_ROWS, DK), F32),
            ],
        )(*blocks, *more)

    own = half_states(taken[:half], (), "own_half")
    later, own = lax.optimization_barrier((taken[half:], own))
    *other, end = half_states(later, own[2:], "other_half")

    if n_groups == 2:
        carried = swapped(end, group)
    elif n_groups > 2:
        carried, mapping = shifted(other[-1], group).astype(F32), shifted(end, group)
        other = other[:-1]
        distance = 1
        while distance < n_groups - 1:
            earlier, earlier_map = shifted(carried, distance * group), shifted(mapping, distance * group)
            carried = carried + jnp.einsum("rkl,rlv->rkv", mapping, earlier, precision="highest")
            mapping = jnp.einsum("rkl,rlv->rkv", mapping, earlier_map, precision="highest")
            distance *= 2
        carried = carried.astype(BF16)
    else:
        carried = jnp.zeros((REP, DK, DV), BF16)

    chunks = min(CHUNKS, out_weight.shape[0] // DV)
    depth = out_weight.shape[0] // chunks

    def inside_part(start, count, rows, micros, limit, fetch):
        return kernel(
            functools.partial(inside_kernel, first=start, shifts=n_head if fetch else 0),
            (
                shape((count * REP, tokens, DV), BF16),
                shape((count * REP, tokens, DK), BF16),
            )
            + ((shape((fetch, depth, width), BF16),) if fetch else ()),
            "inside",
            limit,
            micros,
            scratch=[pltpu.SemaphoreType.DMA((fetch,))] if fetch else (),
            specs=[vmem] * 4 + ([any_space] if fetch else []),
        )(query_proj, key_proj, value_proj, rows, *((out_weight,) if fetch else ()))

    early = half
    rows, end = lax.optimization_barrier((rows, end))
    first = inside_part(0, early, rows, 2.4, 16, 0)
    carried, first = lax.optimization_barrier((carried, first))
    states = kernel(
        carry_kernel,
        shape((group, REP * DK, DV), BF16),
        "carry",
        8,
        0.6,
        scratch=[pltpu.VMEM((group, REP * DK, DV), BF16), pltpu.SemaphoreType.DMA((group,))],
        out_specs=any_space,
    )(*own, *other, carried)
    state_in = lax.all_to_all(states, "ctx", 0, 0, axis_index_groups=groups, tiled=True)
    rows, states = lax.optimization_barrier((rows, states))
    *second, weight_rows = inside_part(early, group - early, rows, 4, 44, chunks // 4)

    early_shape = shape((chunks // 2, depth, width), BF16)
    mixed, own_rows, *others = kernel(
        functools.partial(mixed_kernel, shifts=n_head),
        (shape((tokens, heads * DV), BF16), early_shape)
        + (shape((tokens, width), BF16),) * (n_head - 1),
        "mixed",
        43,
        2.5,
        scratch=[
            pltpu.VMEM(((n_head - 1) * chunks, depth, width), BF16),
            pltpu.SemaphoreType.DMA(((n_head - 1) * chunks,)),
            pltpu.SemaphoreType.DMA((chunks // 2,)),
        ],
        specs=[vmem] * 8 + [any_space],
    )(
        state_in, *first, *second, gate_proj, norm_gain.reshape(1, DV), weight_rows, out_weight
    )
    received = [
        lax.ppermute(other, "head", [(i, (i + 1 + s) % n_head) for i in range(n_head)])
        for s, other in enumerate(others)
    ]
    total = kernel(
        own_columns_kernel,
        shape((tokens, width), BF16),
        "own_columns",
        46,
        2,
        scratch=[
            pltpu.VMEM((chunks - chunks // 2, depth, width), BF16),
            pltpu.SemaphoreType.DMA((chunks - chunks // 2,)),
        ],
        specs=[vmem] * 2 + [any_space],
    )(mixed, own_rows, out_weight).astype(F32)
    for other in received:
        total = total + other.astype(F32)
    return total.astype(BF16)


def solution(mesh):
    return jax.shard_map(
        functools.partial(local, n_ctx=mesh.shape["ctx"], n_head=mesh.shape["head"]),
        mesh=mesh,
        in_specs=(
            P("ctx", "head"),
            P("ctx", "head"),
            P("ctx", "head"),
            P("ctx", "head"),
            P("ctx", "head"),
            P("ctx", "head"),
            P(),
            P("head", None),
        ),
        out_specs=P("ctx", "head"),
        check_vma=False,
    )
```

time: 586 us -> 48.2 us (0.08)
  waiting for transfers between devices: 427 us -> 3.22 us
  other arithmetic: 81 us -> 0.77 us
  matrix products: 38.8 us -> 0 us
  Pallas kernels: 0 us -> 22.2 us
  local copies, waits for them, and re-layouts: 24.1 us -> 2.92 us
  starting transfers between devices: 0.08 us -> 18.4 us
  between operations: 13.5 us -> 0.17 us
    all_gather x2 -> x0, waiting for transfers between devices: 378 us -> none  [carried_in(): gathered = jax.tree.map(lambda a: lax.all_gather(a, axis), part)]
    another operation x5 -> x0, other arithmetic: 76.3 us -> none  [the longest x4 76.1 us: span_terms(): jax.scipy.linalg.solve_triangular(system, right_side, lower=True, unit_di...]
    reduce_scatter x1 -> x0, waiting for transfers between devices: 49.2 us -> none  [local(): lax.psum_scatter(jnp.einsum('fd,tf->dt', out_weight, mixed, preferred_ele...]
    dot_general x15 -> x0, matrix products: 36.8 us -> none  [the longest x6 8.92 us: apply_map(): jnp.einsum('epn,eni->epi', per_step_function, desired_value, precision=ex...]
    pallas_call x0 -> x8, Pallas kernels: none -> 22.2 us  [the longest x2 7.06 us: inside_part(): kernel(functools.partial(inside_kernel, first=start, shifts=n_head if fet...]
    ppermute x0 -> x9, starting transfers between devices: none -> 14.5 us  [the longest x8 14.5 us: swapped(): return lax.ppermute(array, 'ctx', [(i, i ^ distance) for i in range(n_ctx)])]
    while x30 -> x0, local copies, waits for them, and re-layouts: 6.82 us -> none
  transfers between devices with their start and end apart: 3 -> 10, of which waited for: 3 -> 3; matrix products, arithmetic and copies ran while one was open for 1% -> 0% of each run, Pallas kernels for 0% -> 25%
where the time goes in v1:
time: 48.2 us; the launch traced here: 47.7 us
  Pallas kernels  22.2 us (46%)
  starting transfers between devices  18.4 us (38%)
  waiting for transfers between devices  3.22 us (7%)
  local copies, waits for them, and re-layouts  2.92 us (6%)
  other arithmetic  0.77 us (2%)
    ppermute x8, starting transfers between devices, swapped(): return lax.ppermute(array, 'ctx', [(i, i ^ distance) for i in range(n_ctx)])  14.5 us
    pallas_call x2, Pallas kernels, inside_part(): kernel(functools.partial(inside_kernel, first=start, shifts=n_head if fet...  7.06 us
    pallas_call x2, Pallas kernels, half_states(): kernel(functools.partial(half_kernel, blocks=half, group=group, tokens=to...  6.42 us
    all_to_all x1, starting transfers between devices, local(): lax.all_to_all(states, 'ctx', 0, 0, axis_index_groups=groups, tiled=True)  3.82 us
    pallas_call x1, Pallas kernels, local(): kernel(functools.partial(mixed_kernel, shifts=n_head), (shape((tokens, he...  3.63 us
    unnamed x18, local copies, waits for them, and re-layouts  2.92 us
    pallas_call x1, Pallas kernels, local(): kernel(pack_kernel, (shape((packed_rows, DK), BF16),) * group + (shape((g...  2.09 us
    pallas_call x1, Pallas kernels, local(): kernel(own_columns_kernel, shape((tokens, width), BF16), 'own_columns', 4...  1.81 us
  transfers between devices with their start and end apart: 10, of which 3 were waited for; matrix products, arithmetic and copies ran while one was open for 0% of the time, Pallas kernels for 25%

profile of v1, /device:TPU:0, one launch (start us, length us, event | category | flops | bytes accessed | tf_op | source)
XLA Modules:
  0.0 47.7 jit_solution(4009897247295167724)
XLA Ops:
  0.0 2.1 %pack.1 = (bf16[400,128]{1,0:T(8,128)(2,1)}, bf16[400,128]{1,0:T(8,128)(2,1)}, bf16[400,128]{1,0:T(8,128)(2,1)}, bf16[400,128]{1,0:T(8,128)(2,1)}, bf16[400,128]...) custom-call(bf16[128,1024]{1,0:T(8,128)(2,1)} %key_ref.3, ...), custom_call_target="tpu_custom_call" | custom-call | flops 2000000000 | bytes 1048576 | tf_op jit(solution)/shard_map/pack/pallas_call | solution.py:498
  2.1 3.0 %collective-permute-start.4 = (bf16[400,128]{1,0:T(8,128)(2,1)}, bf16[400,128]{1,0:T(8,128)(2,1)S(1)}, u32[]{:S(2)}, u32[]{:S(2)}) collective-permute-start(bf16[400,128]{1,0:T(8,128)(2,1)} %get-tuple-element.49), channel_id=1, source_target_pairs={{0,2},{2,0},{4,6},{6,4},{8,10},{10,8},{12,14},{14,12},{16,18},{18,... | collective-permute-start | bytes 307208 | tf_op jit(solution)/shard_map/ppermute | solution.py:494
  5.1 1.5 %collective-permute-start.5 = (bf16[400,128]{1,0:T(8,128)(2,1)}, bf16[400,128]{1,0:T(8,128)(2,1)S(1)}, u32[]{:S(2)}, u32[]{:S(2)}) collective-permute-start(bf16[400,128]{1,0:T(8,128)(2,1)} %get-tuple-element.50), channel_id=1, source_target_pairs={{0,4},{2,6},{4,0},{6,2},{8,12},{10,14},{12,8},{14,10},{16,20},{18,... | collective-permute-start | bytes 307208 | tf_op jit(solution)/shard_map/ppermute | solution.py:494
  6.6 0.0 collective-permute-start.6
  6.6 2.0 %collective-permute-start = (bf16[400,128]{1,0:T(8,128)(2,1)}, bf16[400,128]{1,0:T(8,128)(2,1)S(1)}, u32[]{:S(2)}, u32[]{:S(2)}) collective-permute-start(bf16[400,128]{1,0:T(8,128)(2,1)} %get-tuple-element.44), channel_id=1, source_target_pairs={{0,8},{2,10},{4,12},{6,14},{8,0},{10,2},{12,4},{14,6},{16,24},{18,... | collective-permute-start | bytes 307208 | tf_op jit(solution)/shard_map/ppermute | solution.py:494
  8.7 1.4 %collective-permute-start.1 = (bf16[400,128]{1,0:T(8,128)(2,1)}, bf16[400,128]{1,0:T(8,128)(2,1)S(1)}, u32[]{:S(2)}, u32[]{:S(2)}) collective-permute-start(bf16[400,128]{1,0:T(8,128)(2,1)} %get-tuple-element.45), channel_id=1, source_target_pairs={{0,10},{2,8},{4,14},{6,12},{8,2},{10,0},{12,6},{14,4},{16,26},{18,... | collective-permute-start | bytes 307208 | tf_op jit(solution)/shard_map/ppermute | solution.py:494
  10.1 0.0 collective-permute-done.4.refs_1_
  10.1 2.5 %collective-permute-start.2 = (bf16[400,128]{1,0:T(8,128)(2,1)}, bf16[400,128]{1,0:T(8,128)(2,1)S(1)}, u32[]{:S(2)}, u32[]{:S(2)}) collective-permute-start(bf16[400,128]{1,0:T(8,128)(2,1)} %get-tuple-element.46), channel_id=1, source_target_pairs={{0,12},{2,14},{4,8},{6,10},{8,4},{10,6},{12,0},{14,2},{16,28},{18,... | collective-permute-start | bytes 307208 | tf_op jit(solution)/shard_map/ppermute | solution.py:494
  12.6 1.3 %collective-permute-start.3 = (bf16[400,128]{1,0:T(8,128)(2,1)}, bf16[400,128]{1,0:T(8,128)(2,1)S(1)}, u32[]{:S(2)}, u32[]{:S(2)}) collective-permute-start(bf16[400,128]{1,0:T(8,128)(2,1)} %get-tuple-element.47), channel_id=1, source_target_pairs={{0,14},{2,12},{4,10},{6,8},{8,6},{10,4},{12,2},{14,0},{16,30},{18,... | collective-permute-start | bytes 307208 | tf_op jit(solution)/shard_map/ppermute | solution.py:494
  13.9 0.9 %copy-done.7 = bf16[400,128]{1,0:T(8,128)(2,1)S(1)} copy-done((bf16[400,128]{1,0:T(8,128)(2,1)S(1)}, bf16[400,128]{1,0:T(8,128)(2,1)}, u32[]{:S(2)}) %copy-start.7) | copy-done | bytes 102424
  14.8 3.1 %own_half.1 = (f32[8,128,128]{2,1,0:T(8,128)S(1)}, bf16[8,128,128]{2,1,0:T(8,128)(2,1)S(1)}, f32[2,128,128]{2,1,0:T(8,128)S(1)}, f32[2,128,128]{2,1,0:T(8,128)S(1)}) custom-call(bf16[400,128]{1,0:T(8,128)(2,1)S(1)} %copy-done.7, bf16[400,128]{1,0:T(8,128)(2,1)S(1)} %collective-permute-done.4.refs_1_, bf16[400,128]{1,0:T(8,128)(2,1)S(1)} %collective-permute-done.5.refs_2_, ...), custom_call_target="tpu_custom_call" | custom-call | flops 3500000000 | bytes 1048576 | tf_op jit(solution)/shard_map/own_half/pallas_call | solution.py:518
  18.0 0.0 copy-start.2
  18.0 0.0 copy-start.4
  18.0 0.0 copy-start.5
  18.0 0.4 collective-permute-done.2.refs_2_
  18.4 1.3 %collective-permute-done.3.refs_3_ = bf16[400,128]{1,0:T(8,128)(2,1)S(1)} collective-permute-done((bf16[400,128]{1,0:T(8,128)(2,1)}, bf16[400,128]{1,0:T(8,128)(2,1)S(1)}, u32[]{:S(2)}, u32[]{:S(2)}) %collective-permute-start.3) | collective-permute-done | bytes 102432 | tf_op jit(solution)/shard_map/ppermute | solution.py:494
  19.7 3.3 %other_half.1 = (f32[8,128,128]{2,1,0:T(8,128)S(1)}, bf16[8,128,128]{2,1,0:T(8,128)(2,1)S(1)}, f32[2,128,128]{2,1,0:T(8,128)S(1)}, f32[2,128,128]{2,1,0:T(8,128)S(1)}, bf16[2,128,128]{2,1,0:T(8,128)(2,1)S(1)}) custom-call(bf16[400,128]{1,0:T(8,128)(2,1)S(1)} %collective-permute-done.refs_0_, bf16[400,128]{1,0:T(8,128)(2,1)S(1)} %collective-permute-done.1.refs_1_, ...), custom_call_target="tpu_custom_call" | custom-call | flops 3500000000 | bytes 1048576 | tf_op jit(solution)/shard_map/other_half/pallas_call | solution.py:518
  23.0 2.7 %collective-permute-start.7 = (bf16[2,128,128]{2,1,0:T(8,128)(2,1)S(1)}, bf16[2,128,128]{2,1,0:T(8,128)(2,1)S(1)}, u32[]{:S(2)}, u32[]{:S(2)}) collective-permute-start(bf16[2,128,128]{2,1,0:T(8,128)(2,1)S(1)} %get-tuple-element.68), channel_id=1, source_target_pairs={{0,16},{2,18},{4,20},{6,22},{8,24},{10,26},{12,28},{14,30},{16,0},... | collective-permute-start | bytes 196616 | tf_op jit(solution)/shard_map/ppermute | solution.py:494
  25.7 3.1 %inside.2 = (bf16[8,128,128]{2,1,0:T(8,128)(2,1)S(1)}, bf16[8,128,128]{2,1,0:T(8,128)(2,1)S(1)}) custom-call(bf16[128,1024]{1,0:T(8,128)(2,1)S(1)} %copy-done.5, bf16[128,1024]{1,0:T(8,128)(2,1)S(1)} %copy-done.4, bf16[128,2048]{1,0:T(8,128)(2,1)S(1)} %copy-done.2, bf16[128,128]{1,0:T(8,128)(2,1)S(1)} %copy-done.8), custom_call_target="tpu_custom_call" | custom-call | flops 2400000000 | bytes 1048576 | tf_op jit(solution)/shard_map/inside/pallas_call | solution.py:561
  28.8 1.2 %carry.1 = bf16[8,256,128]{2,1,0:T(8,128)(2,1)} custom-call(f32[8,128,128]{2,1,0:T(8,128)S(1)} %get-tuple-element.56.own_before, bf16[8,128,128]{2,1,0:T(8,128)(2,1)S(1)} %get-tuple-element.57.own_maps, f32[2,128,128]{2,1,0:T(8,128)S(1)} %get-tuple-element.58.refs_4_.own_end, f32[2,128,128]{2,1,0:T(8,128)S(1)} %get-tuple-element.59.refs_5_.own_map, ...), custom_call_target="tpu_custom_call" | custom-call | flops 600000000 | bytes 1048576 | tf_op jit(solution)/shard_map/carry/pallas_call | solution.py:579
  30.1 0.0 copy-start
  30.1 0.0 copy-start.1
  30.1 3.8 %all-to-all-start = ((bf16[8,256,128]{2,1,0:T(8,128)(2,1)}), bf16[8,256,128]{2,1,0:T(8,128)(2,1)S(1)}, u32[]{:S(2)}, u32[]{:S(2)}) async-start(bf16[8,256,128]{2,1,0:T(8,128)(2,1)} %carry.1), calls=%async_computation | async-start | bytes 1048576 | tf_op jit(solution)/shard_map/all_to_all | solution.py:588
  33.9 0.0 copy-start.3
  33.9 1.0 %copy-done.3 = bf16[128,2048]{1,0:T(8,128)(2,1)S(1)} copy-done((bf16[128,2048]{1,0:T(8,128)(2,1)S(1)}, bf16[128,2048]{1,0:T(8,128)(2,1)}, u32[]{:S(2)}) %copy-start.3) | copy-done | bytes 524312
  34.9 0.9 %copy-done.6 = bf16[128,1024]{1,0:T(8,128)(2,1)S(1)} copy-done((bf16[128,1024]{1,0:T(8,128)(2,1)S(1)}, bf16[128,1024]{1,0:T(8,128)(2,1)}, u32[]{:S(2)}) %copy-start.6) | copy-done | bytes 262168
  35.9 3.9 %inside.3 = (bf16[8,128,128]{2,1,0:T(8,128)(2,1)S(1)}, bf16[8,128,128]{2,1,0:T(8,128)(2,1)S(1)}, bf16[2,256,1024]{2,1,0:T(8,128)(2,1)S(1)}) custom-call(bf16[128,1024]{1,0:T(8,128)(2,1)S(1)} %copy-done.6, bf16[128,1024]{1,0:T(8,128)(2,1)S(1)} %copy-done.4, bf16[128,2048]{1,0:T(8,128)(2,1)S(1)} %copy-done.3, bf16[128,128]{1,0:T(8,128)(2,1)S(1)} %copy-done.8, ...), custom_call_target="tpu_custom_call" | custom-call | flops 4000000000 | bytes 1048576 | tf_op jit(solution)/shard_map/inside/pallas_call | solution.py:561
  39.8 1.5 %all-to-all-done.state_ref = bf16[8,256,128]{2,1,0:T(8,128)(2,1)S(1)} async-done(((bf16[8,256,128]{2,1,0:T(8,128)(2,1)}), bf16[8,256,128]{2,1,0:T(8,128)(2,1)S(1)}, u32[]{:S(2)}, u32[]{:S(2)}) %all-to-all-start) | async-done | bytes 524320 | tf_op jit(solution)/shard_map/all_to_all | solution.py:588
  41.3 3.6 %mixed.1 = (bf16[128,2048]{1,0:T(8,128)(2,1)S(1)}, bf16[4,256,1024]{2,1,0:T(8,128)(2,1)S(1)}, bf16[128,1024]{1,0:T(8,128)(2,1)S(1)}) custom-call(bf16[8,256,128]{2,1,0:T(8,128)(2,1)S(1)} %all-to-all-done.state_ref, bf16[8,128,128]{2,1,0:T(8,128)(2,1)S(1)} %get-tuple-element.74.first_inside, bf16[8,128,128]{2,1,0:T(8,128)(2,1)S(1)} %get-tuple-element.75.first_window, ...), custom_call_target="tpu_custom_call" | custom-call | flops 2500000000 | bytes 1048576 | tf_op jit(solution)/shard_map/mixed/pallas_call | solution.py:593
  45.0 0.1 collective-permute-start.8
  45.1 1.8 %own_columns.1 = bf16[128,1024]{1,0:T(8,128)(2,1)S(1)} custom-call(bf16[128,2048]{1,0:T(8,128)(2,1)S(1)} %get-tuple-element.80.mixed_ref, bf16[4,256,1024]{2,1,0:T(8,128)(2,1)S(1)} %get-tuple-element.81.early_ref, bf16[2048,2048]{1,0:T(8,128)(2,1)} %weight_hbm.3), custom_call_target="tpu_custom_call" | custom-call | flops 2000000000 | bytes 1048576 | tf_op jit(solution)/shard_map/own_columns/pallas_call | solution.py:613
  46.9 0.8 %add_convert_fusion = bf16[128,1024]{1,0:T(8,128)(2,1)} fusion(bf16[128,1024]{1,0:T(8,128)(2,1)S(1)} %collective-permute-done.8, bf16[128,1024]{1,0:T(8,128)(2,1)S(1)} %own_columns.1), kind=kLoop, calls=%fused_computation | loop fusion | flops 524288 | bytes 786432 | tf_op jit(solution)/shard_map/convert_element_type | solution.py:627
  (15 shorter events, 0.0 us)
Async XLA Ops:
  2.1 8.0 %collective-permute-start.4 = (bf16[400,128]{1,0:T(8,128)(2,1)}, bf16[400,128]{1,0:T(8,128)(2,1)S(1)}, u32[]{:S(2)}, u32[]{:S(2)}) collective-permute-start(bf16[400,128]{1,0:T(8,128)(2,1)} %get-tuple-element.49), channel_id=1, source_target_pairs={{0,2},{2,0},{4,6},{6,4},{8,10},{10,8},{12,14},{14,12},{16,18},{18,... | collective-permute-start | bytes 307208 | tf_op jit(solution)/shard_map/ppermute | solution.py:494
  5.1 7.5 %collective-permute-start.5 = (bf16[400,128]{1,0:T(8,128)(2,1)}, bf16[400,128]{1,0:T(8,128)(2,1)S(1)}, u32[]{:S(2)}, u32[]{:S(2)}) collective-permute-start(bf16[400,128]{1,0:T(8,128)(2,1)} %get-tuple-element.50), channel_id=1, source_target_pairs={{0,4},{2,6},{4,0},{6,2},{8,12},{10,14},{12,8},{14,10},{16,20},{18,... | collective-permute-start | bytes 307208 | tf_op jit(solution)/shard_map/ppermute | solution.py:494
  6.6 7.3 %collective-permute-start.6 = (bf16[400,128]{1,0:T(8,128)(2,1)}, bf16[400,128]{1,0:T(8,128)(2,1)S(1)}, u32[]{:S(2)}, u32[]{:S(2)}) collective-permute-start(bf16[400,128]{1,0:T(8,128)(2,1)} %get-tuple-element.51), channel_id=1, source_target_pairs={{0,6},{2,4},{4,2},{6,0},{8,14},{10,12},{12,10},{14,8},{16,22},{18,... | collective-permute-start | bytes 307208 | tf_op jit(solution)/shard_map/ppermute | solution.py:494
  6.6 11.4 %collective-permute-start = (bf16[400,128]{1,0:T(8,128)(2,1)}, bf16[400,128]{1,0:T(8,128)(2,1)S(1)}, u32[]{:S(2)}, u32[]{:S(2)}) collective-permute-start(bf16[400,128]{1,0:T(8,128)(2,1)} %get-tuple-element.44), channel_id=1, source_target_pairs={{0,8},{2,10},{4,12},{6,14},{8,0},{10,2},{12,4},{14,6},{16,24},{18,... | collective-permute-start | bytes 307208 | tf_op jit(solution)/shard_map/ppermute | solution.py:494
  8.7 9.3 %collective-permute-start.1 = (bf16[400,128]{1,0:T(8,128)(2,1)}, bf16[400,128]{1,0:T(8,128)(2,1)S(1)}, u32[]{:S(2)}, u32[]{:S(2)}) collective-permute-start(bf16[400,128]{1,0:T(8,128)(2,1)} %get-tuple-element.45), channel_id=1, source_target_pairs={{0,10},{2,8},{4,14},{6,12},{8,2},{10,0},{12,6},{14,4},{16,26},{18,... | collective-permute-start | bytes 307208 | tf_op jit(solution)/shard_map/ppermute | solution.py:494
  10.1 8.4 %collective-permute-start.2 = (bf16[400,128]{1,0:T(8,128)(2,1)}, bf16[400,128]{1,0:T(8,128)(2,1)S(1)}, u32[]{:S(2)}, u32[]{:S(2)}) collective-permute-start(bf16[400,128]{1,0:T(8,128)(2,1)} %get-tuple-element.46), channel_id=1, source_target_pairs={{0,12},{2,14},{4,8},{6,10},{8,4},{10,6},{12,0},{14,2},{16,28},{18,... | collective-permute-start | bytes 307208 | tf_op jit(solution)/shard_map/ppermute | solution.py:494
  12.6 7.1 %collective-permute-start.3 = (bf16[400,128]{1,0:T(8,128)(2,1)}, bf16[400,128]{1,0:T(8,128)(2,1)S(1)}, u32[]{:S(2)}, u32[]{:S(2)}) collective-permute-start(bf16[400,128]{1,0:T(8,128)(2,1)} %get-tuple-element.47), channel_id=1, source_target_pairs={{0,14},{2,12},{4,10},{6,8},{8,6},{10,4},{12,2},{14,0},{16,30},{18,... | collective-permute-start | bytes 307208 | tf_op jit(solution)/shard_map/ppermute | solution.py:494
  13.9 0.9 %copy-start.7 = (bf16[400,128]{1,0:T(8,128)(2,1)S(1)}, bf16[400,128]{1,0:T(8,128)(2,1)}, u32[]{:S(2)}) copy-start(bf16[400,128]{1,0:T(8,128)(2,1)} %get-tuple-element.48.refs_0_) | copy-start | bytes 307204
  18.0 7.7 %copy-start.2 = (bf16[128,2048]{1,0:T(8,128)(2,1)S(1)}, bf16[128,2048]{1,0:T(8,128)(2,1)}, u32[]{:S(2)}) copy-start(bf16[128,2048]{1,0:T(8,128)(2,1)} %value_ref.3) | copy-start | bytes 1572868
  18.0 7.7 %copy-start.4 = (bf16[128,1024]{1,0:T(8,128)(2,1)S(1)}, bf16[128,1024]{1,0:T(8,128)(2,1)}, u32[]{:S(2)}) copy-start(bf16[128,1024]{1,0:T(8,128)(2,1)} %key_ref.3) | copy-start | bytes 786436
  18.0 7.7 %copy-start.5 = (bf16[128,1024]{1,0:T(8,128)(2,1)S(1)}, bf16[128,1024]{1,0:T(8,128)(2,1)}, u32[]{:S(2)}) copy-start(bf16[128,1024]{1,0:T(8,128)(2,1)} %query_ref.3) | copy-start | bytes 786436
  18.0 7.7 %copy-start.8 = (bf16[128,128]{1,0:T(8,128)(2,1)S(1)}, bf16[128,128]{1,0:T(8,128)(2,1)}, u32[]{:S(2)}) copy-start(bf16[128,128]{1,0:T(8,128)(2,1)} %get-tuple-element.76.rows_ref) | copy-start | bytes 98308
  23.0 5.8 %collective-permute-start.7 = (bf16[2,128,128]{2,1,0:T(8,128)(2,1)S(1)}, bf16[2,128,128]{2,1,0:T(8,128)(2,1)S(1)}, u32[]{:S(2)}, u32[]{:S(2)}) collective-permute-start(bf16[2,128,128]{2,1,0:T(8,128)(2,1)S(1)} %get-tuple-element.68), channel_id=1, source_target_pairs={{0,16},{2,18},{4,20},{6,22},{8,24},{10,26},{12,28},{14,30},{16,0},... | collective-permute-start | bytes 196616 | tf_op jit(solution)/shard_map/ppermute | solution.py:494
  30.1 11.3 %copy-start = (bf16[128,2048]{1,0:T(8,128)(2,1)S(1)}, bf16[128,2048]{1,0:T(8,128)(2,1)}, u32[]{:S(2)}) copy-start(bf16[128,2048]{1,0:T(8,128)(2,1)} %gate_ref.1) | copy-start | bytes 1572868
  30.1 11.3 %copy-start.1 = (f32[128]{0:T(128)S(1)}, f32[128]{0:T(128)}, u32[]{:S(2)}) copy-start(f32[128]{0:T(128)} %param.14) | copy-start | bytes 1540
  30.1 11.3 %all-to-all-start = ((bf16[8,256,128]{2,1,0:T(8,128)(2,1)}), bf16[8,256,128]{2,1,0:T(8,128)(2,1)S(1)}, u32[]{:S(2)}, u32[]{:S(2)}) async-start(bf16[8,256,128]{2,1,0:T(8,128)(2,1)} %carry.1), calls=%async_computation | async-start | bytes 1048576 | tf_op jit(solution)/shard_map/all_to_all | solution.py:588
  33.9 1.0 %copy-start.3 = (bf16[128,2048]{1,0:T(8,128)(2,1)S(1)}, bf16[128,2048]{1,0:T(8,128)(2,1)}, u32[]{:S(2)}) copy-start(bf16[128,2048]{1,0:T(8,128)(2,1)} %value_ref.3) | copy-start | bytes 1572868
  34.9 0.9 %copy-start.6 = (bf16[128,1024]{1,0:T(8,128)(2,1)S(1)}, bf16[128,1024]{1,0:T(8,128)(2,1)}, u32[]{:S(2)}) copy-start(bf16[128,1024]{1,0:T(8,128)(2,1)} %query_ref.3) | copy-start | bytes 786436
  45.0 1.9 %collective-permute-start.8 = (bf16[128,1024]{1,0:T(8,128)(2,1)S(1)}, bf16[128,1024]{1,0:T(8,128)(2,1)S(1)}, u32[]{:S(2)}, u32[]{:S(2)}) collective-permute-start(bf16[128,1024]{1,0:T(8,128)(2,1)S(1)} %get-tuple-element.82), channel_id=1, source_target_pairs={{0,1},{1,0},{2,3},{3,2},{4,5},{5,4},{6,7},{7,6},{8,9},{9,8},{10,11... | collective-permute-start | bytes 786440 | tf_op jit(solution)/shard_map/ppermute | solution.py:610

commit v2 on v1

--- a/solution.py
+++ b/solution.py
@@ -431,14 +431,16 @@
         rows = inside[at].astype(F32) + nn(window[at], state_ref[j, r * DK : (r + 1) * DK, :])
         scale = lax.rsqrt(jnp.mean(rows * rows, axis=1, keepdims=True) + EPSILON)
         gate = gate_ref[:, columns].astype(F32)
-        mixed = (rows * scale * gain * (gate / (1.0 + jnp.exp(-gate)))).astype(BF16)
-        mixed_ref[:, columns] = mixed
-        return mixed
+        mixed_ref[:, columns] = (
+            rows * scale * gain * (gate / (1.0 + jnp.exp(-gate)))
+        ).astype(BF16)
+
+    for h in range(split + second_inside.shape[0]):
+        head(h)
+    rows = mixed_ref[...]
 
     def chunk_of(c):
-        return jnp.concatenate(
-            [head(h) for h in range(c * depth // DV, (c + 1) * depth // DV)], axis=1
-        )
+        return rows[:, c * depth : (c + 1) * depth]
 
     for out_ref, total in zip(out_refs, project(chunk_of, targets)):
         out_ref[...] = total
@@ -572,7 +574,7 @@
             specs=[vmem] * 4 + ([any_space] if fetch else []),
         )(query_proj, key_proj, value_proj, rows, *((out_weight,) if fetch else ()))
 
-    early = half
+    early = max(1, group // 4)
     rows, end = lax.optimization_barrier((rows, end))
     first = inside_part(0, early, rows, 2.4, 16, 0)
     carried, first = lax.optimization_barrier((carried, first))

time: 48.2 us -> 47.3 us (0.981)
  waiting for transfers between devices: 3.22 us -> 2.51 us
    all_to_all x1, waiting for transfers between devices: 1.5 us -> 0.54 us  [local(): lax.all_to_all(states, 'ctx', 0, 0, axis_index_groups=groups, tiled=True)]
  transfers between devices with their start and end apart: 10 -> 10, of which waited for: 3 -> 4; matrix products, arithmetic and copies ran while one was open for 0% -> 0% of each run, Pallas kernels for 25% -> 26%
where the time goes in v2:
time: 47.3 us; the launch traced here: 46.8 us
  Pallas kernels  22.1 us (47%)
  starting transfers between devices  18.4 us (39%)
  local copies, waits for them, and re-layouts  2.92 us (6%)
  waiting for transfers between devices  2.51 us (5%)
  other arithmetic  0.77 us (2%)
    ppermute x8, starting transfers between devices, swapped(): return lax.ppermute(array, 'ctx', [(i, i ^ distance) for i in range(n_ctx)])  14.5 us
    pallas_call x2, Pallas kernels, inside_part(): kernel(functools.partial(inside_kernel, first=start, shifts=n_head if fet...  7.19 us
    pallas_call x2, Pallas kernels, half_states(): kernel(functools.partial(half_kernel, blocks=half, group=group, tokens=to...  6.41 us
    all_to_all x1, starting transfers between devices, local(): lax.all_to_all(states, 'ctx', 0, 0, axis_index_groups=groups, tiled=True)  3.82 us
    pallas_call x1, Pallas kernels, local(): kernel(functools.partial(mixed_kernel, shifts=n_head), (shape((tokens, he...  3.36 us
    unnamed x18, local copies, waits for them, and re-layouts  2.92 us
    pallas_call x1, Pallas kernels, local(): kernel(pack_kernel, (shape((packed_rows, DK), BF16),) * group + (shape((g...  2.09 us
    ppermute x8, waiting for transfers between devices, swapped(): return lax.ppermute(array, 'ctx', [(i, i ^ distance) for i in range(n_ctx)])  1.96 us
  transfers between devices with their start and end apart: 10, of which 4 were waited for; matrix products, arithmetic and copies ran while one was open for 0% of the time, Pallas kernels for 26%

profile of v2, /device:TPU:0, one launch (start us, length us, event | category | flops | bytes accessed | tf_op | source)
XLA Modules:
  0.0 46.8 jit_solution(3105326887314943493)
XLA Ops:
  0.0 2.1 %pack.1 = (bf16[400,128]{1,0:T(8,128)(2,1)}, bf16[400,128]{1,0:T(8,128)(2,1)}, bf16[400,128]{1,0:T(8,128)(2,1)}, bf16[400,128]{1,0:T(8,128)(2,1)}, bf16[400,128]...) custom-call(bf16[128,1024]{1,0:T(8,128)(2,1)} %key_ref.3, ...), custom_call_target="tpu_custom_call" | custom-call | flops 2000000000 | bytes 1048576 | tf_op jit(solution)/shard_map/pack/pallas_call | solution.py:500
  2.1 3.0 %collective-permute-start.4 = (bf16[400,128]{1,0:T(8,128)(2,1)}, bf16[400,128]{1,0:T(8,128)(2,1)S(1)}, u32[]{:S(2)}, u32[]{:S(2)}) collective-permute-start(bf16[400,128]{1,0:T(8,128)(2,1)} %get-tuple-element.49), channel_id=1, source_target_pairs={{0,2},{2,0},{4,6},{6,4},{8,10},{10,8},{12,14},{14,12},{16,18},{18,... | collective-permute-start | bytes 307208 | tf_op jit(solution)/shard_map/ppermute | solution.py:496
  5.1 1.5 %collective-permute-start.5 = (bf16[400,128]{1,0:T(8,128)(2,1)}, bf16[400,128]{1,0:T(8,128)(2,1)S(1)}, u32[]{:S(2)}, u32[]{:S(2)}) collective-permute-start(bf16[400,128]{1,0:T(8,128)(2,1)} %get-tuple-element.50), channel_id=1, source_target_pairs={{0,4},{2,6},{4,0},{6,2},{8,12},{10,14},{12,8},{14,10},{16,20},{18,... | collective-permute-start | bytes 307208 | tf_op jit(solution)/shard_map/ppermute | solution.py:496
  6.6 0.0 collective-permute-start.6
  6.6 2.0 %collective-permute-start = (bf16[400,128]{1,0:T(8,128)(2,1)}, bf16[400,128]{1,0:T(8,128)(2,1)S(1)}, u32[]{:S(2)}, u32[]{:S(2)}) collective-permute-start(bf16[400,128]{1,0:T(8,128)(2,1)} %get-tuple-element.44), channel_id=1, source_target_pairs={{0,8},{2,10},{4,12},{6,14},{8,0},{10,2},{12,4},{14,6},{16,24},{18,... | collective-permute-start | bytes 307208 | tf_op jit(solution)/shard_map/ppermute | solution.py:496
  8.7 1.4 %collective-permute-start.1 = (bf16[400,128]{1,0:T(8,128)(2,1)}, bf16[400,128]{1,0:T(8,128)(2,1)S(1)}, u32[]{:S(2)}, u32[]{:S(2)}) collective-permute-start(bf16[400,128]{1,0:T(8,128)(2,1)} %get-tuple-element.45), channel_id=1, source_target_pairs={{0,10},{2,8},{4,14},{6,12},{8,2},{10,0},{12,6},{14,4},{16,26},{18,... | collective-permute-start | bytes 307208 | tf_op jit(solution)/shard_map/ppermute | solution.py:496
  10.1 2.5 %collective-permute-start.2 = (bf16[400,128]{1,0:T(8,128)(2,1)}, bf16[400,128]{1,0:T(8,128)(2,1)S(1)}, u32[]{:S(2)}, u32[]{:S(2)}) collective-permute-start(bf16[400,128]{1,0:T(8,128)(2,1)} %get-tuple-element.46), channel_id=1, source_target_pairs={{0,12},{2,14},{4,8},{6,10},{8,4},{10,6},{12,0},{14,2},{16,28},{18,... | collective-permute-start | bytes 307208 | tf_op jit(solution)/shard_map/ppermute | solution.py:496
  12.6 1.3 %collective-permute-start.3 = (bf16[400,128]{1,0:T(8,128)(2,1)}, bf16[400,128]{1,0:T(8,128)(2,1)S(1)}, u32[]{:S(2)}, u32[]{:S(2)}) collective-permute-start(bf16[400,128]{1,0:T(8,128)(2,1)} %get-tuple-element.47), channel_id=1, source_target_pairs={{0,14},{2,12},{4,10},{6,8},{8,6},{10,4},{12,2},{14,0},{16,30},{18,... | collective-permute-start | bytes 307208 | tf_op jit(solution)/shard_map/ppermute | solution.py:496
  13.9 0.9 %copy-done.7 = bf16[400,128]{1,0:T(8,128)(2,1)S(1)} copy-done((bf16[400,128]{1,0:T(8,128)(2,1)S(1)}, bf16[400,128]{1,0:T(8,128)(2,1)}, u32[]{:S(2)}) %copy-start.7) | copy-done | bytes 102424
  14.8 3.1 %own_half.1 = (f32[8,128,128]{2,1,0:T(8,128)S(1)}, bf16[8,128,128]{2,1,0:T(8,128)(2,1)S(1)}, f32[2,128,128]{2,1,0:T(8,128)S(1)}, f32[2,128,128]{2,1,0:T(8,128)S(1)}) custom-call(bf16[400,128]{1,0:T(8,128)(2,1)S(1)} %copy-done.7, bf16[400,128]{1,0:T(8,128)(2,1)S(1)} %collective-permute-done.4.refs_1_, bf16[400,128]{1,0:T(8,128)(2,1)S(1)} %collective-permute-done.5.refs_2_, ...), custom_call_target="tpu_custom_call" | custom-call | flops 3500000000 | bytes 1048576 | tf_op jit(solution)/shard_map/own_half/pallas_call | solution.py:520
  17.9 0.0 copy-start.2
  18.0 0.0 copy-start.4
  18.0 0.0 copy-start.5
  18.0 0.4 collective-permute-done.2.refs_2_
  18.4 1.3 %collective-permute-done.3.refs_3_ = bf16[400,128]{1,0:T(8,128)(2,1)S(1)} collective-permute-done((bf16[400,128]{1,0:T(8,128)(2,1)}, bf16[400,128]{1,0:T(8,128)(2,1)S(1)}, u32[]{:S(2)}, u32[]{:S(2)}) %collective-permute-start.3) | collective-permute-done | bytes 102432 | tf_op jit(solution)/shard_map/ppermute | solution.py:496
  19.7 3.3 %other_half.1 = (f32[8,128,128]{2,1,0:T(8,128)S(1)}, bf16[8,128,128]{2,1,0:T(8,128)(2,1)S(1)}, f32[2,128,128]{2,1,0:T(8,128)S(1)}, f32[2,128,128]{2,1,0:T(8,128)S(1)}, bf16[2,128,128]{2,1,0:T(8,128)(2,1)S(1)}) custom-call(bf16[400,128]{1,0:T(8,128)(2,1)S(1)} %collective-permute-done.refs_0_, bf16[400,128]{1,0:T(8,128)(2,1)S(1)} %collective-permute-done.1.refs_1_, ...), custom_call_target="tpu_custom_call" | custom-call | flops 3500000000 | bytes 1048576 | tf_op jit(solution)/shard_map/other_half/pallas_call | solution.py:520
  23.0 2.7 %collective-permute-start.7 = (bf16[2,128,128]{2,1,0:T(8,128)(2,1)S(1)}, bf16[2,128,128]{2,1,0:T(8,128)(2,1)S(1)}, u32[]{:S(2)}, u32[]{:S(2)}) collective-permute-start(bf16[2,128,128]{2,1,0:T(8,128)(2,1)S(1)} %get-tuple-element.68), channel_id=1, source_target_pairs={{0,16},{2,18},{4,20},{6,22},{8,24},{10,26},{12,28},{14,30},{16,0},... | collective-permute-start | bytes 196616 | tf_op jit(solution)/shard_map/ppermute | solution.py:496
  25.7 2.3 %inside.2 = (bf16[4,128,128]{2,1,0:T(8,128)(2,1)S(1)}, bf16[4,128,128]{2,1,0:T(8,128)(2,1)S(1)}) custom-call(bf16[128,1024]{1,0:T(8,128)(2,1)S(1)} %copy-done.5, bf16[128,1024]{1,0:T(8,128)(2,1)S(1)} %copy-done.4, bf16[128,2048]{1,0:T(8,128)(2,1)S(1)} %copy-done.2, bf16[128,128]{1,0:T(8,128)(2,1)S(1)} %copy-done.8), custom_call_target="tpu_custom_call" | custom-call | flops 2400000000 | bytes 1048576 | tf_op jit(solution)/shard_map/inside/pallas_call | solution.py:563
  28.0 0.2 collective-permute-done.7.carried_ref
  28.2 1.2 %carry.1 = bf16[8,256,128]{2,1,0:T(8,128)(2,1)} custom-call(f32[8,128,128]{2,1,0:T(8,128)S(1)} %get-tuple-element.56.own_before, bf16[8,128,128]{2,1,0:T(8,128)(2,1)S(1)} %get-tuple-element.57.own_maps, f32[2,128,128]{2,1,0:T(8,128)S(1)} %get-tuple-element.58.refs_4_.own_end, f32[2,128,128]{2,1,0:T(8,128)S(1)} %get-tuple-element.59.refs_5_.own_map, ...), custom_call_target="tpu_custom_call" | custom-call | flops 600000000 | bytes 1048576 | tf_op jit(solution)/shard_map/carry/pallas_call | solution.py:581
  29.5 0.0 copy-start
  29.5 0.0 copy-start.1
  29.5 3.8 %all-to-all-start = ((bf16[8,256,128]{2,1,0:T(8,128)(2,1)}), bf16[8,256,128]{2,1,0:T(8,128)(2,1)S(1)}, u32[]{:S(2)}, u32[]{:S(2)}) async-start(bf16[8,256,128]{2,1,0:T(8,128)(2,1)} %carry.1), calls=%async_computation | async-start | bytes 1048576 | tf_op jit(solution)/shard_map/all_to_all | solution.py:590
  33.3 0.0 copy-start.3
  33.3 1.0 %copy-done.3 = bf16[128,2048]{1,0:T(8,128)(2,1)S(1)} copy-done((bf16[128,2048]{1,0:T(8,128)(2,1)S(1)}, bf16[128,2048]{1,0:T(8,128)(2,1)}, u32[]{:S(2)}) %copy-start.3) | copy-done | bytes 524312
  34.4 0.9 %copy-done.6 = bf16[128,1024]{1,0:T(8,128)(2,1)S(1)} copy-done((bf16[128,1024]{1,0:T(8,128)(2,1)S(1)}, bf16[128,1024]{1,0:T(8,128)(2,1)}, u32[]{:S(2)}) %copy-start.6) | copy-done | bytes 262168
  35.3 4.9 %inside.3 = (bf16[12,128,128]{2,1,0:T(8,128)(2,1)S(1)}, bf16[12,128,128]{2,1,0:T(8,128)(2,1)S(1)}, bf16[2,256,1024]{2,1,0:T(8,128)(2,1)S(1)}) custom-call(bf16[128,1024]{1,0:T(8,128)(2,1)S(1)} %copy-done.6, bf16[128,1024]{1,0:T(8,128)(2,1)S(1)} %copy-done.4, bf16[128,2048]{1,0:T(8,128)(2,1)S(1)} %copy-done.3, bf16[128,128]{1,0:T(8,128)(2,1)S(1)} %copy-done.8, ...), custom_call_target="tpu_custom_call" | custom-call | flops 4000000000 | bytes 1048576 | tf_op jit(solution)/shard_map/inside/pallas_call | solution.py:563
  40.2 0.5 %all-to-all-done.state_ref = bf16[8,256,128]{2,1,0:T(8,128)(2,1)S(1)} async-done(((bf16[8,256,128]{2,1,0:T(8,128)(2,1)}), bf16[8,256,128]{2,1,0:T(8,128)(2,1)S(1)}, u32[]{:S(2)}, u32[]{:S(2)}) %all-to-all-start) | async-done | bytes 524320 | tf_op jit(solution)/shard_map/all_to_all | solution.py:590
  40.7 3.4 %mixed.1 = (bf16[128,2048]{1,0:T(8,128)(2,1)S(1)}, bf16[4,256,1024]{2,1,0:T(8,128)(2,1)S(1)}, bf16[128,1024]{1,0:T(8,128)(2,1)S(1)}) custom-call(bf16[8,256,128]{2,1,0:T(8,128)(2,1)S(1)} %all-to-all-done.state_ref, bf16[4,128,128]{2,1,0:T(8,128)(2,1)S(1)} %get-tuple-element.74.first_inside, bf16[4,128,128]{2,1,0:T(8,128)(2,1)S(1)} %get-tuple-element.75.first_window, ...), custom_call_target="tpu_custom_call" | custom-call | flops 2500000000 | bytes 1048576 | tf_op jit(solution)/shard_map/mixed/pallas_call | solution.py:595
  44.1 0.1 collective-permute-start.8
  44.2 1.8 %own_columns.1 = bf16[128,1024]{1,0:T(8,128)(2,1)S(1)} custom-call(bf16[128,2048]{1,0:T(8,128)(2,1)S(1)} %get-tuple-element.80.mixed_ref, bf16[4,256,1024]{2,1,0:T(8,128)(2,1)S(1)} %get-tuple-element.81.early_ref, bf16[2048,2048]{1,0:T(8,128)(2,1)} %weight_hbm.3), custom_call_target="tpu_custom_call" | custom-call | flops 2000000000 | bytes 1048576 | tf_op jit(solution)/shard_map/own_columns/pallas_call | solution.py:615
  46.0 0.8 %add_convert_fusion = bf16[128,1024]{1,0:T(8,128)(2,1)} fusion(bf16[128,1024]{1,0:T(8,128)(2,1)S(1)} %collective-permute-done.8, bf16[128,1024]{1,0:T(8,128)(2,1)S(1)} %own_columns.1), kind=kLoop, calls=%fused_computation | loop fusion | flops 524288 | bytes 786432 | tf_op jit(solution)/shard_map/convert_element_type | solution.py:629
  (15 shorter events, 0.0 us)
Async XLA Ops:
  2.1 8.0 %collective-permute-start.4 = (bf16[400,128]{1,0:T(8,128)(2,1)}, bf16[400,128]{1,0:T(8,128)(2,1)S(1)}, u32[]{:S(2)}, u32[]{:S(2)}) collective-permute-start(bf16[400,128]{1,0:T(8,128)(2,1)} %get-tuple-element.49), channel_id=1, source_target_pairs={{0,2},{2,0},{4,6},{6,4},{8,10},{10,8},{12,14},{14,12},{16,18},{18,... | collective-permute-start | bytes 307208 | tf_op jit(solution)/shard_map/ppermute | solution.py:496
  5.1 7.5 %collective-permute-start.5 = (bf16[400,128]{1,0:T(8,128)(2,1)}, bf16[400,128]{1,0:T(8,128)(2,1)S(1)}, u32[]{:S(2)}, u32[]{:S(2)}) collective-permute-start(bf16[400,128]{1,0:T(8,128)(2,1)} %get-tuple-element.50), channel_id=1, source_target_pairs={{0,4},{2,6},{4,0},{6,2},{8,12},{10,14},{12,8},{14,10},{16,20},{18,... | collective-permute-start | bytes 307208 | tf_op jit(solution)/shard_map/ppermute | solution.py:496
  6.6 7.3 %collective-permute-start.6 = (bf16[400,128]{1,0:T(8,128)(2,1)}, bf16[400,128]{1,0:T(8,128)(2,1)S(1)}, u32[]{:S(2)}, u32[]{:S(2)}) collective-permute-start(bf16[400,128]{1,0:T(8,128)(2,1)} %get-tuple-element.51), channel_id=1, source_target_pairs={{0,6},{2,4},{4,2},{6,0},{8,14},{10,12},{12,10},{14,8},{16,22},{18,... | collective-permute-start | bytes 307208 | tf_op jit(solution)/shard_map/ppermute | solution.py:496
  6.6 11.4 %collective-permute-start = (bf16[400,128]{1,0:T(8,128)(2,1)}, bf16[400,128]{1,0:T(8,128)(2,1)S(1)}, u32[]{:S(2)}, u32[]{:S(2)}) collective-permute-start(bf16[400,128]{1,0:T(8,128)(2,1)} %get-tuple-element.44), channel_id=1, source_target_pairs={{0,8},{2,10},{4,12},{6,14},{8,0},{10,2},{12,4},{14,6},{16,24},{18,... | collective-permute-start | bytes 307208 | tf_op jit(solution)/shard_map/ppermute | solution.py:496
  8.7 9.3 %collective-permute-start.1 = (bf16[400,128]{1,0:T(8,128)(2,1)}, bf16[400,128]{1,0:T(8,128)(2,1)S(1)}, u32[]{:S(2)}, u32[]{:S(2)}) collective-permute-start(bf16[400,128]{1,0:T(8,128)(2,1)} %get-tuple-element.45), channel_id=1, source_target_pairs={{0,10},{2,8},{4,14},{6,12},{8,2},{10,0},{12,6},{14,4},{16,26},{18,... | collective-permute-start | bytes 307208 | tf_op jit(solution)/shard_map/ppermute | solution.py:496
  10.1 8.4 %collective-permute-start.2 = (bf16[400,128]{1,0:T(8,128)(2,1)}, bf16[400,128]{1,0:T(8,128)(2,1)S(1)}, u32[]{:S(2)}, u32[]{:S(2)}) collective-permute-start(bf16[400,128]{1,0:T(8,128)(2,1)} %get-tuple-element.46), channel_id=1, source_target_pairs={{0,12},{2,14},{4,8},{6,10},{8,4},{10,6},{12,0},{14,2},{16,28},{18,... | collective-permute-start | bytes 307208 | tf_op jit(solution)/shard_map/ppermute | solution.py:496
  12.6 7.1 %collective-permute-start.3 = (bf16[400,128]{1,0:T(8,128)(2,1)}, bf16[400,128]{1,0:T(8,128)(2,1)S(1)}, u32[]{:S(2)}, u32[]{:S(2)}) collective-permute-start(bf16[400,128]{1,0:T(8,128)(2,1)} %get-tuple-element.47), channel_id=1, source_target_pairs={{0,14},{2,12},{4,10},{6,8},{8,6},{10,4},{12,2},{14,0},{16,30},{18,... | collective-permute-start | bytes 307208 | tf_op jit(solution)/shard_map/ppermute | solution.py:496
  13.9 0.9 %copy-start.7 = (bf16[400,128]{1,0:T(8,128)(2,1)S(1)}, bf16[400,128]{1,0:T(8,128)(2,1)}, u32[]{:S(2)}) copy-start(bf16[400,128]{1,0:T(8,128)(2,1)} %get-tuple-element.48.refs_0_) | copy-start | bytes 307204
  17.9 7.7 %copy-start.2 = (bf16[128,2048]{1,0:T(8,128)(2,1)S(1)}, bf16[128,2048]{1,0:T(8,128)(2,1)}, u32[]{:S(2)}) copy-start(bf16[128,2048]{1,0:T(8,128)(2,1)} %value_ref.3) | copy-start | bytes 1572868
  18.0 7.7 %copy-start.4 = (bf16[128,1024]{1,0:T(8,128)(2,1)S(1)}, bf16[128,1024]{1,0:T(8,128)(2,1)}, u32[]{:S(2)}) copy-start(bf16[128,1024]{1,0:T(8,128)(2,1)} %key_ref.3) | copy-start | bytes 786436
  18.0 7.7 %copy-start.5 = (bf16[128,1024]{1,0:T(8,128)(2,1)S(1)}, bf16[128,1024]{1,0:T(8,128)(2,1)}, u32[]{:S(2)}) copy-start(bf16[128,1024]{1,0:T(8,128)(2,1)} %query_ref.3) | copy-start | bytes 786436
  18.0 7.7 %copy-start.8 = (bf16[128,128]{1,0:T(8,128)(2,1)S(1)}, bf16[128,128]{1,0:T(8,128)(2,1)}, u32[]{:S(2)}) copy-start(bf16[128,128]{1,0:T(8,128)(2,1)} %get-tuple-element.76.rows_ref) | copy-start | bytes 98308
  23.0 5.2 %collective-permute-start.7 = (bf16[2,128,128]{2,1,0:T(8,128)(2,1)S(1)}, bf16[2,128,128]{2,1,0:T(8,128)(2,1)S(1)}, u32[]{:S(2)}, u32[]{:S(2)}) collective-permute-start(bf16[2,128,128]{2,1,0:T(8,128)(2,1)S(1)} %get-tuple-element.68), channel_id=1, source_target_pairs={{0,16},{2,18},{4,20},{6,22},{8,24},{10,26},{12,28},{14,30},{16,0},... | collective-permute-start | bytes 196616 | tf_op jit(solution)/shard_map/ppermute | solution.py:496
  29.5 11.3 %copy-start = (bf16[128,2048]{1,0:T(8,128)(2,1)S(1)}, bf16[128,2048]{1,0:T(8,128)(2,1)}, u32[]{:S(2)}) copy-start(bf16[128,2048]{1,0:T(8,128)(2,1)} %gate_ref.1) | copy-start | bytes 1572868
  29.5 11.3 %copy-start.1 = (f32[128]{0:T(128)S(1)}, f32[128]{0:T(128)}, u32[]{:S(2)}) copy-start(f32[128]{0:T(128)} %param.14) | copy-start | bytes 1540
  29.5 11.3 %all-to-all-start = ((bf16[8,256,128]{2,1,0:T(8,128)(2,1)}), bf16[8,256,128]{2,1,0:T(8,128)(2,1)S(1)}, u32[]{:S(2)}, u32[]{:S(2)}) async-start(bf16[8,256,128]{2,1,0:T(8,128)(2,1)} %carry.1), calls=%async_computation | async-start | bytes 1048576 | tf_op jit(solution)/shard_map/all_to_all | solution.py:590
  33.3 1.0 %copy-start.3 = (bf16[128,2048]{1,0:T(8,128)(2,1)S(1)}, bf16[128,2048]{1,0:T(8,128)(2,1)}, u32[]{:S(2)}) copy-start(bf16[128,2048]{1,0:T(8,128)(2,1)} %value_ref.3) | copy-start | bytes 1572868
  34.4 0.9 %copy-start.6 = (bf16[128,1024]{1,0:T(8,128)(2,1)S(1)}, bf16[128,1024]{1,0:T(8,128)(2,1)}, u32[]{:S(2)}) copy-start(bf16[128,1024]{1,0:T(8,128)(2,1)} %query_ref.3) | copy-start | bytes 786436
  44.1 1.9 %collective-permute-start.8 = (bf16[128,1024]{1,0:T(8,128)(2,1)S(1)}, bf16[128,1024]{1,0:T(8,128)(2,1)S(1)}, u32[]{:S(2)}, u32[]{:S(2)}) collective-permute-start(bf16[128,1024]{1,0:T(8,128)(2,1)S(1)} %get-tuple-element.82), channel_id=1, source_target_pairs={{0,1},{1,0},{2,3},{3,2},{4,5},{5,4},{6,7},{7,6},{8,9},{9,8},{10,11... | collective-permute-start | bytes 786440 | tf_op jit(solution)/shard_map/ppermute | solution.py:612

commit v3 on v1

--- a/solution.py
+++ b/solution.py
@@ -14,7 +14,6 @@
 REP = HV // HK
 SMALL_BITS = 4
 SMALL_ROWS = 1 << SMALL_BITS
-CHUNKS = 8
 BASE_BITS = 3
 BASE = 1 << BASE_BITS
 PIECE_ROWS = 8
@@ -213,16 +212,8 @@
     return solved(lowers, rights, tokens), works
 
 
-def inside_kernel(query_ref, key_ref, value_ref, rows_ref, *refs, first, shifts=0):
-    copies = []
-    if shifts:
-        weight_hbm, inside_ref, window_ref, early_ref, sems = refs
-        target = lax.rem(lax.axis_index("head") + 1, shifts)
-        copies = weight_copies(weight_hbm, target, 0, early_ref, sems)
-    else:
-        inside_ref, window_ref = refs
+def inside_heads(query_ref, key_ref, value_ref, rows_ref, inside_ref, window_ref, first, blocks):
     tokens = query_ref.shape[0]
-    blocks = inside_ref.shape[0] // REP
 
     def columns(ref, start, size):
         return ref[:, start * size : (start + 1) * size]
@@ -253,25 +244,53 @@
             _, cum_col, _, _, factors = works[at]
             scores = (products * factors).astype(BF16)
             both = nn(scores, sides[at].astype(BF16))
-            inside_ref[at] = both[:, :DV].astype(BF16)
-            window_ref[at] = (jnp.exp(cum_col) * queries - both[:, DV:]).astype(BF16)
-    for copy in copies:
-        copy.wait()
+            to = first * REP + at
+            inside_ref[to] = both[:, :DV].astype(BF16)
+            window_ref[to] = (jnp.exp(cum_col) * queries - both[:, DV:]).astype(BF16)
+
+
+def early_inside_kernel(*refs, group):
+    @pl.when(lax.axis_index("ctx") < group)
+    def _():
+        inside_heads(*refs, 0, group // 2)
+
+
+def inside_kernel(early_inside, early_window, *refs, group):
+    known = (group // 2) * REP
+    first_group = lax.axis_index("ctx") < group
+
+    @pl.when(first_group)
+    def _():
+        inside_ref, window_ref = refs[-2:]
+        inside_ref[0:known] = early_inside[...]
+        window_ref[0:known] = early_window[...]
+        inside_heads(*refs, group // 2, group - group // 2)
+
+    @pl.when(jnp.logical_not(first_group))
+    def _():
+        inside_heads(*refs, 0, group)
 
 
 def in_order(own_half, own, other):
     return jnp.where(own_half == 0, own, other), jnp.where(own_half == 0, other, own)
 
 
-def half_kernel(*refs, blocks, group, tokens, own, with_map):
-    taken, refs = refs[:blocks], refs[blocks:]
+def half_kernel(*refs, blocks, extra, group, tokens, own, with_map):
+    count = blocks + extra if own else blocks - extra
+    taken, refs = refs[:count], refs[count:]
     if not own:
         (own_end, own_map), refs = refs[:2], refs[2:]
+    known = ()
+    if extra and not own:
+        known, refs = refs[:3], refs[3:]
     before_ref, map_ref, end_ref, end_map_ref, *refs = refs
     if not own:
         group_ref, *refs = refs
         if with_map:
             group_map_ref, *refs = refs
+    handed = ()
+    if extra and own:
+        handed, refs = refs[:3], refs[3:]
     offsets, removals, decays = refs
     place = place_in_group(group)
     low = lax.rem(place, blocks)
@@ -284,18 +303,24 @@
         jnp.concatenate([t[base : base + SMALL_ROWS, :][:, :tokens] for t in taken], axis=0),
         tokens,
     )
-    for b in range(blocks):
+    if known:
+        for held, ref in zip((offsets, removals, decays), known):
+            held[0 : extra * REP] = ref[...]
+    for b in range(count):
         keys_turned = works[b * REP][0].T
         for r in range(REP):
             at = b * REP + r
             _, cum_col, key_col, _, _ = works[at]
             last = cum_col[tokens - 1 : tokens, :]
-            decays[at] = jnp.broadcast_to(jnp.exp(last), (PIECE_ROWS, DK))
             tail = key_col * jnp.exp(last - cum_col)
             tail = jnp.concatenate([tail, tail], axis=1)
             both = nn(keys_turned, (sides[at] * tail).astype(BF16))
-            offsets[at] = both[:, :DV]
-            removals[at] = both[:, DV:].astype(BF16)
+            to, held = at if own else at + extra * REP, (offsets, removals, decays)
+            if own and b >= blocks:
+                to, held = at - blocks * REP, handed
+            held[0][to] = both[:, :DV]
+            held[1][to] = both[:, DV:].astype(BF16)
+            held[2][to] = jnp.broadcast_to(jnp.exp(last), (PIECE_ROWS, DK))
 
     key_row, key_col = iotas((DK, DK))
     eye = (key_row == key_col).astype(F32)
@@ -344,9 +369,9 @@
 
 def carry_kernel(
     own_before, own_maps, own_end, own_map, other_before, other_maps, other_end, other_map,
-    carried_ref, out_ref, held, sems,
+    carried_ref, out_ref,
 ):
-    group = held.shape[0]
+    group = out_ref.shape[0]
     half = group // 2
     place = place_in_group(group)
     own_half = place // half
@@ -358,100 +383,44 @@
         first_map, _ = in_order(own_half, own_map[r], other_map[r])
         middle = first_end + nn(first_map.astype(BF16), carried.astype(BF16))
         starts.append([x.astype(BF16) for x in in_order(own_half, carried, middle)])
-    copies = []
     for s in range(group):
         before, maps = (own_before, own_maps) if s < half else (other_before, other_maps)
         for r in range(REP):
             at = (s % half) * REP + r
             start = starts[r][0] if s < half else starts[r][1]
-            held[s, r * DK : (r + 1) * DK, :] = (before[at] + nn(maps[at], start)).astype(BF16)
-        copies.append(pltpu.make_async_copy(held.at[s], out_ref.at[place ^ s], sems.at[s]))
-        copies[-1].start()
-    for copy in copies:
-        copy.wait()
-
-
-def weight_copies(weight_hbm, target, first, held, sems):
-    count, depth, width = held.shape
-    columns = pl.ds(pl.multiple_of(target * width, width), width)
-    copies = [
-        pltpu.make_async_copy(
-            weight_hbm.at[pl.ds((first + c) * depth, depth), columns], held.at[c], sems.at[c]
-        )
-        for c in range(count)
-    ]
-    for copy in copies:
-        copy.start()
-    return copies
-
-
-def project(chunk_of, targets):
-    totals = [None] * len(targets)
-    for c in range(len(targets[0])):
-        rows = chunk_of(c)
-        for n, chunks in enumerate(targets):
-            chunk, copy = chunks[c]
-            if copy is not None:
-                copy.wait()
-            part = nn(rows, chunk[...])
-            totals[n] = part if totals[n] is None else totals[n] + part
-    return [total.astype(BF16) for total in totals]
+            out_ref[place ^ s, r * DK : (r + 1) * DK, :] = (
+                before[at] + nn(maps[at], start)
+            ).astype(BF16)
+
+
+def columns_of(width, target):
+    return pl.ds(pl.multiple_of(target * width, width), width)
 
 
 def mixed_kernel(
-    state_ref, first_inside, first_window, second_inside, second_window, gate_ref, gain_ref,
-    early_ref, weight_hbm, mixed_ref, own_early_ref, *refs, shifts,
+    state_ref, inside_ref, window_ref, gate_ref, gain_ref, weight_ref, mixed_ref, *out_refs, shifts
 ):
-    out_refs, (held, sems, own_sems) = refs[:-3], refs[-3:]
     me = lax.axis_index("head")
-    early, depth, _ = early_ref.shape
-    chunks = held.shape[0] // (shifts - 1)
-    targets = []
-    for n in range(shifts - 1):
-        known = early if n == 0 else 0
-        slots = pl.ds(n * chunks, chunks - known)
-        copies = weight_copies(
-            weight_hbm, lax.rem(me + 1 + n, shifts), known, held.at[slots], sems.at[slots]
-        )
-        targets.append(
-            [(early_ref.at[c], None) for c in range(known)]
-            + [(held.at[n * chunks + c], copy) for c, copy in enumerate(copies)]
-        )
-    own_copies = weight_copies(weight_hbm, me, 0, own_early_ref, own_sems)
     gain = gain_ref[...]
-    split = first_inside.shape[0]
-
-    def head(h):
-        inside, window, at = (
-            (first_inside, first_window, h) if h < split
-            else (second_inside, second_window, h - split)
-        )
-        j, r = h // REP, h % REP
-        columns = pl.ds(h * DV, DV)
-        rows = inside[at].astype(F32) + nn(window[at], state_ref[j, r * DK : (r + 1) * DK, :])
-        scale = lax.rsqrt(jnp.mean(rows * rows, axis=1, keepdims=True) + EPSILON)
-        gate = gate_ref[:, columns].astype(F32)
-        mixed = (rows * scale * gain * (gate / (1.0 + jnp.exp(-gate)))).astype(BF16)
-        mixed_ref[:, columns] = mixed
-        return mixed
-
-    def chunk_of(c):
-        return jnp.concatenate(
-            [head(h) for h in range(c * depth // DV, (c + 1) * depth // DV)], axis=1
-        )
-
-    for out_ref, total in zip(out_refs, project(chunk_of, targets)):
-        out_ref[...] = total
-    for copy in own_copies:
-        copy.wait()
-
-
-def own_columns_kernel(mixed_ref, early_ref, weight_hbm, out_ref, held, sems):
-    early, depth, _ = early_ref.shape
-    copies = weight_copies(weight_hbm, lax.axis_index("head"), early, held, sems)
-    chunks = [(early_ref.at[c], None) for c in range(early)]
-    chunks += [(held.at[c], copy) for c, copy in enumerate(copies)]
-    (out_ref[...],) = project(lambda c: mixed_ref[:, c * depth : (c + 1) * depth], [chunks])
+    for j in range(state_ref.shape[0]):
+        for r in range(REP):
+            h = j * REP + r
+            columns = pl.ds(h * DV, DV)
+            state = state_ref[j, r * DK : (r + 1) * DK, :]
+            rows = inside_ref[h].astype(F32) + nn(window_ref[h], state)
+            scale = lax.rsqrt(jnp.mean(rows * rows, axis=1, keepdims=True) + EPSILON)
+            gate = gate_ref[:, columns].astype(F32)
+            mixed_ref[:, columns] = (
+                rows * scale * gain * (gate / (1.0 + jnp.exp(-gate)))
+            ).astype(BF16)
+    for n, out_ref in enumerate(out_refs):
+        columns = columns_of(out_ref.shape[1], lax.rem(me + 1 + n, shifts))
+        out_ref[...] = nn(mixed_ref[...], weight_ref[:, columns]).astype(BF16)
+
+
+def own_columns_kernel(mixed_ref, weight_ref, out_ref):
+    columns = columns_of(out_ref.shape[1], lax.axis_index("head"))
+    out_ref[...] = nn(mixed_ref[...], weight_ref[:, columns]).astype(BF16)
 
 
 def local(
@@ -464,7 +433,6 @@
     half = group // 2
     width = out_weight.shape[1] // n_head
     n_groups = n_ctx // group
-    groups = [list(range(g, g + group)) for g in range(0, n_ctx, group)]
     packed_rows = (1 + REP) * tokens + SMALL_ROWS
     mib = 1024 * 1024
 
@@ -474,7 +442,7 @@
             out_shape=out,
             scratch_shapes=scratch,
             compiler_params=pltpu.CompilerParams(
-                vmem_limit_bytes=None if limit is None else limit * mib
+                vmem_limit_bytes=None if limit is None else int(limit * mib)
             ),
             cost_estimate=pl.CostEstimate(
                 flops=int(micros * 1e9), bytes_accessed=mib, transcendentals=0
@@ -513,10 +481,20 @@
     )(key_proj, value_proj, write_strength.T, log_decay.T)
     taken = [packed[0]] + [swapped(packed[s], s) for s in range(1, group)]
 
+    extra = 1 if half >= 4 else 0
+
     def half_states(blocks, more, name):
         own, with_map = not more, n_groups > 2
+        passed = (
+            shape((extra * REP, DK, DV), F32),
+            shape((extra * REP, DK, DK), BF16),
+            shape((extra * REP, PIECE_ROWS, DK), F32),
+        )
         return kernel(
-            functools.partial(half_kernel, blocks=half, group=group, tokens=tokens, own=own, with_map=with_map),
+            functools.partial(
+                half_kernel, blocks=half, extra=extra, group=group, tokens=tokens, own=own,
+                with_map=with_map,
+            ),
             (
                 shape((half * REP, DK, DV), F32),
                 shape((half * REP, DK, DK), BF16),
@@ -524,7 +502,8 @@
                 shape((REP, DK, DK), F32),
             )
             + (() if own else (shape((REP, DK, DV), BF16),))
-            + ((shape((REP, DK, DK), F32),) if with_map and not own else ()),
+            + ((shape((REP, DK, DK), F32),) if with_map and not own else ())
+            + (passed if own and extra else ()),
             name,
             16,
             3.5,
@@ -535,9 +514,24 @@
             ],
         )(*blocks, *more)
 
-    own = half_states(taken[:half], (), "own_half")
-    later, own = lax.optimization_barrier((taken[half:], own))
+    own = half_states(taken[: half + extra], (), "own_half")
+    later, own = lax.optimization_barrier((taken[half + extra :], own))
     *other, end = half_states(later, own[2:], "other_half")
+    own = own[:4]
+
+    def inside_part(body, name, count, micros, operands):
+        return kernel(
+            functools.partial(body, group=group),
+            (shape((count, tokens, DV), BF16), shape((count, tokens, DK), BF16)),
+            name,
+            16,
+            micros,
+        )(*operands)
+
+    rows, end = lax.optimization_barrier((rows, end))
+    activations = (query_proj, key_proj, value_proj, rows)
+    early = inside_part(early_inside_kernel, "early_inside", half * REP, 3, activations)
+    end, *early = lax.optimization_barrier((end, *early))
 
     if n_groups == 2:
         carried = swapped(end, group)
@@ -554,74 +548,28 @@
     else:
         carried = jnp.zeros((REP, DK, DV), BF16)
 
-    chunks = min(CHUNKS, out_weight.shape[0] // DV)
-    depth = out_weight.shape[0] // chunks
-
-    def inside_part(start, count, rows, micros, limit, fetch):
-        return kernel(
-            functools.partial(inside_kernel, first=start, shifts=n_head if fetch else 0),
-            (
-                shape((count * REP, tokens, DV), BF16),
-                shape((count * REP, tokens, DK), BF16),
-            )
-            + ((shape((fetch, depth, width), BF16),) if fetch else ()),
-            "inside",
-            limit,
-            micros,
-            scratch=[pltpu.SemaphoreType.DMA((fetch,))] if fetch else (),
-            specs=[vmem] * 4 + ([any_space] if fetch else []),
-        )(query_proj, key_proj, value_proj, rows, *((out_weight,) if fetch else ()))
-
-    early = half
-    rows, end = lax.optimization_barrier((rows, end))
-    first = inside_part(0, early, rows, 2.4, 16, 0)
-    carried, first = lax.optimization_barrier((carried, first))
+    inside, window = inside_part(inside_kernel, "inside", heads, 5, (*early, *activations))
+    carried, inside, window = lax.optimization_barrier((carried, inside, window))
     states = kernel(
-        carry_kernel,
-        shape((group, REP * DK, DV), BF16),
-        "carry",
-        8,
-        0.6,
-        scratch=[pltpu.VMEM((group, REP * DK, DV), BF16), pltpu.SemaphoreType.DMA((group,))],
-        out_specs=any_space,
+        carry_kernel, shape((group, REP * DK, DV), BF16), "carry", 8, 0.6
     )(*own, *other, carried)
+    groups = [list(range(g, g + group)) for g in range(0, n_ctx, group)]
     state_in = lax.all_to_all(states, "ctx", 0, 0, axis_index_groups=groups, tiled=True)
-    rows, states = lax.optimization_barrier((rows, states))
-    *second, weight_rows = inside_part(early, group - early, rows, 4, 44, chunks // 4)
-
-    early_shape = shape((chunks // 2, depth, width), BF16)
-    mixed, own_rows, *others = kernel(
+
+    mixed, *others = kernel(
         functools.partial(mixed_kernel, shifts=n_head),
-        (shape((tokens, heads * DV), BF16), early_shape)
-        + (shape((tokens, width), BF16),) * (n_head - 1),
+        (shape((tokens, heads * DV), BF16),) + (shape((tokens, width), BF16),) * (n_head - 1),
         "mixed",
-        43,
-        2.5,
-        scratch=[
-            pltpu.VMEM(((n_head - 1) * chunks, depth, width), BF16),
-            pltpu.SemaphoreType.DMA(((n_head - 1) * chunks,)),
-            pltpu.SemaphoreType.DMA((chunks // 2,)),
-        ],
-        specs=[vmem] * 8 + [any_space],
-    )(
-        state_in, *first, *second, gate_proj, norm_gain.reshape(1, DV), weight_rows, out_weight
-    )
+        16,
+        2,
+    )(state_in, inside, window, gate_proj, norm_gain.reshape(1, DV), out_weight)
     received = [
         lax.ppermute(other, "head", [(i, (i + 1 + s) % n_head) for i in range(n_head)])
         for s, other in enumerate(others)
     ]
-    total = kernel(
-        own_columns_kernel,
-        shape((tokens, width), BF16),
-        "own_columns",
-        46,
-        2,
-        scratch=[
-            pltpu.VMEM((chunks - chunks // 2, depth, width), BF16),
-            pltpu.SemaphoreType.DMA((chunks - chunks // 2,)),
-        ],
-        specs=[vmem] * 2 + [any_space],
-    )(mixed, own_rows, out_weight).astype(F32)
+    total = kernel(own_columns_kernel, shape((tokens, width), BF16), "own_columns", 16, 1)(
+        mixed, out_weight
+    ).astype(F32)
     for other in received:
         total = total + other.astype(F32)
     return total.astype(BF16)

time: 48.2 us -> 46.9 us (0.973)
  blocking collectives: 0 us -> 11 us
  starting transfers between devices: 18.4 us -> 12 us
  Pallas kernels: 22.2 us -> 17.8 us
  local copies, waits for them, and re-layouts: 2.92 us -> 0.94 us
  waiting for transfers between devices: 3.22 us -> 3.9 us
    all_to_all x0 -> x1, blocking collectives: none -> 11 us  [local(): lax.all_to_all(states, 'ctx', 0, 0, axis_index_groups=groups, tiled=True)]
    all_to_all x1 -> x0, starting transfers between devices: 3.82 us -> none  [local(): lax.all_to_all(states, 'ctx', 0, 0, axis_index_groups=groups, tiled=True)]
    ppermute x8, starting transfers between devices: 14.5 us -> 11.9 us  [swapped(): return lax.ppermute(array, 'ctx', [(i, i ^ distance) for i in range(n_ctx)])]
    pallas_call x1, Pallas kernels: 3.63 us -> 1.35 us  [local(): kernel(functools.partial(mixed_kernel, shifts=n_head), (shape((tokens, he...]
    pallas_call x6, Pallas kernels: 16.5 us -> 14.3 us  [the longest x2 6.56 us: inside_part(): kernel(functools.partial(body, group=group), (shape((count, tokens, DV),...]
    unnamed x18, local copies, waits for them, and re-layouts: 2.92 us -> 0.94 us
    all_to_all x1 -> x0, waiting for transfers between devices: 1.5 us -> none  [local(): lax.all_to_all(states, 'ctx', 0, 0, axis_index_groups=groups, tiled=True)]
    ppermute x8, waiting for transfers between devices: 1.72 us -> 3.15 us  [swapped(): return lax.ppermute(array, 'ctx', [(i, i ^ distance) for i in range(n_ctx)])]
  transfers between devices with their start and end apart: 10 -> 9, of which waited for: 3 -> 4; matrix products, arithmetic and copies ran while one was open for 0% -> 0% of each run, Pallas kernels for 25% -> 16%
where the time goes in v3:
time: 46.9 us; the launch traced here: 46.6 us
  Pallas kernels  17.8 us (38%)
  starting transfers between devices  12 us (26%)
  blocking collectives  11 us (23%)
  waiting for transfers between devices  3.9 us (8%)
  local copies, waits for them, and re-layouts  0.94 us (2%)
  other arithmetic  0.77 us (2%)
    ppermute x8, starting transfers between devices, swapped(): return lax.ppermute(array, 'ctx', [(i, i ^ distance) for i in range(n_ctx)])  11.9 us
    all_to_all x1, blocking collectives, local(): lax.all_to_all(states, 'ctx', 0, 0, axis_index_groups=groups, tiled=True)  11 us
    pallas_call x2, Pallas kernels, inside_part(): kernel(functools.partial(body, group=group), (shape((count, tokens, DV),...  6.56 us
    pallas_call x2, Pallas kernels, half_states(): kernel(functools.partial(half_kernel, blocks=half, extra=extra, group=gro...  6.54 us
    ppermute x8, waiting for transfers between devices, swapped(): return lax.ppermute(array, 'ctx', [(i, i ^ distance) for i in range(n_ctx)])  3.15 us
    pallas_call x1, Pallas kernels, local(): kernel(pack_kernel, (shape((packed_rows, DK), BF16),) * group + (shape((g...  2.09 us
    pallas_call x1, Pallas kernels, local(): kernel(functools.partial(mixed_kernel, shifts=n_head), (shape((tokens, he...  1.35 us
    unnamed x18, local copies, waits for them, and re-layouts  0.94 us
  transfers between devices with their start and end apart: 9, of which 4 were waited for; matrix products, arithmetic and copies ran while one was open for 0% of the time, Pallas kernels for 16%

profile of v3, /device:TPU:0, one launch (start us, length us, event | category | flops | bytes accessed | tf_op | source)
XLA Modules:
  0.0 46.6 jit_solution(1120791599615626625)
XLA Ops:
  0.0 2.1 %pack.1 = (bf16[400,128]{1,0:T(8,128)(2,1)}, bf16[400,128]{1,0:T(8,128)(2,1)}, bf16[400,128]{1,0:T(8,128)(2,1)}, bf16[400,128]{1,0:T(8,128)(2,1)}, bf16[400,128]...) custom-call(bf16[128,1024]{1,0:T(8,128)(2,1)} %refs_1_.3, ...), custom_call_target="tpu_custom_call" | custom-call | flops 2000000000 | bytes 1048576 | tf_op jit(solution)/shard_map/pack/pallas_call | solution.py:466
  2.1 3.0 %collective-permute-start.3 = (bf16[400,128]{1,0:T(8,128)(2,1)}, bf16[400,128]{1,0:T(8,128)(2,1)S(1)}, u32[]{:S(2)}, u32[]{:S(2)}) collective-permute-start(bf16[400,128]{1,0:T(8,128)(2,1)} %get-tuple-element.54), channel_id=1, source_target_pairs={{0,2},{2,0},{4,6},{6,4},{8,10},{10,8},{12,14},{14,12},{16,18},{18,... | collective-permute-start | bytes 307208 | tf_op jit(solution)/shard_map/ppermute | solution.py:462
  5.1 1.5 %collective-permute-start.4 = (bf16[400,128]{1,0:T(8,128)(2,1)}, bf16[400,128]{1,0:T(8,128)(2,1)S(1)}, u32[]{:S(2)}, u32[]{:S(2)}) collective-permute-start(bf16[400,128]{1,0:T(8,128)(2,1)} %get-tuple-element.55), channel_id=1, source_target_pairs={{0,4},{2,6},{4,0},{6,2},{8,12},{10,14},{12,8},{14,10},{16,20},{18,... | collective-permute-start | bytes 307208 | tf_op jit(solution)/shard_map/ppermute | solution.py:462
  6.6 0.0 collective-permute-start.5
  6.6 2.0 %collective-permute-start.6 = (bf16[400,128]{1,0:T(8,128)(2,1)}, bf16[400,128]{1,0:T(8,128)(2,1)S(1)}, u32[]{:S(2)}, u32[]{:S(2)}) collective-permute-start(bf16[400,128]{1,0:T(8,128)(2,1)} %get-tuple-element.57), channel_id=1, source_target_pairs={{0,8},{2,10},{4,12},{6,14},{8,0},{10,2},{12,4},{14,6},{16,24},{18,... | collective-permute-start | bytes 307208 | tf_op jit(solution)/shard_map/ppermute | solution.py:462
  8.7 1.4 %collective-permute-start = (bf16[400,128]{1,0:T(8,128)(2,1)}, bf16[400,128]{1,0:T(8,128)(2,1)S(1)}, u32[]{:S(2)}, u32[]{:S(2)}) collective-permute-start(bf16[400,128]{1,0:T(8,128)(2,1)} %get-tuple-element.50), channel_id=1, source_target_pairs={{0,10},{2,8},{4,14},{6,12},{8,2},{10,0},{12,6},{14,4},{16,26},{18,... | collective-permute-start | bytes 307208 | tf_op jit(solution)/shard_map/ppermute | solution.py:462
  10.1 2.5 %collective-permute-start.1 = (bf16[400,128]{1,0:T(8,128)(2,1)}, bf16[400,128]{1,0:T(8,128)(2,1)S(1)}, u32[]{:S(2)}, u32[]{:S(2)}) collective-permute-start(bf16[400,128]{1,0:T(8,128)(2,1)} %get-tuple-element.51), channel_id=1, source_target_pairs={{0,12},{2,14},{4,8},{6,10},{8,4},{10,6},{12,0},{14,2},{16,28},{18,... | collective-permute-start | bytes 307208 | tf_op jit(solution)/shard_map/ppermute | solution.py:462
  12.6 0.0 collective-permute-done.4.refs_2_
  12.6 1.3 %collective-permute-start.2 = (bf16[400,128]{1,0:T(8,128)(2,1)}, bf16[400,128]{1,0:T(8,128)(2,1)S(1)}, u32[]{:S(2)}, u32[]{:S(2)}) collective-permute-start(bf16[400,128]{1,0:T(8,128)(2,1)} %get-tuple-element.52), channel_id=1, source_target_pairs={{0,14},{2,12},{4,10},{6,8},{8,6},{10,4},{12,2},{14,0},{16,30},{18,... | collective-permute-start | bytes 307208 | tf_op jit(solution)/shard_map/ppermute | solution.py:462
  13.9 0.0 collective-permute-done.5.refs_3_
  13.9 0.9 %copy-done.5 = bf16[400,128]{1,0:T(8,128)(2,1)S(1)} copy-done((bf16[400,128]{1,0:T(8,128)(2,1)S(1)}, bf16[400,128]{1,0:T(8,128)(2,1)}, u32[]{:S(2)}) %copy-start.5) | copy-done | bytes 102424
  14.8 3.5 %own_half.1 = (f32[8,128,128]{2,1,0:T(8,128)S(1)}, bf16[8,128,128]{2,1,0:T(8,128)(2,1)S(1)}, f32[2,128,128]{2,1,0:T(8,128)S(1)}, f32[2,128,128]{2,1,0:T(8,128)S(...) custom-call(bf16[400,128]{1,0:T(8,128)(2,1)S(1)} %copy-done.5, ...), custom_call_target="tpu_custom_call" | custom-call | flops 3500000000 | bytes 1048576 | tf_op jit(solution)/shard_map/own_half/pallas_call | solution.py:493
  18.3 0.0 copy-start.2
  18.3 0.0 copy-start.3
  18.3 0.0 copy-start.4
  18.3 0.1 collective-permute-done.1.refs_1_
  18.4 1.3 %collective-permute-done.2.refs_2_ = bf16[400,128]{1,0:T(8,128)(2,1)S(1)} collective-permute-done((bf16[400,128]{1,0:T(8,128)(2,1)}, bf16[400,128]{1,0:T(8,128)(2,1)S(1)}, u32[]{:S(2)}, u32[]{:S(2)}) %collective-permute-start.2) | collective-permute-done | bytes 102432 | tf_op jit(solution)/shard_map/ppermute | solution.py:462
  19.7 3.1 %other_half.1 = (f32[8,128,128]{2,1,0:T(8,128)S(1)}, bf16[8,128,128]{2,1,0:T(8,128)(2,1)S(1)}, f32[2,128,128]{2,1,0:T(8,128)S(1)}, f32[2,128,128]{2,1,0:T(8,128)S(1)}, bf16[2,128,128]{2,1,0:T(8,128)(2,1)S(1)}) custom-call(bf16[400,128]{1,0:T(8,128)(2,1)S(1)} %collective-permute-done.refs_0_, bf16[400,128]{1,0:T(8,128)(2,1)S(1)} %collective-permute-done.1.refs_1_, ...), custom_call_target="tpu_custom_call" | custom-call | flops 3500000000 | bytes 1048576 | tf_op jit(solution)/shard_map/other_half/pallas_call | solution.py:493
  22.9 3.2 %early_inside.1 = (bf16[8,128,128]{2,1,0:T(8,128)(2,1)S(1)}, bf16[8,128,128]{2,1,0:T(8,128)(2,1)S(1)}) custom-call(bf16[128,1024]{1,0:T(8,128)(2,1)S(1)} %copy-done.4, bf16[128,1024]{1,0:T(8,128)(2,1)S(1)} %copy-done.3, bf16[128,2048]{1,0:T(8,128)(2,1)S(1)} %copy-done.2, bf16[128,128]{1,0:T(8,128)(2,1)S(1)} %copy-done.6), custom_call_target="tpu_custom_call" | custom-call | flops 3000000000 | bytes 1048576 | tf_op jit(solution)/shard_map/early_inside/pallas_call | solution.py:523
  26.0 0.0 slice-start
  26.1 0.0 copy-start
  26.1 0.0 copy-start.1
  26.1 0.1 collective-permute-start.7
  26.2 3.4 %inside.1 = (bf16[16,128,128]{2,1,0:T(8,128)(2,1)S(1)}, bf16[16,128,128]{2,1,0:T(8,128)(2,1)S(1)}) custom-call(bf16[8,128,128]{2,1,0:T(8,128)(2,1)S(1)} %get-tuple-element.86.early_inside, bf16[8,128,128]{2,1,0:T(8,128)(2,1)S(1)} %get-tuple-element.87.early_window, bf16[128,1024]{1,0:T(8,128)(2,1)S(1)} %copy-done.4, bf16[128,1024]{1,0:T(8,128)(2,1)S(1)} %copy-done.3, ...), custom_call_target="tpu_custom_call" | custom-call | flops 5000000000 | bytes 1048576 | tf_op jit(solution)/shard_map/inside/pallas_call | solution.py:523
  29.6 1.8 %collective-permute-done.7.carried_ref = bf16[2,128,128]{2,1,0:T(8,128)(2,1)S(1)} collective-permute-done((bf16[2,128,128]{2,1,0:T(8,128)(2,1)S(1)}, bf16[2,128,128]{2,1,0:T(8,128)(2,1)S(1)}, u32[]{:S(2)}, u32[]{:S(2)}) %collective-permute-start.7) | collective-permute-done | bytes 65568 | tf_op jit(solution)/shard_map/ppermute | solution.py:462
  31.3 0.5 carry.1
  31.8 11.0 %all_to_all.5.state_ref = bf16[8,256,128]{2,1,0:T(8,128)(2,1)S(1)} all-to-all(bf16[8,256,128]{2,1,0:T(8,128)(2,1)S(1)} %carry.1), channel_id=1, replica_groups={{0,2,4,6,8,10,12,14},{16,18,20,22,24,26,28,30},{1,3,5,7,9,11,13,15},{17..., dimensions={0} | all-to-all | bytes 1048576 | tf_op jit(solution)/shard_map/all_to_all | solution.py:557
  42.8 1.3 %mixed.1 = (bf16[128,2048]{1,0:T(8,128)(2,1)S(1)}, bf16[128,1024]{1,0:T(8,128)(2,1)S(1)}) custom-call(bf16[8,256,128]{2,1,0:T(8,128)(2,1)S(1)} %all_to_all.5.state_ref, bf16[16,128,128]{2,1,0:T(8,128)(2,1)S(1)} %get-tuple-element.91.inside_ref, bf16[16,128,128]{2,1,0:T(8,128)(2,1)S(1)} %get-tuple-element.92.window_ref, bf16[128,2048]{1,0:T(8,128)(2,1)S(1)} %copy-done, ...), custom_call_target="tpu_custom_call" | custom-call | flops 2000000000 | bytes 1048576 | tf_op jit(solution)/shard_map/mixed/pallas_call | solution.py:559
  44.2 0.1 collective-permute-start.8
  44.3 0.8 %own_columns.1 = bf16[128,1024]{1,0:T(8,128)(2,1)S(1)} custom-call(bf16[128,2048]{1,0:T(8,128)(2,1)S(1)} %get-tuple-element.93.mixed_ref, bf16[2048,2048]{1,0:T(8,128)(2,1)S(1)} %bitcast.4), custom_call_target="tpu_custom_call" | custom-call | flops 1000000000 | bytes 1048576 | tf_op jit(solution)/shard_map/own_columns/pallas_call | solution.py:570
  45.1 0.7 %collective-permute-done.8 = bf16[128,1024]{1,0:T(8,128)(2,1)S(1)} collective-permute-done((bf16[128,1024]{1,0:T(8,128)(2,1)S(1)}, bf16[128,1024]{1,0:T(8,128)(2,1)S(1)}, u32[]{:S(2)}, u32[]{:S(2)}) %collective-permute-start.8) | collective-permute-done | bytes 262176 | tf_op jit(solution)/shard_map/ppermute | solution.py:567
  45.8 0.8 %add_convert_fusion = bf16[128,1024]{1,0:T(8,128)(2,1)} fusion(bf16[128,1024]{1,0:T(8,128)(2,1)S(1)} %collective-permute-done.8, bf16[128,1024]{1,0:T(8,128)(2,1)S(1)} %own_columns.1), kind=kLoop, calls=%fused_computation | loop fusion | flops 524288 | bytes 786432 | tf_op jit(solution)/shard_map/convert_element_type | solution.py:575
  (15 shorter events, 0.0 us)
Async XLA Ops:
  2.1 8.0 %collective-permute-start.3 = (bf16[400,128]{1,0:T(8,128)(2,1)}, bf16[400,128]{1,0:T(8,128)(2,1)S(1)}, u32[]{:S(2)}, u32[]{:S(2)}) collective-permute-start(bf16[400,128]{1,0:T(8,128)(2,1)} %get-tuple-element.54), channel_id=1, source_target_pairs={{0,2},{2,0},{4,6},{6,4},{8,10},{10,8},{12,14},{14,12},{16,18},{18,... | collective-permute-start | bytes 307208 | tf_op jit(solution)/shard_map/ppermute | solution.py:462
  5.1 7.5 %collective-permute-start.4 = (bf16[400,128]{1,0:T(8,128)(2,1)}, bf16[400,128]{1,0:T(8,128)(2,1)S(1)}, u32[]{:S(2)}, u32[]{:S(2)}) collective-permute-start(bf16[400,128]{1,0:T(8,128)(2,1)} %get-tuple-element.55), channel_id=1, source_target_pairs={{0,4},{2,6},{4,0},{6,2},{8,12},{10,14},{12,8},{14,10},{16,20},{18,... | collective-permute-start | bytes 307208 | tf_op jit(solution)/shard_map/ppermute | solution.py:462
  6.6 7.3 %collective-permute-start.5 = (bf16[400,128]{1,0:T(8,128)(2,1)}, bf16[400,128]{1,0:T(8,128)(2,1)S(1)}, u32[]{:S(2)}, u32[]{:S(2)}) collective-permute-start(bf16[400,128]{1,0:T(8,128)(2,1)} %get-tuple-element.56), channel_id=1, source_target_pairs={{0,6},{2,4},{4,2},{6,0},{8,14},{10,12},{12,10},{14,8},{16,22},{18,... | collective-permute-start | bytes 307208 | tf_op jit(solution)/shard_map/ppermute | solution.py:462
  6.6 7.3 %collective-permute-start.6 = (bf16[400,128]{1,0:T(8,128)(2,1)}, bf16[400,128]{1,0:T(8,128)(2,1)S(1)}, u32[]{:S(2)}, u32[]{:S(2)}) collective-permute-start(bf16[400,128]{1,0:T(8,128)(2,1)} %get-tuple-element.57), channel_id=1, source_target_pairs={{0,8},{2,10},{4,12},{6,14},{8,0},{10,2},{12,4},{14,6},{16,24},{18,... | collective-permute-start | bytes 307208 | tf_op jit(solution)/shard_map/ppermute | solution.py:462
  8.7 9.7 %collective-permute-start = (bf16[400,128]{1,0:T(8,128)(2,1)}, bf16[400,128]{1,0:T(8,128)(2,1)S(1)}, u32[]{:S(2)}, u32[]{:S(2)}) collective-permute-start(bf16[400,128]{1,0:T(8,128)(2,1)} %get-tuple-element.50), channel_id=1, source_target_pairs={{0,10},{2,8},{4,14},{6,12},{8,2},{10,0},{12,6},{14,4},{16,26},{18,... | collective-permute-start | bytes 307208 | tf_op jit(solution)/shard_map/ppermute | solution.py:462
  10.1 8.4 %collective-permute-start.1 = (bf16[400,128]{1,0:T(8,128)(2,1)}, bf16[400,128]{1,0:T(8,128)(2,1)S(1)}, u32[]{:S(2)}, u32[]{:S(2)}) collective-permute-start(bf16[400,128]{1,0:T(8,128)(2,1)} %get-tuple-element.51), channel_id=1, source_target_pairs={{0,12},{2,14},{4,8},{6,10},{8,4},{10,6},{12,0},{14,2},{16,28},{18,... | collective-permute-start | bytes 307208 | tf_op jit(solution)/shard_map/ppermute | solution.py:462
  12.6 7.1 %collective-permute-start.2 = (bf16[400,128]{1,0:T(8,128)(2,1)}, bf16[400,128]{1,0:T(8,128)(2,1)S(1)}, u32[]{:S(2)}, u32[]{:S(2)}) collective-permute-start(bf16[400,128]{1,0:T(8,128)(2,1)} %get-tuple-element.52), channel_id=1, source_target_pairs={{0,14},{2,12},{4,10},{6,8},{8,6},{10,4},{12,2},{14,0},{16,30},{18,... | collective-permute-start | bytes 307208 | tf_op jit(solution)/shard_map/ppermute | solution.py:462
  13.9 0.9 %copy-start.5 = (bf16[400,128]{1,0:T(8,128)(2,1)S(1)}, bf16[400,128]{1,0:T(8,128)(2,1)}, u32[]{:S(2)}) copy-start(bf16[400,128]{1,0:T(8,128)(2,1)} %get-tuple-element.53.refs_0_) | copy-start | bytes 307204
  18.3 4.5 %copy-start.2 = (bf16[128,2048]{1,0:T(8,128)(2,1)S(1)}, bf16[128,2048]{1,0:T(8,128)(2,1)}, u32[]{:S(2)}) copy-start(bf16[128,2048]{1,0:T(8,128)(2,1)} %refs_2_.3) | copy-start | bytes 1572868
  18.3 4.5 %copy-start.3 = (bf16[128,1024]{1,0:T(8,128)(2,1)S(1)}, bf16[128,1024]{1,0:T(8,128)(2,1)}, u32[]{:S(2)}) copy-start(bf16[128,1024]{1,0:T(8,128)(2,1)} %refs_1_.3) | copy-start | bytes 786436
  18.3 4.5 %copy-start.4 = (bf16[128,1024]{1,0:T(8,128)(2,1)S(1)}, bf16[128,1024]{1,0:T(8,128)(2,1)}, u32[]{:S(2)}) copy-start(bf16[128,1024]{1,0:T(8,128)(2,1)} %refs_0_.3) | copy-start | bytes 786436
  18.3 4.5 %copy-start.6 = (bf16[128,128]{1,0:T(8,128)(2,1)S(1)}, bf16[128,128]{1,0:T(8,128)(2,1)}, u32[]{:S(2)}) copy-start(bf16[128,128]{1,0:T(8,128)(2,1)} %get-tuple-element.82.refs_3_) | copy-start | bytes 98308
  26.0 16.8 %slice-start = ((s8[8388608]{0:T(1024)(128)(4,1)}), s8[4194304]{0:T(1024)(128)(4,1)S(1)}, s32[]{:S(2)}) async-start(s8[8388608]{0:T(1024)(128)(4,1)} %bitcast.3), calls=%async_computation.1 | async-start | bytes 8388608
  26.0 16.8 %slice-start.1 = ((s8[8388608]{0:T(1024)(128)(4,1)}), s8[4194304]{0:T(1024)(128)(4,1)S(1)}, s32[]{:S(2)}) async-start(s8[8388608]{0:T(1024)(128)(4,1)} %bitcast.3), calls=%async_computation.2 | async-start | bytes 8388608
  26.1 16.8 %copy-start = (bf16[128,2048]{1,0:T(8,128)(2,1)S(1)}, bf16[128,2048]{1,0:T(8,128)(2,1)}, u32[]{:S(2)}) copy-start(bf16[128,2048]{1,0:T(8,128)(2,1)} %gate_ref.1) | copy-start | bytes 1572868
  26.1 16.8 %copy-start.1 = (f32[128]{0:T(128)S(1)}, f32[128]{0:T(128)}, u32[]{:S(2)}) copy-start(f32[128]{0:T(128)} %param.14) | copy-start | bytes 1540
  26.1 5.2 %collective-permute-start.7 = (bf16[2,128,128]{2,1,0:T(8,128)(2,1)S(1)}, bf16[2,128,128]{2,1,0:T(8,128)(2,1)S(1)}, u32[]{:S(2)}, u32[]{:S(2)}) collective-permute-start(bf16[2,128,128]{2,1,0:T(8,128)(2,1)S(1)} %get-tuple-element.85), channel_id=1, source_target_pairs={{0,16},{2,18},{4,20},{6,22},{8,24},{10,26},{12,28},{14,30},{16,0},... | collective-permute-start | bytes 196616 | tf_op jit(solution)/shard_map/ppermute | solution.py:462
  44.2 1.6 %collective-permute-start.8 = (bf16[128,1024]{1,0:T(8,128)(2,1)S(1)}, bf16[128,1024]{1,0:T(8,128)(2,1)S(1)}, u32[]{:S(2)}, u32[]{:S(2)}) collective-permute-start(bf16[128,1024]{1,0:T(8,128)(2,1)S(1)} %get-tuple-element.94), channel_id=1, source_target_pairs={{0,1},{1,0},{2,3},{3,2},{4,5},{5,4},{6,7},{7,6},{8,9},{9,8},{10,11... | collective-permute-start | bytes 786440 | tf_op jit(solution)/shard_map/ppermute | solution.py:567

commit v4 on v3

--- a/solution.py
+++ b/solution.py
@@ -14,7 +14,7 @@
 REP = HV // HK
 SMALL_BITS = 4
 SMALL_ROWS = 1 << SMALL_BITS
-BASE_BITS = 3
+BASE_BITS = 4
 BASE = 1 << BASE_BITS
 PIECE_ROWS = 8
 EPSILON = 1e-06
@@ -212,8 +212,9 @@
     return solved(lowers, rights, tokens), works
 
 
-def inside_heads(query_ref, key_ref, value_ref, rows_ref, inside_ref, window_ref, first, blocks):
+def inside_kernel(query_ref, key_ref, value_ref, rows_ref, inside_ref, window_ref):
     tokens = query_ref.shape[0]
+    blocks = inside_ref.shape[0] // REP
 
     def columns(ref, start, size):
         return ref[:, start * size : (start + 1) * size]
@@ -224,13 +225,13 @@
                 columns(key_ref, j, DK),
                 [columns(value_ref, j * REP + r, DV) for r in range(REP)],
             )
-            for j in range(first, first + blocks)
+            for j in range(blocks)
         ],
-        rows_ref[first * SMALL_ROWS : (first + blocks) * SMALL_ROWS, :][:, :tokens],
+        rows_ref[:, :tokens],
         tokens,
     )
     for b in range(blocks):
-        queries = columns(query_ref, first + b, DK)
+        queries = columns(query_ref, b, DK)
         products = nt(queries, works[b * REP][0])
         queries = queries.astype(F32)
         query_col = lax.rsqrt(
@@ -244,31 +245,8 @@
             _, cum_col, _, _, factors = works[at]
             scores = (products * factors).astype(BF16)
             both = nn(scores, sides[at].astype(BF16))
-            to = first * REP + at
-            inside_ref[to] = both[:, :DV].astype(BF16)
-            window_ref[to] = (jnp.exp(cum_col) * queries - both[:, DV:]).astype(BF16)
-
-
-def early_inside_kernel(*refs, group):
-    @pl.when(lax.axis_index("ctx") < group)
-    def _():
-        inside_heads(*refs, 0, group // 2)
-
-
-def inside_kernel(early_inside, early_window, *refs, group):
-    known = (group // 2) * REP
-    first_group = lax.axis_index("ctx") < group
-
-    @pl.when(first_group)
-    def _():
-        inside_ref, window_ref = refs[-2:]
-        inside_ref[0:known] = early_inside[...]
-        window_ref[0:known] = early_window[...]
-        inside_heads(*refs, group // 2, group - group // 2)
-
-    @pl.when(jnp.logical_not(first_group))
-    def _():
-        inside_heads(*refs, 0, group)
+            inside_ref[at] = both[:, :DV].astype(BF16)
+            window_ref[at] = (jnp.exp(cum_col) * queries - both[:, DV:]).astype(BF16)
 
 
 def in_order(own_half, own, other):
@@ -519,20 +497,6 @@
     *other, end = half_states(later, own[2:], "other_half")
     own = own[:4]
 
-    def inside_part(body, name, count, micros, operands):
-        return kernel(
-            functools.partial(body, group=group),
-            (shape((count, tokens, DV), BF16), shape((count, tokens, DK), BF16)),
-            name,
-            16,
-            micros,
-        )(*operands)
-
-    rows, end = lax.optimization_barrier((rows, end))
-    activations = (query_proj, key_proj, value_proj, rows)
-    early = inside_part(early_inside_kernel, "early_inside", half * REP, 3, activations)
-    end, *early = lax.optimization_barrier((end, *early))
-
     if n_groups == 2:
         carried = swapped(end, group)
     elif n_groups > 2:
@@ -548,7 +512,17 @@
     else:
         carried = jnp.zeros((REP, DK, DV), BF16)
 
-    inside, window = inside_part(inside_kernel, "inside", heads, 5, (*early, *activations))
+    rows, end = lax.optimization_barrier((rows, end))
+    inside, window = kernel(
+        inside_kernel,
+        (
+            shape((heads, tokens, DV), BF16),
+            shape((heads, tokens, DK), BF16),
+        ),
+        "inside",
+        16,
+        5,
+    )(query_proj, key_proj, value_proj, rows)
     carried, inside, window = lax.optimization_barrier((carried, inside, window))
     states = kernel(
         carry_kernel, shape((group, REP * DK, DV), BF16), "carry", 8, 0.6

time: 46.9 us -> 45.8 us (0.977)
  starting transfers between devices: 12 us -> 14.5 us
  Pallas kernels: 17.8 us -> 16 us
  waiting for transfers between devices: 3.9 us -> 2.31 us
    ppermute x8, starting transfers between devices: 11.9 us -> 14.5 us  [swapped(): return lax.ppermute(array, 'ctx', [(i, i ^ distance) for i in range(n_ctx)])]
    ppermute x8, waiting for transfers between devices: 3.15 us -> 1.56 us  [swapped(): return lax.ppermute(array, 'ctx', [(i, i ^ distance) for i in range(n_ctx)])]
    pallas_call x2 -> x1, Pallas kernels: 6.56 us -> 5.13 us  [local(): kernel(inside_kernel, (shape((heads, tokens, DV), BF16), shape((heads, to...]
  transfers between devices with their start and end apart: 9 -> 9, of which waited for: 4 -> 3; matrix products, arithmetic and copies ran while one was open for 0% -> 0% of each run, Pallas kernels for 16% -> 20%
where the time goes in v4:
time: 45.8 us; the launch traced here: 45.5 us
  Pallas kernels  16 us (35%)
  starting transfers between devices  14.5 us (32%)
  blocking collectives  10.7 us (23%)
  waiting for transfers between devices  2.31 us (5%)
  local copies, waits for them, and re-layouts  0.94 us (2%)
  other arithmetic  0.77 us (2%)
    ppermute x8, starting transfers between devices, swapped(): return lax.ppermute(array, 'ctx', [(i, i ^ distance) for i in range(n_ctx)])  14.5 us
    all_to_all x1, blocking collectives, local(): lax.all_to_all(states, 'ctx', 0, 0, axis_index_groups=groups, tiled=True)  10.7 us
    pallas_call x2, Pallas kernels, half_states(): kernel(functools.partial(half_kernel, blocks=half, extra=extra, group=gro...  6.25 us
    pallas_call x1, Pallas kernels, local(): kernel(inside_kernel, (shape((heads, tokens, DV), BF16), shape((heads, to...  5.13 us
    pallas_call x1, Pallas kernels, local(): kernel(pack_kernel, (shape((packed_rows, DK), BF16),) * group + (shape((g...  2.09 us
    ppermute x8, waiting for transfers between devices, swapped(): return lax.ppermute(array, 'ctx', [(i, i ^ distance) for i in range(n_ctx)])  1.56 us
    pallas_call x1, Pallas kernels, local(): kernel(functools.partial(mixed_kernel, shifts=n_head), (shape((tokens, he...  1.35 us
    unnamed x18, local copies, waits for them, and re-layouts  0.94 us
  transfers between devices with their start and end apart: 9, of which 3 were waited for; matrix products, arithmetic and copies ran while one was open for 0% of the time, Pallas kernels for 20%

profile of v4, /device:TPU:0, one launch (start us, length us, event | category | flops | bytes accessed | tf_op | source)
XLA Modules:
  0.0 45.5 jit_solution(6159628819466993099)
XLA Ops:
  0.0 2.1 %pack.1 = (bf16[400,128]{1,0:T(8,128)(2,1)}, bf16[400,128]{1,0:T(8,128)(2,1)}, bf16[400,128]{1,0:T(8,128)(2,1)}, bf16[400,128]{1,0:T(8,128)(2,1)}, bf16[400,128]...) custom-call(bf16[128,1024]{1,0:T(8,128)(2,1)} %key_ref.1, ...), custom_call_target="tpu_custom_call" | custom-call | flops 2000000000 | bytes 1048576 | tf_op jit(solution)/shard_map/pack/pallas_call | solution.py:444
  2.1 3.0 %collective-permute-start.3 = (bf16[400,128]{1,0:T(8,128)(2,1)}, bf16[400,128]{1,0:T(8,128)(2,1)S(1)}, u32[]{:S(2)}, u32[]{:S(2)}) collective-permute-start(bf16[400,128]{1,0:T(8,128)(2,1)} %get-tuple-element.48), channel_id=1, source_target_pairs={{0,2},{2,0},{4,6},{6,4},{8,10},{10,8},{12,14},{14,12},{16,18},{18,... | collective-permute-start | bytes 307208 | tf_op jit(solution)/shard_map/ppermute | solution.py:440
  5.1 1.5 %collective-permute-start.4 = (bf16[400,128]{1,0:T(8,128)(2,1)}, bf16[400,128]{1,0:T(8,128)(2,1)S(1)}, u32[]{:S(2)}, u32[]{:S(2)}) collective-permute-start(bf16[400,128]{1,0:T(8,128)(2,1)} %get-tuple-element.49), channel_id=1, source_target_pairs={{0,4},{2,6},{4,0},{6,2},{8,12},{10,14},{12,8},{14,10},{16,20},{18,... | collective-permute-start | bytes 307208 | tf_op jit(solution)/shard_map/ppermute | solution.py:440
  6.6 0.0 collective-permute-start.5
  6.6 2.0 %collective-permute-start.6 = (bf16[400,128]{1,0:T(8,128)(2,1)}, bf16[400,128]{1,0:T(8,128)(2,1)S(1)}, u32[]{:S(2)}, u32[]{:S(2)}) collective-permute-start(bf16[400,128]{1,0:T(8,128)(2,1)} %get-tuple-element.51), channel_id=1, source_target_pairs={{0,8},{2,10},{4,12},{6,14},{8,0},{10,2},{12,4},{14,6},{16,24},{18,... | collective-permute-start | bytes 307208 | tf_op jit(solution)/shard_map/ppermute | solution.py:440
  8.7 1.4 %collective-permute-start = (bf16[400,128]{1,0:T(8,128)(2,1)}, bf16[400,128]{1,0:T(8,128)(2,1)S(1)}, u32[]{:S(2)}, u32[]{:S(2)}) collective-permute-start(bf16[400,128]{1,0:T(8,128)(2,1)} %get-tuple-element.44), channel_id=1, source_target_pairs={{0,10},{2,8},{4,14},{6,12},{8,2},{10,0},{12,6},{14,4},{16,26},{18,... | collective-permute-start | bytes 307208 | tf_op jit(solution)/shard_map/ppermute | solution.py:440
  10.1 0.0 collective-permute-done.3.refs_1_
  10.1 2.5 %collective-permute-start.1 = (bf16[400,128]{1,0:T(8,128)(2,1)}, bf16[400,128]{1,0:T(8,128)(2,1)S(1)}, u32[]{:S(2)}, u32[]{:S(2)}) collective-permute-start(bf16[400,128]{1,0:T(8,128)(2,1)} %get-tuple-element.45), channel_id=1, source_target_pairs={{0,12},{2,14},{4,8},{6,10},{8,4},{10,6},{12,0},{14,2},{16,28},{18,... | collective-permute-start | bytes 307208 | tf_op jit(solution)/shard_map/ppermute | solution.py:440
  12.6 0.0 collective-permute-done.4.refs_2_
  12.6 1.3 %collective-permute-start.2 = (bf16[400,128]{1,0:T(8,128)(2,1)}, bf16[400,128]{1,0:T(8,128)(2,1)S(1)}, u32[]{:S(2)}, u32[]{:S(2)}) collective-permute-start(bf16[400,128]{1,0:T(8,128)(2,1)} %get-tuple-element.46), channel_id=1, source_target_pairs={{0,14},{2,12},{4,10},{6,8},{8,6},{10,4},{12,2},{14,0},{16,30},{18,... | collective-permute-start | bytes 307208 | tf_op jit(solution)/shard_map/ppermute | solution.py:440
  13.9 0.0 collective-permute-done.5.refs_3_
  13.9 0.9 %copy-done.5 = bf16[400,128]{1,0:T(8,128)(2,1)S(1)} copy-done((bf16[400,128]{1,0:T(8,128)(2,1)S(1)}, bf16[400,128]{1,0:T(8,128)(2,1)}, u32[]{:S(2)}) %copy-start.5) | copy-done | bytes 102424
  14.8 3.3 %own_half.1 = (f32[8,128,128]{2,1,0:T(8,128)S(1)}, bf16[8,128,128]{2,1,0:T(8,128)(2,1)S(1)}, f32[2,128,128]{2,1,0:T(8,128)S(1)}, f32[2,128,128]{2,1,0:T(8,128)S(...) custom-call(bf16[400,128]{1,0:T(8,128)(2,1)S(1)} %copy-done.5, ...), custom_call_target="tpu_custom_call" | custom-call | flops 3500000000 | bytes 1048576 | tf_op jit(solution)/shard_map/own_half/pallas_call | solution.py:471
  18.1 0.0 copy-start.2
  18.1 0.0 copy-start.3
  18.2 0.0 copy-start.4
  18.2 0.0 collective-permute-done.refs_0_
  18.2 0.2 collective-permute-done.1.refs_1_
  18.4 1.3 %collective-permute-done.2.refs_2_ = bf16[400,128]{1,0:T(8,128)(2,1)S(1)} collective-permute-done((bf16[400,128]{1,0:T(8,128)(2,1)}, bf16[400,128]{1,0:T(8,128)(2,1)S(1)}, u32[]{:S(2)}, u32[]{:S(2)}) %collective-permute-start.2) | collective-permute-done | bytes 102432 | tf_op jit(solution)/shard_map/ppermute | solution.py:440
  19.7 2.9 %other_half.1 = (f32[8,128,128]{2,1,0:T(8,128)S(1)}, bf16[8,128,128]{2,1,0:T(8,128)(2,1)S(1)}, f32[2,128,128]{2,1,0:T(8,128)S(1)}, f32[2,128,128]{2,1,0:T(8,128)S(1)}, bf16[2,128,128]{2,1,0:T(8,128)(2,1)S(1)}) custom-call(bf16[400,128]{1,0:T(8,128)(2,1)S(1)} %collective-permute-done.refs_0_, bf16[400,128]{1,0:T(8,128)(2,1)S(1)} %collective-permute-done.1.refs_1_, ...), custom_call_target="tpu_custom_call" | custom-call | flops 3500000000 | bytes 1048576 | tf_op jit(solution)/shard_map/other_half/pallas_call | solution.py:471
  22.7 2.7 %collective-permute-start.7 = (bf16[2,128,128]{2,1,0:T(8,128)(2,1)S(1)}, bf16[2,128,128]{2,1,0:T(8,128)(2,1)S(1)}, u32[]{:S(2)}, u32[]{:S(2)}) collective-permute-start(bf16[2,128,128]{2,1,0:T(8,128)(2,1)S(1)} %get-tuple-element.73), channel_id=1, source_target_pairs={{0,16},{2,18},{4,20},{6,22},{8,24},{10,26},{12,28},{14,30},{16,0},... | collective-permute-start | bytes 196616 | tf_op jit(solution)/shard_map/ppermute | solution.py:440
  25.4 0.0 slice-start.1
  25.4 0.0 copy-start
  25.4 0.0 copy-start.1
  25.4 5.1 %inside.1 = (bf16[16,128,128]{2,1,0:T(8,128)(2,1)S(1)}, bf16[16,128,128]{2,1,0:T(8,128)(2,1)S(1)}) custom-call(bf16[128,1024]{1,0:T(8,128)(2,1)S(1)} %copy-done.4, bf16[128,1024]{1,0:T(8,128)(2,1)S(1)} %copy-done.3, bf16[128,2048]{1,0:T(8,128)(2,1)S(1)} %copy-done.2, bf16[128,128]{1,0:T(8,128)(2,1)S(1)} %copy-done.6), custom_call_target="tpu_custom_call" | custom-call | flops 5000000000 | bytes 1048576 | tf_op jit(solution)/shard_map/inside/pallas_call | solution.py:516
  30.5 0.5 %carry.1 = bf16[8,256,128]{2,1,0:T(8,128)(2,1)S(1)} custom-call(f32[8,128,128]{2,1,0:T(8,128)S(1)} %get-tuple-element.59.own_before, bf16[8,128,128]{2,1,0:T(8,128)(2,1)S(1)} %get-tuple-element.60.own_maps, f32[2,128,128]{2,1,0:T(8,128)S(1)} %get-tuple-element.61.refs_3_.own_end, f32[2,128,128]{2,1,0:T(8,128)S(1)} %get-tuple-element.62.refs_4_.own_map, ...), custom_call_target="tpu_custom_call" | custom-call | flops 600000000 | bytes 1048576 | tf_op jit(solution)/shard_map/carry/pallas_call | solution.py:527
  31.0 10.7 %all_to_all.5.state_ref = bf16[8,256,128]{2,1,0:T(8,128)(2,1)S(1)} all-to-all(bf16[8,256,128]{2,1,0:T(8,128)(2,1)S(1)} %carry.1), channel_id=1, replica_groups={{0,2,4,6,8,10,12,14},{16,18,20,22,24,26,28,30},{1,3,5,7,9,11,13,15},{17..., dimensions={0} | all-to-all | bytes 1048576 | tf_op jit(solution)/shard_map/all_to_all | solution.py:531
  41.8 1.4 %mixed.1 = (bf16[128,2048]{1,0:T(8,128)(2,1)S(1)}, bf16[128,1024]{1,0:T(8,128)(2,1)S(1)}) custom-call(bf16[8,256,128]{2,1,0:T(8,128)(2,1)S(1)} %all_to_all.5.state_ref, bf16[16,128,128]{2,1,0:T(8,128)(2,1)S(1)} %get-tuple-element.79.inside_ref, bf16[16,128,128]{2,1,0:T(8,128)(2,1)S(1)} %get-tuple-element.80.window_ref, bf16[128,2048]{1,0:T(8,128)(2,1)S(1)} %copy-done, ...), custom_call_target="tpu_custom_call" | custom-call | flops 2000000000 | bytes 1048576 | tf_op jit(solution)/shard_map/mixed/pallas_call | solution.py:533
  43.1 0.1 collective-permute-start.8
  43.2 0.8 %own_columns.1 = bf16[128,1024]{1,0:T(8,128)(2,1)S(1)} custom-call(bf16[128,2048]{1,0:T(8,128)(2,1)S(1)} %get-tuple-element.81.mixed_ref, bf16[2048,2048]{1,0:T(8,128)(2,1)S(1)} %bitcast.4), custom_call_target="tpu_custom_call" | custom-call | flops 1000000000 | bytes 1048576 | tf_op jit(solution)/shard_map/own_columns/pallas_call | solution.py:544
  44.0 0.7 %collective-permute-done.8 = bf16[128,1024]{1,0:T(8,128)(2,1)S(1)} collective-permute-done((bf16[128,1024]{1,0:T(8,128)(2,1)S(1)}, bf16[128,1024]{1,0:T(8,128)(2,1)S(1)}, u32[]{:S(2)}, u32[]{:S(2)}) %collective-permute-start.8) | collective-permute-done | bytes 262176 | tf_op jit(solution)/shard_map/ppermute | solution.py:541
  44.7 0.8 %add_convert_fusion = bf16[128,1024]{1,0:T(8,128)(2,1)} fusion(bf16[128,1024]{1,0:T(8,128)(2,1)S(1)} %collective-permute-done.8, bf16[128,1024]{1,0:T(8,128)(2,1)S(1)} %own_columns.1), kind=kLoop, calls=%fused_computation | loop fusion | flops 524288 | bytes 786432 | tf_op jit(solution)/shard_map/convert_element_type | solution.py:549
  (14 shorter events, 0.0 us)
Async XLA Ops:
  2.1 8.0 %collective-permute-start.3 = (bf16[400,128]{1,0:T(8,128)(2,1)}, bf16[400,128]{1,0:T(8,128)(2,1)S(1)}, u32[]{:S(2)}, u32[]{:S(2)}) collective-permute-start(bf16[400,128]{1,0:T(8,128)(2,1)} %get-tuple-element.48), channel_id=1, source_target_pairs={{0,2},{2,0},{4,6},{6,4},{8,10},{10,8},{12,14},{14,12},{16,18},{18,... | collective-permute-start | bytes 307208 | tf_op jit(solution)/shard_map/ppermute | solution.py:440
  5.1 7.5 %collective-permute-start.4 = (bf16[400,128]{1,0:T(8,128)(2,1)}, bf16[400,128]{1,0:T(8,128)(2,1)S(1)}, u32[]{:S(2)}, u32[]{:S(2)}) collective-permute-start(bf16[400,128]{1,0:T(8,128)(2,1)} %get-tuple-element.49), channel_id=1, source_target_pairs={{0,4},{2,6},{4,0},{6,2},{8,12},{10,14},{12,8},{14,10},{16,20},{18,... | collective-permute-start | bytes 307208 | tf_op jit(solution)/shard_map/ppermute | solution.py:440
  6.6 7.3 %collective-permute-start.5 = (bf16[400,128]{1,0:T(8,128)(2,1)}, bf16[400,128]{1,0:T(8,128)(2,1)S(1)}, u32[]{:S(2)}, u32[]{:S(2)}) collective-permute-start(bf16[400,128]{1,0:T(8,128)(2,1)} %get-tuple-element.50), channel_id=1, source_target_pairs={{0,6},{2,4},{4,2},{6,0},{8,14},{10,12},{12,10},{14,8},{16,22},{18,... | collective-permute-start | bytes 307208 | tf_op jit(solution)/shard_map/ppermute | solution.py:440
  6.6 7.3 %collective-permute-start.6 = (bf16[400,128]{1,0:T(8,128)(2,1)}, bf16[400,128]{1,0:T(8,128)(2,1)S(1)}, u32[]{:S(2)}, u32[]{:S(2)}) collective-permute-start(bf16[400,128]{1,0:T(8,128)(2,1)} %get-tuple-element.51), channel_id=1, source_target_pairs={{0,8},{2,10},{4,12},{6,14},{8,0},{10,2},{12,4},{14,6},{16,24},{18,... | collective-permute-start | bytes 307208 | tf_op jit(solution)/shard_map/ppermute | solution.py:440
  8.7 9.5 %collective-permute-start = (bf16[400,128]{1,0:T(8,128)(2,1)}, bf16[400,128]{1,0:T(8,128)(2,1)S(1)}, u32[]{:S(2)}, u32[]{:S(2)}) collective-permute-start(bf16[400,128]{1,0:T(8,128)(2,1)} %get-tuple-element.44), channel_id=1, source_target_pairs={{0,10},{2,8},{4,14},{6,12},{8,2},{10,0},{12,6},{14,4},{16,26},{18,... | collective-permute-start | bytes 307208 | tf_op jit(solution)/shard_map/ppermute | solution.py:440
  10.1 8.4 %collective-permute-start.1 = (bf16[400,128]{1,0:T(8,128)(2,1)}, bf16[400,128]{1,0:T(8,128)(2,1)S(1)}, u32[]{:S(2)}, u32[]{:S(2)}) collective-permute-start(bf16[400,128]{1,0:T(8,128)(2,1)} %get-tuple-element.45), channel_id=1, source_target_pairs={{0,12},{2,14},{4,8},{6,10},{8,4},{10,6},{12,0},{14,2},{16,28},{18,... | collective-permute-start | bytes 307208 | tf_op jit(solution)/shard_map/ppermute | solution.py:440
  12.6 7.1 %collective-permute-start.2 = (bf16[400,128]{1,0:T(8,128)(2,1)}, bf16[400,128]{1,0:T(8,128)(2,1)S(1)}, u32[]{:S(2)}, u32[]{:S(2)}) collective-permute-start(bf16[400,128]{1,0:T(8,128)(2,1)} %get-tuple-element.46), channel_id=1, source_target_pairs={{0,14},{2,12},{4,10},{6,8},{8,6},{10,4},{12,2},{14,0},{16,30},{18,... | collective-permute-start | bytes 307208 | tf_op jit(solution)/shard_map/ppermute | solution.py:440
  13.9 0.9 %copy-start.5 = (bf16[400,128]{1,0:T(8,128)(2,1)S(1)}, bf16[400,128]{1,0:T(8,128)(2,1)}, u32[]{:S(2)}) copy-start(bf16[400,128]{1,0:T(8,128)(2,1)} %get-tuple-element.47.refs_0_) | copy-start | bytes 307204
  18.1 7.2 %copy-start.2 = (bf16[128,2048]{1,0:T(8,128)(2,1)S(1)}, bf16[128,2048]{1,0:T(8,128)(2,1)}, u32[]{:S(2)}) copy-start(bf16[128,2048]{1,0:T(8,128)(2,1)} %value_ref.1) | copy-start | bytes 1572868
  18.1 7.2 %copy-start.3 = (bf16[128,1024]{1,0:T(8,128)(2,1)S(1)}, bf16[128,1024]{1,0:T(8,128)(2,1)}, u32[]{:S(2)}) copy-start(bf16[128,1024]{1,0:T(8,128)(2,1)} %key_ref.1) | copy-start | bytes 786436
  18.2 7.2 %copy-start.4 = (bf16[128,1024]{1,0:T(8,128)(2,1)S(1)}, bf16[128,1024]{1,0:T(8,128)(2,1)}, u32[]{:S(2)}) copy-start(bf16[128,1024]{1,0:T(8,128)(2,1)} %query_ref.1) | copy-start | bytes 786436
  18.2 7.2 %copy-start.6 = (bf16[128,128]{1,0:T(8,128)(2,1)S(1)}, bf16[128,128]{1,0:T(8,128)(2,1)}, u32[]{:S(2)}) copy-start(bf16[128,128]{1,0:T(8,128)(2,1)} %get-tuple-element.75.rows_ref) | copy-start | bytes 98308
  19.7 22.0 %slice-start = ((s8[8388608]{0:T(1024)(128)(4,1)}), s8[4194304]{0:T(1024)(128)(4,1)S(1)}, s32[]{:S(2)}) async-start(s8[8388608]{0:T(1024)(128)(4,1)} %bitcast.3), calls=%async_computation.1 | async-start | bytes 8388608
  22.7 7.8 %collective-permute-start.7 = (bf16[2,128,128]{2,1,0:T(8,128)(2,1)S(1)}, bf16[2,128,128]{2,1,0:T(8,128)(2,1)S(1)}, u32[]{:S(2)}, u32[]{:S(2)}) collective-permute-start(bf16[2,128,128]{2,1,0:T(8,128)(2,1)S(1)} %get-tuple-element.73), channel_id=1, source_target_pairs={{0,16},{2,18},{4,20},{6,22},{8,24},{10,26},{12,28},{14,30},{16,0},... | collective-permute-start | bytes 196616 | tf_op jit(solution)/shard_map/ppermute | solution.py:440
  25.4 16.4 %slice-start.1 = ((s8[8388608]{0:T(1024)(128)(4,1)}), s8[4194304]{0:T(1024)(128)(4,1)S(1)}, s32[]{:S(2)}) async-start(s8[8388608]{0:T(1024)(128)(4,1)} %bitcast.3), calls=%async_computation.2 | async-start | bytes 8388608
  25.4 16.4 %copy-start = (bf16[128,2048]{1,0:T(8,128)(2,1)S(1)}, bf16[128,2048]{1,0:T(8,128)(2,1)}, u32[]{:S(2)}) copy-start(bf16[128,2048]{1,0:T(8,128)(2,1)} %gate_ref.1) | copy-start | bytes 1572868
  25.4 16.4 %copy-start.1 = (f32[128]{0:T(128)S(1)}, f32[128]{0:T(128)}, u32[]{:S(2)}) copy-start(f32[128]{0:T(128)} %param.14) | copy-start | bytes 1540
  43.1 1.6 %collective-permute-start.8 = (bf16[128,1024]{1,0:T(8,128)(2,1)S(1)}, bf16[128,1024]{1,0:T(8,128)(2,1)S(1)}, u32[]{:S(2)}, u32[]{:S(2)}) collective-permute-start(bf16[128,1024]{1,0:T(8,128)(2,1)S(1)} %get-tuple-element.82), channel_id=1, source_target_pairs={{0,1},{1,0},{2,3},{3,2},{4,5},{5,4},{6,7},{7,6},{8,9},{9,8},{10,11... | collective-permute-start | bytes 786440 | tf_op jit(solution)/shard_map/ppermute | solution.py:541

commit v5 on v4

--- a/solution.py
+++ b/solution.py
@@ -14,8 +14,6 @@
 REP = HV // HK
 SMALL_BITS = 4
 SMALL_ROWS = 1 << SMALL_BITS
-BASE_BITS = 4
-BASE = 1 << BASE_BITS
 PIECE_ROWS = 8
 EPSILON = 1e-06
 BF16 = jnp.bfloat16
@@ -44,27 +42,27 @@
     return row, col, (col <= row).astype(BF16), (row <= col).astype(BF16), (row == col).astype(BF16)
 
 
-def solved(lowers, rights, size):
-    count = len(lowers)
+def solved(lowers, rights, size, base_bits):
+    count, base = len(lowers), 1 << base_bits
     row, col = iotas((size, size))
-    place, lane = iotas((BASE, size))
+    place, lane = iotas((base, size))
     packed = []
     for low in lowers:
-        held = low[0:BASE]
-        for b in range(1, size // BASE):
-            held = jnp.where(lane >> BASE_BITS == b, low[b * BASE : (b + 1) * BASE], held)
+        held = low[0:base]
+        for b in range(1, size // base):
+            held = jnp.where(lane >> base_bits == b, low[b * base : (b + 1) * base], held)
         packed.append(held)
     packed = jnp.concatenate(packed, axis=0).astype(BF16)
-    found = [jnp.where(place == (lane & (BASE - 1)), 1.0, 0.0)] * count
-    first_col = col & ~(BASE - 1)
-    for k in range(BASE - 1):
+    found = [jnp.where(place == (lane & (base - 1)), 1.0, 0.0)] * count
+    first_col = col & ~(base - 1)
+    for k in range(base - 1):
         spread = jnp.where(row == first_col + k, 1.0, 0.0).astype(BF16)
         column = nn(packed, spread)
         found = [
-            x - column[h * BASE : (h + 1) * BASE] * x[k : k + 1] for h, x in enumerate(found)
+            x - column[h * base : (h + 1) * base] * x[k : k + 1] for h, x in enumerate(found)
         ]
     rounded = [low.astype(BF16) for low in lowers]
-    step, apart = BASE, row ^ col
+    step, apart = base, row ^ col
     while True:
         pair = 2 * step
         below = jnp.where((apart >= step) & (apart < pair) & (col < row), 1.0, 0.0).astype(BF16)
@@ -106,17 +104,13 @@
     return lax.rem(lax.axis_index("ctx"), group)
 
 
-def pack_kernel(key_hbm, value_hbm, strength_hbm, decay_hbm, *refs):
-    group = len(refs) - 6
-    out_refs, (rows_ref, held, scalars, small, in_sems, out_sems) = refs[:group], refs[group:]
+def pack_kernel(key_hbm, value_hbm, scalars_ref, *refs):
+    group = len(refs) - 2
+    out_refs, (rows_ref, in_sems) = refs[:group], refs[group:]
     tokens = key_hbm.shape[0]
-    heads = strength_hbm.shape[0]
+    heads = scalars_ref.shape[1]
     place = place_in_group(group)
     base = (1 + REP) * tokens
-    scalar_copies = [
-        pltpu.make_async_copy(ref, scalars.at[kind], in_sems.at[group, kind])
-        for kind, ref in enumerate((strength_hbm, decay_hbm))
-    ]
     arrivals = []
     for s in range(group):
         j = place ^ s
@@ -126,12 +120,12 @@
         arrivals.append(
             [
                 pltpu.make_async_copy(
-                    source, held.at[s, pl.ds(n * tokens, tokens), :], in_sems.at[s, n]
+                    source, out_refs[s].at[pl.ds(n * tokens, tokens), :], in_sems.at[s, n]
                 )
                 for n, source in enumerate(sources)
             ]
         )
-    for copy in scalar_copies + sum(arrivals, []):
+    for copy in sum(arrivals, []):
         copy.start()
     row, col = iotas((SMALL_ROWS * group, 4 * heads))
     slot, target = row & (SMALL_ROWS - 1), row >> SMALL_BITS
@@ -146,27 +140,21 @@
         return pick.astype(BF16)
 
     picks = picked(target ^ place), picked(target)
-    for copy in scalar_copies:
-        copy.wait()
-    pieces = jnp.concatenate(two_pieces(scalars[0]) + two_pieces(scalars[1]), axis=0)
+    pieces = jnp.concatenate(
+        two_pieces(scalars_ref[0]) + two_pieces(scalars_ref[1]), axis=0
+    )
     sent, natural = [nn(pick, pieces).astype(BF16) for pick in picks]
     if tokens < DK:
         fill = jnp.zeros((sent.shape[0], DK - tokens), BF16)
         sent, natural = [jnp.concatenate([x, fill], axis=1) for x in (sent, natural)]
-    small[...] = natural
-    departures = [pltpu.make_async_copy(small, rows_ref, out_sems.at[group])]
-    departures[0].start()
+    rows_ref[...] = natural
     for s, out_ref in enumerate(out_refs):
-        held[s, base : base + SMALL_ROWS, :] = sent[s * SMALL_ROWS : (s + 1) * SMALL_ROWS, :]
+        out_ref[base : base + SMALL_ROWS, :] = sent[s * SMALL_ROWS : (s + 1) * SMALL_ROWS, :]
         for copy in arrivals[s]:
             copy.wait()
-        departures.append(pltpu.make_async_copy(held.at[s], out_ref, out_sems.at[s]))
-        departures[-1].start()
-    for copy in departures:
-        copy.wait()
-
-
-def solved_blocks(blocks, small, tokens):
+
+
+def solved_blocks(blocks, small, tokens, base_bits):
     row, col, lower_ones, upper_ones, eye = triangles(tokens)
     small = small.astype(F32)
     pieces = [
@@ -209,7 +197,7 @@
                 )
             )
             works.append((keys, cum_col, key_col, key_row, factors))
-    return solved(lowers, rights, tokens), works
+    return solved(lowers, rights, tokens, base_bits), works
 
 
 def inside_kernel(query_ref, key_ref, value_ref, rows_ref, inside_ref, window_ref):
@@ -229,6 +217,7 @@
         ],
         rows_ref[:, :tokens],
         tokens,
+        3,
     )
     for b in range(blocks):
         queries = columns(query_ref, b, DK)
@@ -280,6 +269,7 @@
         ],
         jnp.concatenate([t[base : base + SMALL_ROWS, :][:, :tokens] for t in taken], axis=0),
         tokens,
+        4,
     )
     if known:
         for held, ref in zip((offsets, removals, decays), known):
@@ -445,18 +435,11 @@
         pack_kernel,
         (shape((packed_rows, DK), BF16),) * group + (shape((group * SMALL_ROWS, DK), BF16),),
         "pack",
-        None,
+        53,
         2,
-        scratch=[
-            pltpu.VMEM((group, packed_rows, DK), BF16),
-            pltpu.VMEM((2, heads, tokens), F32),
-            pltpu.VMEM((group * SMALL_ROWS, DK), BF16),
-            pltpu.SemaphoreType.DMA((group + 1, 1 + REP)),
-            pltpu.SemaphoreType.DMA((group + 1,)),
-        ],
-        specs=[any_space] * 4,
-        out_specs=(any_space,) * (group + 1),
-    )(key_proj, value_proj, write_strength.T, log_decay.T)
+        scratch=[pltpu.SemaphoreType.DMA((group, 1 + REP))],
+        specs=[any_space, any_space, vmem],
+    )(key_proj, value_proj, jnp.stack([write_strength.T, log_decay.T]))
     taken = [packed[0]] + [swapped(packed[s], s) for s in range(1, group)]
 
     extra = 1 if half >= 4 else 0

time: 45.8 us -> 45.4 us (level)
  waiting for transfers between devices: 2.31 us -> 3.22 us
  Pallas kernels: 16 us -> 15.1 us
  local copies, waits for them, and re-layouts: 0.94 us -> 0.04 us
  other arithmetic: 0.77 us -> 1.49 us
    ppermute x8, waiting for transfers between devices: 1.56 us -> 2.47 us  [swapped(): return lax.ppermute(array, 'ctx', [(i, i ^ distance) for i in range(n_ctx)])]
    unnamed x18 -> x14, local copies, waits for them, and re-layouts: 0.94 us -> 0.04 us
    pallas_call x1, Pallas kernels: 2.09 us -> 1.33 us  [local(): kernel(pack_kernel, (shape((packed_rows, DK), BF16),) * group + (shape((g...]
    another operation x0 -> x1, other arithmetic: none -> 0.72 us  [local(): jnp.stack([write_strength.T, log_decay.T])]
where the time goes in v5:
time: 45.4 us; the launch traced here: 45.1 us
  Pallas kernels  15.1 us (33%)
  starting transfers between devices  14.3 us (31%)
  blocking collectives  10.7 us (24%)
  waiting for transfers between devices  3.22 us (7%)
  other arithmetic  1.49 us (3%)
    ppermute x8, starting transfers between devices, swapped(): return lax.ppermute(array, 'ctx', [(i, i ^ distance) for i in range(n_ctx)])  14.3 us
    all_to_all x1, blocking collectives, local(): lax.all_to_all(states, 'ctx', 0, 0, axis_index_groups=groups, tiled=True)  10.7 us
    pallas_call x2, Pallas kernels, half_states(): kernel(functools.partial(half_kernel, blocks=half, extra=extra, group=gro...  6.25 us
    pallas_call x1, Pallas kernels, local(): kernel(inside_kernel, (shape((heads, tokens, DV), BF16), shape((heads, to...  4.96 us
    ppermute x8, waiting for transfers between devices, swapped(): return lax.ppermute(array, 'ctx', [(i, i ^ distance) for i in range(n_ctx)])  2.47 us
    pallas_call x1, Pallas kernels, local(): kernel(functools.partial(mixed_kernel, shifts=n_head), (shape((tokens, he...  1.35 us
    pallas_call x1, Pallas kernels, local(): kernel(pack_kernel, (shape((packed_rows, DK), BF16),) * group + (shape((g...  1.33 us
  transfers between devices with their start and end apart: 9, of which 3 were waited for; matrix products, arithmetic and copies ran while one was open for 0% of the time, Pallas kernels for 20%

profile of v5, /device:TPU:0, one launch (start us, length us, event | category | flops | bytes accessed | tf_op | source)
XLA Modules:
  0.0 45.1 jit_solution(8637286919666146965)
XLA Ops:
  0.0 0.7 %pad_maximum_fusion.scalars_ref = f32[2,16,128]{2,1,0:T(8,128)S(1)} fusion(f32[1,16,128]{2,1,0:T(8,128)} %bitcast.10, f32[1,16,128]{2,1,0:T(8,128)} %bitcast.11), kind=kLoop, calls=%fused_computation.1 | loop fusion | flops 4096 | bytes 32768 | tf_op jit(solution)/shard_map/stack | solution.py:442
  0.7 1.3 %pack.1 = (bf16[400,128]{1,0:T(8,128)(2,1)S(1)}, bf16[400,128]{1,0:T(8,128)(2,1)S(1)}, bf16[400,128]{1,0:T(8,128)(2,1)S(1)}, bf16[400,128]{1,0:T(8,128)(2,1)S(1)...) custom-call(bf16[128,1024]{1,0:T(8,128)(2,1)} %key_ref.1, ...), custom_call_target="tpu_custom_call" | custom-call | flops 2000000000 | bytes 1048576 | tf_op jit(solution)/shard_map/pack/pallas_call | solution.py:434
  2.1 3.0 %collective-permute-start.3 = (bf16[400,128]{1,0:T(8,128)(2,1)S(1)}, bf16[400,128]{1,0:T(8,128)(2,1)S(1)}, u32[]{:S(2)}, u32[]{:S(2)}) collective-permute-start(bf16[400,128]{1,0:T(8,128)(2,1)S(1)} %get-tuple-element.48), channel_id=1, source_target_pairs={{0,2},{2,0},{4,6},{6,4},{8,10},{10,8},{12,14},{14,12},{16,18},{18,... | collective-permute-start | bytes 307208 | tf_op jit(solution)/shard_map/ppermute | solution.py:430
  5.1 1.5 %collective-permute-start.4 = (bf16[400,128]{1,0:T(8,128)(2,1)S(1)}, bf16[400,128]{1,0:T(8,128)(2,1)S(1)}, u32[]{:S(2)}, u32[]{:S(2)}) collective-permute-start(bf16[400,128]{1,0:T(8,128)(2,1)S(1)} %get-tuple-element.49), channel_id=1, source_target_pairs={{0,4},{2,6},{4,0},{6,2},{8,12},{10,14},{12,8},{14,10},{16,20},{18,... | collective-permute-start | bytes 307208 | tf_op jit(solution)/shard_map/ppermute | solution.py:430
  6.6 0.0 collective-permute-start.5
  6.6 2.0 %collective-permute-start.6 = (bf16[400,128]{1,0:T(8,128)(2,1)S(1)}, bf16[400,128]{1,0:T(8,128)(2,1)S(1)}, u32[]{:S(2)}, u32[]{:S(2)}) collective-permute-start(bf16[400,128]{1,0:T(8,128)(2,1)S(1)} %get-tuple-element.51), channel_id=1, source_target_pairs={{0,8},{2,10},{4,12},{6,14},{8,0},{10,2},{12,4},{14,6},{16,24},{18,... | collective-permute-start | bytes 307208 | tf_op jit(solution)/shard_map/ppermute | solution.py:430
  8.6 1.4 %collective-permute-start = (bf16[400,128]{1,0:T(8,128)(2,1)S(1)}, bf16[400,128]{1,0:T(8,128)(2,1)S(1)}, u32[]{:S(2)}, u32[]{:S(2)}) collective-permute-start(bf16[400,128]{1,0:T(8,128)(2,1)S(1)} %get-tuple-element.44), channel_id=1, source_target_pairs={{0,10},{2,8},{4,14},{6,12},{8,2},{10,0},{12,6},{14,4},{16,26},{18,... | collective-permute-start | bytes 307208 | tf_op jit(solution)/shard_map/ppermute | solution.py:430
  10.0 0.0 collective-permute-done.3.refs_1_
  10.0 2.5 %collective-permute-start.1 = (bf16[400,128]{1,0:T(8,128)(2,1)S(1)}, bf16[400,128]{1,0:T(8,128)(2,1)S(1)}, u32[]{:S(2)}, u32[]{:S(2)}) collective-permute-start(bf16[400,128]{1,0:T(8,128)(2,1)S(1)} %get-tuple-element.45), channel_id=1, source_target_pairs={{0,12},{2,14},{4,8},{6,10},{8,4},{10,6},{12,0},{14,2},{16,28},{18,... | collective-permute-start | bytes 307208 | tf_op jit(solution)/shard_map/ppermute | solution.py:430
  12.6 0.0 collective-permute-done.4.refs_2_
  12.6 1.1 %collective-permute-start.2 = (bf16[400,128]{1,0:T(8,128)(2,1)S(1)}, bf16[400,128]{1,0:T(8,128)(2,1)S(1)}, u32[]{:S(2)}, u32[]{:S(2)}) collective-permute-start(bf16[400,128]{1,0:T(8,128)(2,1)S(1)} %get-tuple-element.46), channel_id=1, source_target_pairs={{0,14},{2,12},{4,10},{6,8},{8,6},{10,4},{12,2},{14,0},{16,30},{18,... | collective-permute-start | bytes 307208 | tf_op jit(solution)/shard_map/ppermute | solution.py:430
  13.7 0.0 collective-permute-done.5.refs_3_
  13.7 0.0 collective-permute-done.6.refs_4_
  13.7 3.3 %own_half.1 = (f32[8,128,128]{2,1,0:T(8,128)S(1)}, bf16[8,128,128]{2,1,0:T(8,128)(2,1)S(1)}, f32[2,128,128]{2,1,0:T(8,128)S(1)}, f32[2,128,128]{2,1,0:T(8,128)S(...) custom-call(bf16[400,128]{1,0:T(8,128)(2,1)S(1)} %get-tuple-element.47.refs_0_, ...), custom_call_target="tpu_custom_call" | custom-call | flops 3500000000 | bytes 1048576 | tf_op jit(solution)/shard_map/own_half/pallas_call | solution.py:454
  17.0 0.0 copy-start.2
  17.0 0.0 copy-start.3
  17.0 0.0 copy-start.4
  17.0 0.0 collective-permute-done.refs_0_
  17.0 1.1 %collective-permute-done.1.refs_1_ = bf16[400,128]{1,0:T(8,128)(2,1)S(1)} collective-permute-done((bf16[400,128]{1,0:T(8,128)(2,1)S(1)}, bf16[400,128]{1,0:T(8,128)(2,1)S(1)}, u32[]{:S(2)}, u32[]{:S(2)}) %collective-permute-start.1) | collective-permute-done | bytes 102432 | tf_op jit(solution)/shard_map/ppermute | solution.py:430
  18.2 1.3 %collective-permute-done.2.refs_2_ = bf16[400,128]{1,0:T(8,128)(2,1)S(1)} collective-permute-done((bf16[400,128]{1,0:T(8,128)(2,1)S(1)}, bf16[400,128]{1,0:T(8,128)(2,1)S(1)}, u32[]{:S(2)}, u32[]{:S(2)}) %collective-permute-start.2) | collective-permute-done | bytes 102432 | tf_op jit(solution)/shard_map/ppermute | solution.py:430
  19.5 2.9 %other_half.1 = (f32[8,128,128]{2,1,0:T(8,128)S(1)}, bf16[8,128,128]{2,1,0:T(8,128)(2,1)S(1)}, f32[2,128,128]{2,1,0:T(8,128)S(1)}, f32[2,128,128]{2,1,0:T(8,128)S(1)}, bf16[2,128,128]{2,1,0:T(8,128)(2,1)S(1)}) custom-call(bf16[400,128]{1,0:T(8,128)(2,1)S(1)} %collective-permute-done.refs_0_, bf16[400,128]{1,0:T(8,128)(2,1)S(1)} %collective-permute-done.1.refs_1_, ...), custom_call_target="tpu_custom_call" | custom-call | flops 3500000000 | bytes 1048576 | tf_op jit(solution)/shard_map/other_half/pallas_call | solution.py:454
  22.4 2.7 %collective-permute-start.7 = (bf16[2,128,128]{2,1,0:T(8,128)(2,1)S(1)}, bf16[2,128,128]{2,1,0:T(8,128)(2,1)S(1)}, u32[]{:S(2)}, u32[]{:S(2)}) collective-permute-start(bf16[2,128,128]{2,1,0:T(8,128)(2,1)S(1)} %get-tuple-element.73), channel_id=1, source_target_pairs={{0,16},{2,18},{4,20},{6,22},{8,24},{10,26},{12,28},{14,30},{16,0},... | collective-permute-start | bytes 196616 | tf_op jit(solution)/shard_map/ppermute | solution.py:430
  25.1 0.0 copy-start
  25.1 0.0 copy-start.1
  25.1 5.0 %inside.1 = (bf16[16,128,128]{2,1,0:T(8,128)(2,1)S(1)}, bf16[16,128,128]{2,1,0:T(8,128)(2,1)S(1)}) custom-call(bf16[128,1024]{1,0:T(8,128)(2,1)S(1)} %copy-done.4, bf16[128,1024]{1,0:T(8,128)(2,1)S(1)} %copy-done.3, bf16[128,2048]{1,0:T(8,128)(2,1)S(1)} %copy-done.2, bf16[128,128]{1,0:T(8,128)(2,1)S(1)} %get-tuple-element.75.rows_ref), custom_call_target="tpu_custom_call" | custom-call | flops 5000000000 | bytes 1048576 | tf_op jit(solution)/shard_map/inside/pallas_call | solution.py:499
  30.1 0.5 %carry.1 = bf16[8,256,128]{2,1,0:T(8,128)(2,1)S(1)} custom-call(f32[8,128,128]{2,1,0:T(8,128)S(1)} %get-tuple-element.59.own_before, bf16[8,128,128]{2,1,0:T(8,128)(2,1)S(1)} %get-tuple-element.60.own_maps, f32[2,128,128]{2,1,0:T(8,128)S(1)} %get-tuple-element.61.refs_3_.own_end, f32[2,128,128]{2,1,0:T(8,128)S(1)} %get-tuple-element.62.refs_4_.own_map, ...), custom_call_target="tpu_custom_call" | custom-call | flops 600000000 | bytes 1048576 | tf_op jit(solution)/shard_map/carry/pallas_call | solution.py:510
  30.6 10.7 %all_to_all.5.state_ref = bf16[8,256,128]{2,1,0:T(8,128)(2,1)S(1)} all-to-all(bf16[8,256,128]{2,1,0:T(8,128)(2,1)S(1)} %carry.1), channel_id=1, replica_groups={{0,2,4,6,8,10,12,14},{16,18,20,22,24,26,28,30},{1,3,5,7,9,11,13,15},{17..., dimensions={0} | all-to-all | bytes 1048576 | tf_op jit(solution)/shard_map/all_to_all | solution.py:514
  41.3 1.3 %mixed.1 = (bf16[128,2048]{1,0:T(8,128)(2,1)S(1)}, bf16[128,1024]{1,0:T(8,128)(2,1)S(1)}) custom-call(bf16[8,256,128]{2,1,0:T(8,128)(2,1)S(1)} %all_to_all.5.state_ref, bf16[16,128,128]{2,1,0:T(8,128)(2,1)S(1)} %get-tuple-element.79.inside_ref, bf16[16,128,128]{2,1,0:T(8,128)(2,1)S(1)} %get-tuple-element.80.window_ref, bf16[128,2048]{1,0:T(8,128)(2,1)S(1)} %copy-done, ...), custom_call_target="tpu_custom_call" | custom-call | flops 2000000000 | bytes 1048576 | tf_op jit(solution)/shard_map/mixed/pallas_call | solution.py:516
  42.7 0.1 collective-permute-start.8
  42.8 0.8 %own_columns.1 = bf16[128,1024]{1,0:T(8,128)(2,1)S(1)} custom-call(bf16[128,2048]{1,0:T(8,128)(2,1)S(1)} %get-tuple-element.81.mixed_ref, bf16[2048,2048]{1,0:T(8,128)(2,1)S(1)} %bitcast.8), custom_call_target="tpu_custom_call" | custom-call | flops 1000000000 | bytes 1048576 | tf_op jit(solution)/shard_map/own_columns/pallas_call | solution.py:527
  43.5 0.8 %collective-permute-done.8 = bf16[128,1024]{1,0:T(8,128)(2,1)S(1)} collective-permute-done((bf16[128,1024]{1,0:T(8,128)(2,1)S(1)}, bf16[128,1024]{1,0:T(8,128)(2,1)S(1)}, u32[]{:S(2)}, u32[]{:S(2)}) %collective-permute-start.8) | collective-permute-done | bytes 262176 | tf_op jit(solution)/shard_map/ppermute | solution.py:524
  44.3 0.8 %add_convert_fusion = bf16[128,1024]{1,0:T(8,128)(2,1)} fusion(bf16[128,1024]{1,0:T(8,128)(2,1)S(1)} %collective-permute-done.8, bf16[128,1024]{1,0:T(8,128)(2,1)S(1)} %own_columns.1), kind=kLoop, calls=%fused_computation | loop fusion | flops 524288 | bytes 786432 | tf_op jit(solution)/shard_map/convert_element_type | solution.py:532
  (11 shorter events, 0.0 us)
Async XLA Ops:
  2.1 8.0 %collective-permute-start.3 = (bf16[400,128]{1,0:T(8,128)(2,1)S(1)}, bf16[400,128]{1,0:T(8,128)(2,1)S(1)}, u32[]{:S(2)}, u32[]{:S(2)}) collective-permute-start(bf16[400,128]{1,0:T(8,128)(2,1)S(1)} %get-tuple-element.48), channel_id=1, source_target_pairs={{0,2},{2,0},{4,6},{6,4},{8,10},{10,8},{12,14},{14,12},{16,18},{18,... | collective-permute-start | bytes 307208 | tf_op jit(solution)/shard_map/ppermute | solution.py:430
  5.1 7.5 %collective-permute-start.4 = (bf16[400,128]{1,0:T(8,128)(2,1)S(1)}, bf16[400,128]{1,0:T(8,128)(2,1)S(1)}, u32[]{:S(2)}, u32[]{:S(2)}) collective-permute-start(bf16[400,128]{1,0:T(8,128)(2,1)S(1)} %get-tuple-element.49), channel_id=1, source_target_pairs={{0,4},{2,6},{4,0},{6,2},{8,12},{10,14},{12,8},{14,10},{16,20},{18,... | collective-permute-start | bytes 307208 | tf_op jit(solution)/shard_map/ppermute | solution.py:430
  6.6 7.1 %collective-permute-start.5 = (bf16[400,128]{1,0:T(8,128)(2,1)S(1)}, bf16[400,128]{1,0:T(8,128)(2,1)S(1)}, u32[]{:S(2)}, u32[]{:S(2)}) collective-permute-start(bf16[400,128]{1,0:T(8,128)(2,1)S(1)} %get-tuple-element.50), channel_id=1, source_target_pairs={{0,6},{2,4},{4,2},{6,0},{8,14},{10,12},{12,10},{14,8},{16,22},{18,... | collective-permute-start | bytes 307208 | tf_op jit(solution)/shard_map/ppermute | solution.py:430
  6.6 7.1 %collective-permute-start.6 = (bf16[400,128]{1,0:T(8,128)(2,1)S(1)}, bf16[400,128]{1,0:T(8,128)(2,1)S(1)}, u32[]{:S(2)}, u32[]{:S(2)}) collective-permute-start(bf16[400,128]{1,0:T(8,128)(2,1)S(1)} %get-tuple-element.51), channel_id=1, source_target_pairs={{0,8},{2,10},{4,12},{6,14},{8,0},{10,2},{12,4},{14,6},{16,24},{18,... | collective-permute-start | bytes 307208 | tf_op jit(solution)/shard_map/ppermute | solution.py:430
  8.6 8.4 %collective-permute-start = (bf16[400,128]{1,0:T(8,128)(2,1)S(1)}, bf16[400,128]{1,0:T(8,128)(2,1)S(1)}, u32[]{:S(2)}, u32[]{:S(2)}) collective-permute-start(bf16[400,128]{1,0:T(8,128)(2,1)S(1)} %get-tuple-element.44), channel_id=1, source_target_pairs={{0,10},{2,8},{4,14},{6,12},{8,2},{10,0},{12,6},{14,4},{16,26},{18,... | collective-permute-start | bytes 307208 | tf_op jit(solution)/shard_map/ppermute | solution.py:430
  10.0 8.1 %collective-permute-start.1 = (bf16[400,128]{1,0:T(8,128)(2,1)S(1)}, bf16[400,128]{1,0:T(8,128)(2,1)S(1)}, u32[]{:S(2)}, u32[]{:S(2)}) collective-permute-start(bf16[400,128]{1,0:T(8,128)(2,1)S(1)} %get-tuple-element.45), channel_id=1, source_target_pairs={{0,12},{2,14},{4,8},{6,10},{8,4},{10,6},{12,0},{14,2},{16,28},{18,... | collective-permute-start | bytes 307208 | tf_op jit(solution)/shard_map/ppermute | solution.py:430
  12.6 6.9 %collective-permute-start.2 = (bf16[400,128]{1,0:T(8,128)(2,1)S(1)}, bf16[400,128]{1,0:T(8,128)(2,1)S(1)}, u32[]{:S(2)}, u32[]{:S(2)}) collective-permute-start(bf16[400,128]{1,0:T(8,128)(2,1)S(1)} %get-tuple-element.46), channel_id=1, source_target_pairs={{0,14},{2,12},{4,10},{6,8},{8,6},{10,4},{12,2},{14,0},{16,30},{18,... | collective-permute-start | bytes 307208 | tf_op jit(solution)/shard_map/ppermute | solution.py:430
  17.0 8.1 %copy-start.2 = (bf16[128,2048]{1,0:T(8,128)(2,1)S(1)}, bf16[128,2048]{1,0:T(8,128)(2,1)}, u32[]{:S(2)}) copy-start(bf16[128,2048]{1,0:T(8,128)(2,1)} %value_ref.1) | copy-start | bytes 1572868
  17.0 8.1 %copy-start.3 = (bf16[128,1024]{1,0:T(8,128)(2,1)S(1)}, bf16[128,1024]{1,0:T(8,128)(2,1)}, u32[]{:S(2)}) copy-start(bf16[128,1024]{1,0:T(8,128)(2,1)} %key_ref.1) | copy-start | bytes 786436
  17.0 8.1 %copy-start.4 = (bf16[128,1024]{1,0:T(8,128)(2,1)S(1)}, bf16[128,1024]{1,0:T(8,128)(2,1)}, u32[]{:S(2)}) copy-start(bf16[128,1024]{1,0:T(8,128)(2,1)} %query_ref.1) | copy-start | bytes 786436
  19.5 21.8 %slice-start = ((s8[8388608]{0:T(1024)(128)(4,1)}), s8[4194304]{0:T(1024)(128)(4,1)S(1)}, s32[]{:S(2)}) async-start(s8[8388608]{0:T(1024)(128)(4,1)} %bitcast.7), calls=%async_computation.1 | async-start | bytes 8388608
  22.4 7.7 %collective-permute-start.7 = (bf16[2,128,128]{2,1,0:T(8,128)(2,1)S(1)}, bf16[2,128,128]{2,1,0:T(8,128)(2,1)S(1)}, u32[]{:S(2)}, u32[]{:S(2)}) collective-permute-start(bf16[2,128,128]{2,1,0:T(8,128)(2,1)S(1)} %get-tuple-element.73), channel_id=1, source_target_pairs={{0,16},{2,18},{4,20},{6,22},{8,24},{10,26},{12,28},{14,30},{16,0},... | collective-permute-start | bytes 196616 | tf_op jit(solution)/shard_map/ppermute | solution.py:430
  25.1 16.2 %slice-start.1 = ((s8[8388608]{0:T(1024)(128)(4,1)}), s8[4194304]{0:T(1024)(128)(4,1)S(1)}, s32[]{:S(2)}) async-start(s8[8388608]{0:T(1024)(128)(4,1)} %bitcast.7), calls=%async_computation.2 | async-start | bytes 8388608
  25.1 16.2 %copy-start = (bf16[128,2048]{1,0:T(8,128)(2,1)S(1)}, bf16[128,2048]{1,0:T(8,128)(2,1)}, u32[]{:S(2)}) copy-start(bf16[128,2048]{1,0:T(8,128)(2,1)} %gate_ref.1) | copy-start | bytes 1572868
  25.1 16.2 %copy-start.1 = (f32[128]{0:T(128)S(1)}, f32[128]{0:T(128)}, u32[]{:S(2)}) copy-start(f32[128]{0:T(128)} %param.14) | copy-start | bytes 1540
  42.7 1.6 %collective-permute-start.8 = (bf16[128,1024]{1,0:T(8,128)(2,1)S(1)}, bf16[128,1024]{1,0:T(8,128)(2,1)S(1)}, u32[]{:S(2)}, u32[]{:S(2)}) collective-permute-start(bf16[128,1024]{1,0:T(8,128)(2,1)S(1)} %get-tuple-element.82), channel_id=1, source_target_pairs={{0,1},{1,0},{2,3},{3,2},{4,5},{5,4},{6,7},{7,6},{8,9},{9,8},{10,11... | collective-permute-start | bytes 786440 | tf_op jit(solution)/shard_map/ppermute | solution.py:524

commit v6 on v5

--- a/solution.py
+++ b/solution.py
@@ -200,7 +200,9 @@
     return solved(lowers, rights, tokens, base_bits), works
 
 
-def inside_kernel(query_ref, key_ref, value_ref, rows_ref, inside_ref, window_ref):
+def inside_kernel(
+    query_ref, key_ref, value_ref, rows_ref, inside_ref, window_ref, *, first, base_bits
+):
     tokens = query_ref.shape[0]
     blocks = inside_ref.shape[0] // REP
 
@@ -213,14 +215,14 @@
                 columns(key_ref, j, DK),
                 [columns(value_ref, j * REP + r, DV) for r in range(REP)],
             )
-            for j in range(blocks)
+            for j in range(first, first + blocks)
         ],
-        rows_ref[:, :tokens],
+        rows_ref[first * SMALL_ROWS : (first + blocks) * SMALL_ROWS, :][:, :tokens],
         tokens,
-        3,
+        base_bits,
     )
     for b in range(blocks):
-        queries = columns(query_ref, b, DK)
+        queries = columns(query_ref, first + b, DK)
         products = nt(queries, works[b * REP][0])
         queries = queries.astype(F32)
         query_col = lax.rsqrt(
@@ -366,16 +368,21 @@
 
 
 def mixed_kernel(
-    state_ref, inside_ref, window_ref, gate_ref, gain_ref, weight_ref, mixed_ref, *out_refs, shifts
+    state_ref, first_inside, first_window, second_inside, second_window, gate_ref, gain_ref,
+    weight_ref, mixed_ref, *out_refs, shifts,
 ):
     me = lax.axis_index("head")
-    gain = gain_ref[...]
+    gain, split = gain_ref[...], first_inside.shape[0]
     for j in range(state_ref.shape[0]):
         for r in range(REP):
             h = j * REP + r
             columns = pl.ds(h * DV, DV)
             state = state_ref[j, r * DK : (r + 1) * DK, :]
-            rows = inside_ref[h].astype(F32) + nn(window_ref[h], state)
+            inside, window, at = (
+                (first_inside, first_window, h) if h < split
+                else (second_inside, second_window, h - split)
+            )
+            rows = inside[at].astype(F32) + nn(window[at], state)
             scale = lax.rsqrt(jnp.mean(rows * rows, axis=1, keepdims=True) + EPSILON)
             gate = gate_ref[:, columns].astype(F32)
             mixed_ref[:, columns] = (
@@ -476,7 +483,22 @@
         )(*blocks, *more)
 
     own = half_states(taken[: half + extra], (), "own_half")
-    later, own = lax.optimization_barrier((taken[half + extra :], own))
+    def inside_part(start, count, rows, micros, base_bits):
+        return kernel(
+            functools.partial(inside_kernel, first=start, base_bits=base_bits),
+            (
+                shape((count * REP, tokens, DV), BF16),
+                shape((count * REP, tokens, DK), BF16),
+            ),
+            "inside",
+            16,
+            micros,
+        )(query_proj, key_proj, value_proj, rows)
+
+    early = max(1, group // 4)
+    rows, own = lax.optimization_barrier((rows, own))
+    first = inside_part(0, early, rows, 2.3, 4)
+    later, own, first = lax.optimization_barrier((taken[half + extra :], own, first))
     *other, end = half_states(later, own[2:], "other_half")
     own = own[:4]
 
@@ -496,17 +518,8 @@
         carried = jnp.zeros((REP, DK, DV), BF16)
 
     rows, end = lax.optimization_barrier((rows, end))
-    inside, window = kernel(
-        inside_kernel,
-        (
-            shape((heads, tokens, DV), BF16),
-            shape((heads, tokens, DK), BF16),
-        ),
-        "inside",
-        16,
-        5,
-    )(query_proj, key_proj, value_proj, rows)
-    carried, inside, window = lax.optimization_barrier((carried, inside, window))
+    second = inside_part(early, group - early, rows, 5, 3)
+    carried, second = lax.optimization_barrier((carried, second))
     states = kernel(
         carry_kernel, shape((group, REP * DK, DV), BF16), "carry", 8, 0.6
     )(*own, *other, carried)
@@ -519,7 +532,7 @@
         "mixed",
         16,
         2,
-    )(state_in, inside, window, gate_proj, norm_gain.reshape(1, DV), out_weight)
+    )(state_in, *first, *second, gate_proj, norm_gain.reshape(1, DV), out_weight)
     received = [
         lax.ppermute(other, "head", [(i, (i + 1 + s) % n_head) for i in range(n_head)])
         for s, other in enumerate(others)

time: 45.4 us -> 45.4 us (level)
  waiting for transfers between devices: 3.22 us -> 1.09 us
  Pallas kernels: 15.1 us -> 16.4 us
  blocking collectives: 10.7 us -> 11.5 us
    ppermute x8, waiting for transfers between devices: 2.47 us -> 0.34 us  [swapped(): return lax.ppermute(array, 'ctx', [(i, i ^ distance) for i in range(n_ctx)])]
    pallas_call x1 -> x2, Pallas kernels: 4.96 us -> 6.21 us  [inside_part(): kernel(functools.partial(inside_kernel, first=start, base_bits=base_bits)...]
    all_to_all x1, blocking collectives: 10.7 us -> 11.5 us  [local(): lax.all_to_all(states, 'ctx', 0, 0, axis_index_groups=groups, tiled=True)]
  transfers between devices with their start and end apart: 9 -> 9, of which waited for: 3 -> 2; matrix products, arithmetic and copies ran while one was open for 0% -> 0% of each run, Pallas kernels for 20% -> 23%
where the time goes in v6:
time: 45.4 us; the launch traced here: 45.1 us
  Pallas kernels  16.4 us (36%)
  starting transfers between devices  14.3 us (31%)
  blocking collectives  11.5 us (25%)
  other arithmetic  1.49 us (3%)
  waiting for transfers between devices  1.09 us (2%)
    ppermute x8, starting transfers between devices, swapped(): return lax.ppermute(array, 'ctx', [(i, i ^ distance) for i in range(n_ctx)])  14.3 us
    all_to_all x1, blocking collectives, local(): lax.all_to_all(states, 'ctx', 0, 0, axis_index_groups=groups, tiled=True)  11.5 us
    pallas_call x2, Pallas kernels, half_states(): kernel(functools.partial(half_kernel, blocks=half, extra=extra, group=gro...  6.26 us
    pallas_call x2, Pallas kernels, inside_part(): kernel(functools.partial(inside_kernel, first=start, base_bits=base_bits)...  6.21 us
    pallas_call x1, Pallas kernels, local(): kernel(pack_kernel, (shape((packed_rows, DK), BF16),) * group + (shape((g...  1.41 us
    pallas_call x1, Pallas kernels, local(): kernel(functools.partial(mixed_kernel, shifts=n_head), (shape((tokens, he...  1.35 us
  transfers between devices with their start and end apart: 9, of which 2 were waited for; matrix products, arithmetic and copies ran while one was open for 0% of the time, Pallas kernels for 23%

profile of v6, /device:TPU:0, one launch (start us, length us, event | category | flops | bytes accessed | tf_op | source)
XLA Modules:
  0.0 45.1 jit_solution(4182343964749203122)
XLA Ops:
  0.0 0.7 %pad_maximum_fusion.scalars_ref = f32[2,16,128]{2,1,0:T(8,128)S(1)} fusion(f32[1,16,128]{2,1,0:T(8,128)} %bitcast.10, f32[1,16,128]{2,1,0:T(8,128)} %bitcast.11), kind=kLoop, calls=%fused_computation.1 | loop fusion | flops 4096 | bytes 32768 | tf_op jit(solution)/shard_map/stack | solution.py:449
  0.7 1.4 %pack.1 = (bf16[400,128]{1,0:T(8,128)(2,1)S(1)}, bf16[400,128]{1,0:T(8,128)(2,1)S(1)}, bf16[400,128]{1,0:T(8,128)(2,1)S(1)}, bf16[400,128]{1,0:T(8,128)(2,1)S(1)...) custom-call(bf16[128,1024]{1,0:T(8,128)(2,1)} %key_ref.3, ...), custom_call_target="tpu_custom_call" | custom-call | flops 2000000000 | bytes 1048576 | tf_op jit(solution)/shard_map/pack/pallas_call | solution.py:441
  2.1 3.0 %collective-permute-start.3 = (bf16[400,128]{1,0:T(8,128)(2,1)S(1)}, bf16[400,128]{1,0:T(8,128)(2,1)S(1)}, u32[]{:S(2)}, u32[]{:S(2)}) collective-permute-start(bf16[400,128]{1,0:T(8,128)(2,1)S(1)} %get-tuple-element.61), channel_id=1, source_target_pairs={{0,2},{2,0},{4,6},{6,4},{8,10},{10,8},{12,14},{14,12},{16,18},{18,... | collective-permute-start | bytes 307208 | tf_op jit(solution)/shard_map/ppermute | solution.py:437
  5.1 1.5 %collective-permute-start.4 = (bf16[400,128]{1,0:T(8,128)(2,1)S(1)}, bf16[400,128]{1,0:T(8,128)(2,1)S(1)}, u32[]{:S(2)}, u32[]{:S(2)}) collective-permute-start(bf16[400,128]{1,0:T(8,128)(2,1)S(1)} %get-tuple-element.62), channel_id=1, source_target_pairs={{0,4},{2,6},{4,0},{6,2},{8,12},{10,14},{12,8},{14,10},{16,20},{18,... | collective-permute-start | bytes 307208 | tf_op jit(solution)/shard_map/ppermute | solution.py:437
  6.7 0.0 collective-permute-start.5
  6.7 2.0 %collective-permute-start.6 = (bf16[400,128]{1,0:T(8,128)(2,1)S(1)}, bf16[400,128]{1,0:T(8,128)(2,1)S(1)}, u32[]{:S(2)}, u32[]{:S(2)}) collective-permute-start(bf16[400,128]{1,0:T(8,128)(2,1)S(1)} %get-tuple-element.64), channel_id=1, source_target_pairs={{0,8},{2,10},{4,12},{6,14},{8,0},{10,2},{12,4},{14,6},{16,24},{18,... | collective-permute-start | bytes 307208 | tf_op jit(solution)/shard_map/ppermute | solution.py:437
  8.7 1.4 %collective-permute-start = (bf16[400,128]{1,0:T(8,128)(2,1)S(1)}, bf16[400,128]{1,0:T(8,128)(2,1)S(1)}, u32[]{:S(2)}, u32[]{:S(2)}) collective-permute-start(bf16[400,128]{1,0:T(8,128)(2,1)S(1)} %get-tuple-element.56), channel_id=1, source_target_pairs={{0,10},{2,8},{4,14},{6,12},{8,2},{10,0},{12,6},{14,4},{16,26},{18,... | collective-permute-start | bytes 307208 | tf_op jit(solution)/shard_map/ppermute | solution.py:437
  10.1 0.0 collective-permute-done.3.refs_1_
  10.1 2.5 %collective-permute-start.1 = (bf16[400,128]{1,0:T(8,128)(2,1)S(1)}, bf16[400,128]{1,0:T(8,128)(2,1)S(1)}, u32[]{:S(2)}, u32[]{:S(2)}) collective-permute-start(bf16[400,128]{1,0:T(8,128)(2,1)S(1)} %get-tuple-element.57), channel_id=1, source_target_pairs={{0,12},{2,14},{4,8},{6,10},{8,4},{10,6},{12,0},{14,2},{16,28},{18,... | collective-permute-start | bytes 307208 | tf_op jit(solution)/shard_map/ppermute | solution.py:437
  12.6 0.0 collective-permute-done.4.refs_2_
  12.6 1.1 %collective-permute-start.2 = (bf16[400,128]{1,0:T(8,128)(2,1)S(1)}, bf16[400,128]{1,0:T(8,128)(2,1)S(1)}, u32[]{:S(2)}, u32[]{:S(2)}) collective-permute-start(bf16[400,128]{1,0:T(8,128)(2,1)S(1)} %get-tuple-element.58), channel_id=1, source_target_pairs={{0,14},{2,12},{4,10},{6,8},{8,6},{10,4},{12,2},{14,0},{16,30},{18,... | collective-permute-start | bytes 307208 | tf_op jit(solution)/shard_map/ppermute | solution.py:437
  13.7 0.0 collective-permute-done.5.refs_3_
  13.8 0.0 collective-permute-done.6.refs_4_
  13.8 3.3 %own_half.1 = (f32[8,128,128]{2,1,0:T(8,128)S(1)}, bf16[8,128,128]{2,1,0:T(8,128)(2,1)S(1)}, f32[2,128,128]{2,1,0:T(8,128)S(1)}, f32[2,128,128]{2,1,0:T(8,128)S(...) custom-call(bf16[400,128]{1,0:T(8,128)(2,1)S(1)} %get-tuple-element.60.refs_0_, ...), custom_call_target="tpu_custom_call" | custom-call | flops 3500000000 | bytes 1048576 | tf_op jit(solution)/shard_map/own_half/pallas_call | solution.py:461
  17.1 2.1 %inside.2 = (bf16[4,128,128]{2,1,0:T(8,128)(2,1)S(1)}, bf16[4,128,128]{2,1,0:T(8,128)(2,1)S(1)}) custom-call(bf16[128,1024]{1,0:T(8,128)(2,1)S(1)} %copy-done.4, bf16[128,1024]{1,0:T(8,128)(2,1)S(1)} %copy-done.3, bf16[128,2048]{1,0:T(8,128)(2,1)S(1)} %copy-done.2, bf16[128,128]{1,0:T(8,128)(2,1)S(1)} %get-tuple-element.97.rows_ref), custom_call_target="tpu_custom_call" | custom-call | flops 2300000000 | bytes 1048576 | tf_op jit(solution)/shard_map/inside/pallas_call | solution.py:487
  19.2 0.0 collective-permute-done.refs_0_
  19.2 0.0 collective-permute-done.1.refs_1_
  19.2 0.3 collective-permute-done.2.refs_2_
  19.6 2.9 %other_half.1 = (f32[8,128,128]{2,1,0:T(8,128)S(1)}, bf16[8,128,128]{2,1,0:T(8,128)(2,1)S(1)}, f32[2,128,128]{2,1,0:T(8,128)S(1)}, f32[2,128,128]{2,1,0:T(8,128)S(1)}, bf16[2,128,128]{2,1,0:T(8,128)(2,1)S(1)}) custom-call(bf16[400,128]{1,0:T(8,128)(2,1)S(1)} %collective-permute-done.refs_0_, bf16[400,128]{1,0:T(8,128)(2,1)S(1)} %collective-permute-done.1.refs_1_, ...), custom_call_target="tpu_custom_call" | custom-call | flops 3500000000 | bytes 1048576 | tf_op jit(solution)/shard_map/other_half/pallas_call | solution.py:461
  22.5 0.0 slice-start
  22.5 0.0 slice-start.1
  22.5 0.0 copy-start
  22.6 0.0 copy-start.1
  22.6 2.7 %collective-permute-start.7 = (bf16[2,128,128]{2,1,0:T(8,128)(2,1)S(1)}, bf16[2,128,128]{2,1,0:T(8,128)(2,1)S(1)}, u32[]{:S(2)}, u32[]{:S(2)}) collective-permute-start(bf16[2,128,128]{2,1,0:T(8,128)(2,1)S(1)} %get-tuple-element.96), channel_id=1, source_target_pairs={{0,16},{2,18},{4,20},{6,22},{8,24},{10,26},{12,28},{14,30},{16,0},... | collective-permute-start | bytes 196616 | tf_op jit(solution)/shard_map/ppermute | solution.py:437
  25.2 4.1 %inside.3 = (bf16[12,128,128]{2,1,0:T(8,128)(2,1)S(1)}, bf16[12,128,128]{2,1,0:T(8,128)(2,1)S(1)}) custom-call(bf16[128,1024]{1,0:T(8,128)(2,1)S(1)} %copy-done.4, bf16[128,1024]{1,0:T(8,128)(2,1)S(1)} %copy-done.3, bf16[128,2048]{1,0:T(8,128)(2,1)S(1)} %copy-done.2, bf16[128,128]{1,0:T(8,128)(2,1)S(1)} %get-tuple-element.97.rows_ref), custom_call_target="tpu_custom_call" | custom-call | flops 5000000000 | bytes 1048576 | tf_op jit(solution)/shard_map/inside/pallas_call | solution.py:487
  29.3 0.5 %carry.1 = bf16[8,256,128]{2,1,0:T(8,128)(2,1)S(1)} custom-call(f32[8,128,128]{2,1,0:T(8,128)S(1)} %get-tuple-element.82.own_before, bf16[8,128,128]{2,1,0:T(8,128)(2,1)S(1)} %get-tuple-element.83.own_maps, f32[2,128,128]{2,1,0:T(8,128)S(1)} %get-tuple-element.84.refs_3_.own_end, f32[2,128,128]{2,1,0:T(8,128)S(1)} %get-tuple-element.85.refs_4_.own_map, ...), custom_call_target="tpu_custom_call" | custom-call | flops 600000000 | bytes 1048576 | tf_op jit(solution)/shard_map/carry/pallas_call | solution.py:523
  29.8 11.5 %all_to_all.5.state_ref = bf16[8,256,128]{2,1,0:T(8,128)(2,1)S(1)} all-to-all(bf16[8,256,128]{2,1,0:T(8,128)(2,1)S(1)} %carry.1), channel_id=1, replica_groups={{0,2,4,6,8,10,12,14},{16,18,20,22,24,26,28,30},{1,3,5,7,9,11,13,15},{17..., dimensions={0} | all-to-all | bytes 1048576 | tf_op jit(solution)/shard_map/all_to_all | solution.py:527
  41.3 1.4 %mixed.1 = (bf16[128,2048]{1,0:T(8,128)(2,1)S(1)}, bf16[128,1024]{1,0:T(8,128)(2,1)S(1)}) custom-call(bf16[8,256,128]{2,1,0:T(8,128)(2,1)S(1)} %all_to_all.5.state_ref, bf16[4,128,128]{2,1,0:T(8,128)(2,1)S(1)} %get-tuple-element.101.first_inside, bf16[4,128,128]{2,1,0:T(8,128)(2,1)S(1)} %get-tuple-element.102.first_window, ...), custom_call_target="tpu_custom_call" | custom-call | flops 2000000000 | bytes 1048576 | tf_op jit(solution)/shard_map/mixed/pallas_call | solution.py:529
  42.7 0.1 collective-permute-start.8
  42.8 0.8 %own_columns.1 = bf16[128,1024]{1,0:T(8,128)(2,1)S(1)} custom-call(bf16[128,2048]{1,0:T(8,128)(2,1)S(1)} %get-tuple-element.105.mixed_ref, bf16[2048,2048]{1,0:T(8,128)(2,1)S(1)} %bitcast.8), custom_call_target="tpu_custom_call" | custom-call | flops 1000000000 | bytes 1048576 | tf_op jit(solution)/shard_map/own_columns/pallas_call | solution.py:540
  43.5 0.8 %collective-permute-done.8 = bf16[128,1024]{1,0:T(8,128)(2,1)S(1)} collective-permute-done((bf16[128,1024]{1,0:T(8,128)(2,1)S(1)}, bf16[128,1024]{1,0:T(8,128)(2,1)S(1)}, u32[]{:S(2)}, u32[]{:S(2)}) %collective-permute-start.8) | collective-permute-done | bytes 262176 | tf_op jit(solution)/shard_map/ppermute | solution.py:537
  44.3 0.8 %add_convert_fusion = bf16[128,1024]{1,0:T(8,128)(2,1)} fusion(bf16[128,1024]{1,0:T(8,128)(2,1)S(1)} %collective-permute-done.8, bf16[128,1024]{1,0:T(8,128)(2,1)S(1)} %own_columns.1), kind=kLoop, calls=%fused_computation | loop fusion | flops 524288 | bytes 786432 | tf_op jit(solution)/shard_map/convert_element_type | solution.py:545
  (12 shorter events, 0.0 us)
Async XLA Ops:
  0.7 16.4 %copy-start.2 = (bf16[128,2048]{1,0:T(8,128)(2,1)S(1)}, bf16[128,2048]{1,0:T(8,128)(2,1)}, u32[]{:S(2)}) copy-start(bf16[128,2048]{1,0:T(8,128)(2,1)} %value_ref.3) | copy-start | bytes 1572868
  0.7 16.4 %copy-start.3 = (bf16[128,1024]{1,0:T(8,128)(2,1)S(1)}, bf16[128,1024]{1,0:T(8,128)(2,1)}, u32[]{:S(2)}) copy-start(bf16[128,1024]{1,0:T(8,128)(2,1)} %key_ref.3) | copy-start | bytes 786436
  0.7 16.4 %copy-start.4 = (bf16[128,1024]{1,0:T(8,128)(2,1)S(1)}, bf16[128,1024]{1,0:T(8,128)(2,1)}, u32[]{:S(2)}) copy-start(bf16[128,1024]{1,0:T(8,128)(2,1)} %query_ref.3) | copy-start | bytes 786436
  2.1 8.0 %collective-permute-start.3 = (bf16[400,128]{1,0:T(8,128)(2,1)S(1)}, bf16[400,128]{1,0:T(8,128)(2,1)S(1)}, u32[]{:S(2)}, u32[]{:S(2)}) collective-permute-start(bf16[400,128]{1,0:T(8,128)(2,1)S(1)} %get-tuple-element.61), channel_id=1, source_target_pairs={{0,2},{2,0},{4,6},{6,4},{8,10},{10,8},{12,14},{14,12},{16,18},{18,... | collective-permute-start | bytes 307208 | tf_op jit(solution)/shard_map/ppermute | solution.py:437
  5.1 7.5 %collective-permute-start.4 = (bf16[400,128]{1,0:T(8,128)(2,1)S(1)}, bf16[400,128]{1,0:T(8,128)(2,1)S(1)}, u32[]{:S(2)}, u32[]{:S(2)}) collective-permute-start(bf16[400,128]{1,0:T(8,128)(2,1)S(1)} %get-tuple-element.62), channel_id=1, source_target_pairs={{0,4},{2,6},{4,0},{6,2},{8,12},{10,14},{12,8},{14,10},{16,20},{18,... | collective-permute-start | bytes 307208 | tf_op jit(solution)/shard_map/ppermute | solution.py:437
  6.7 7.1 %collective-permute-start.5 = (bf16[400,128]{1,0:T(8,128)(2,1)S(1)}, bf16[400,128]{1,0:T(8,128)(2,1)S(1)}, u32[]{:S(2)}, u32[]{:S(2)}) collective-permute-start(bf16[400,128]{1,0:T(8,128)(2,1)S(1)} %get-tuple-element.63), channel_id=1, source_target_pairs={{0,6},{2,4},{4,2},{6,0},{8,14},{10,12},{12,10},{14,8},{16,22},{18,... | collective-permute-start | bytes 307208 | tf_op jit(solution)/shard_map/ppermute | solution.py:437
  6.7 7.1 %collective-permute-start.6 = (bf16[400,128]{1,0:T(8,128)(2,1)S(1)}, bf16[400,128]{1,0:T(8,128)(2,1)S(1)}, u32[]{:S(2)}, u32[]{:S(2)}) collective-permute-start(bf16[400,128]{1,0:T(8,128)(2,1)S(1)} %get-tuple-element.64), channel_id=1, source_target_pairs={{0,8},{2,10},{4,12},{6,14},{8,0},{10,2},{12,4},{14,6},{16,24},{18,... | collective-permute-start | bytes 307208 | tf_op jit(solution)/shard_map/ppermute | solution.py:437
  8.7 10.5 %collective-permute-start = (bf16[400,128]{1,0:T(8,128)(2,1)S(1)}, bf16[400,128]{1,0:T(8,128)(2,1)S(1)}, u32[]{:S(2)}, u32[]{:S(2)}) collective-permute-start(bf16[400,128]{1,0:T(8,128)(2,1)S(1)} %get-tuple-element.56), channel_id=1, source_target_pairs={{0,10},{2,8},{4,14},{6,12},{8,2},{10,0},{12,6},{14,4},{16,26},{18,... | collective-permute-start | bytes 307208 | tf_op jit(solution)/shard_map/ppermute | solution.py:437
  10.1 9.1 %collective-permute-start.1 = (bf16[400,128]{1,0:T(8,128)(2,1)S(1)}, bf16[400,128]{1,0:T(8,128)(2,1)S(1)}, u32[]{:S(2)}, u32[]{:S(2)}) collective-permute-start(bf16[400,128]{1,0:T(8,128)(2,1)S(1)} %get-tuple-element.57), channel_id=1, source_target_pairs={{0,12},{2,14},{4,8},{6,10},{8,4},{10,6},{12,0},{14,2},{16,28},{18,... | collective-permute-start | bytes 307208 | tf_op jit(solution)/shard_map/ppermute | solution.py:437
  12.6 6.9 %collective-permute-start.2 = (bf16[400,128]{1,0:T(8,128)(2,1)S(1)}, bf16[400,128]{1,0:T(8,128)(2,1)S(1)}, u32[]{:S(2)}, u32[]{:S(2)}) collective-permute-start(bf16[400,128]{1,0:T(8,128)(2,1)S(1)} %get-tuple-element.58), channel_id=1, source_target_pairs={{0,14},{2,12},{4,10},{6,8},{8,6},{10,4},{12,2},{14,0},{16,30},{18,... | collective-permute-start | bytes 307208 | tf_op jit(solution)/shard_map/ppermute | solution.py:437
  22.5 18.8 %slice-start = ((s8[8388608]{0:T(1024)(128)(4,1)}), s8[4194304]{0:T(1024)(128)(4,1)S(1)}, s32[]{:S(2)}) async-start(s8[8388608]{0:T(1024)(128)(4,1)} %bitcast.7), calls=%async_computation.1 | async-start | bytes 8388608
  22.5 18.8 %slice-start.1 = ((s8[8388608]{0:T(1024)(128)(4,1)}), s8[4194304]{0:T(1024)(128)(4,1)S(1)}, s32[]{:S(2)}) async-start(s8[8388608]{0:T(1024)(128)(4,1)} %bitcast.7), calls=%async_computation.2 | async-start | bytes 8388608
  22.5 18.8 %copy-start = (bf16[128,2048]{1,0:T(8,128)(2,1)S(1)}, bf16[128,2048]{1,0:T(8,128)(2,1)}, u32[]{:S(2)}) copy-start(bf16[128,2048]{1,0:T(8,128)(2,1)} %gate_ref.1) | copy-start | bytes 1572868
  22.6 18.8 %copy-start.1 = (f32[128]{0:T(128)S(1)}, f32[128]{0:T(128)}, u32[]{:S(2)}) copy-start(f32[128]{0:T(128)} %param.14) | copy-start | bytes 1540
  22.6 6.8 %collective-permute-start.7 = (bf16[2,128,128]{2,1,0:T(8,128)(2,1)S(1)}, bf16[2,128,128]{2,1,0:T(8,128)(2,1)S(1)}, u32[]{:S(2)}, u32[]{:S(2)}) collective-permute-start(bf16[2,128,128]{2,1,0:T(8,128)(2,1)S(1)} %get-tuple-element.96), channel_id=1, source_target_pairs={{0,16},{2,18},{4,20},{6,22},{8,24},{10,26},{12,28},{14,30},{16,0},... | collective-permute-start | bytes 196616 | tf_op jit(solution)/shard_map/ppermute | solution.py:437
  42.7 1.6 %collective-permute-start.8 = (bf16[128,1024]{1,0:T(8,128)(2,1)S(1)}, bf16[128,1024]{1,0:T(8,128)(2,1)S(1)}, u32[]{:S(2)}, u32[]{:S(2)}) collective-permute-start(bf16[128,1024]{1,0:T(8,128)(2,1)S(1)} %get-tuple-element.106), channel_id=1, source_target_pairs={{0,1},{1,0},{2,3},{3,2},{4,5},{5,4},{6,7},{7,6},{8,9},{9,8},{10,11... | collective-permute-start | bytes 786440 | tf_op jit(solution)/shard_map/ppermute | solution.py:537

commit v7 on v6

--- a/solution.py
+++ b/solution.py
@@ -386,7 +386,7 @@
             scale = lax.rsqrt(jnp.mean(rows * rows, axis=1, keepdims=True) + EPSILON)
             gate = gate_ref[:, columns].astype(F32)
             mixed_ref[:, columns] = (
-                rows * scale * gain * (gate / (1.0 + jnp.exp(-gate)))
+                rows * scale * gain * (0.5 * gate * (1.0 + jnp.tanh(0.5 * gate)))
             ).astype(BF16)
     for n, out_ref in enumerate(out_refs):
         columns = columns_of(out_ref.shape[1], lax.rem(me + 1 + n, shifts))

time: 45.4 us -> 45.2 us (level)
  no operation moved by 1% of the time
where the time goes in v7:
time: 45.2 us; the launch traced here: 45 us
  Pallas kernels  16.3 us (36%)
  starting transfers between devices  14.3 us (32%)
  blocking collectives  11.5 us (25%)
  other arithmetic  1.49 us (3%)
  waiting for transfers between devices  1.09 us (2%)
    ppermute x8, starting transfers between devices, swapped(): return lax.ppermute(array, 'ctx', [(i, i ^ distance) for i in range(n_ctx)])  14.3 us
    all_to_all x1, blocking collectives, local(): lax.all_to_all(states, 'ctx', 0, 0, axis_index_groups=groups, tiled=True)  11.5 us
    pallas_call x2, Pallas kernels, half_states(): kernel(functools.partial(half_kernel, blocks=half, extra=extra, group=gro...  6.26 us
    pallas_call x2, Pallas kernels, inside_part(): kernel(functools.partial(inside_kernel, first=start, base_bits=base_bits)...  6.21 us
    pallas_call x1, Pallas kernels, local(): kernel(pack_kernel, (shape((packed_rows, DK), BF16),) * group + (shape((g...  1.41 us
    pallas_call x1, Pallas kernels, local(): kernel(functools.partial(mixed_kernel, shifts=n_head), (shape((tokens, he...  1.24 us
  transfers between devices with their start and end apart: 9, of which 2 were waited for; matrix products, arithmetic and copies ran while one was open for 0% of the time, Pallas kernels for 23%

profile of v7, /device:TPU:0, one launch (start us, length us, event | category | flops | bytes accessed | tf_op | source)
XLA Modules:
  0.0 45.0 jit_solution(17162068595355785019)
XLA Ops:
  0.0 0.7 %pad_maximum_fusion.scalars_ref = f32[2,16,128]{2,1,0:T(8,128)S(1)} fusion(f32[1,16,128]{2,1,0:T(8,128)} %bitcast.10, f32[1,16,128]{2,1,0:T(8,128)} %bitcast.11), kind=kLoop, calls=%fused_computation.1 | loop fusion | flops 4096 | bytes 32768 | tf_op jit(solution)/shard_map/stack | solution.py:449
  0.7 1.4 %pack.1 = (bf16[400,128]{1,0:T(8,128)(2,1)S(1)}, bf16[400,128]{1,0:T(8,128)(2,1)S(1)}, bf16[400,128]{1,0:T(8,128)(2,1)S(1)}, bf16[400,128]{1,0:T(8,128)(2,1)S(1)...) custom-call(bf16[128,1024]{1,0:T(8,128)(2,1)} %key_ref.3, ...), custom_call_target="tpu_custom_call" | custom-call | flops 2000000000 | bytes 1048576 | tf_op jit(solution)/shard_map/pack/pallas_call | solution.py:441
  2.1 3.0 %collective-permute-start.3 = (bf16[400,128]{1,0:T(8,128)(2,1)S(1)}, bf16[400,128]{1,0:T(8,128)(2,1)S(1)}, u32[]{:S(2)}, u32[]{:S(2)}) collective-permute-start(bf16[400,128]{1,0:T(8,128)(2,1)S(1)} %get-tuple-element.61), channel_id=1, source_target_pairs={{0,2},{2,0},{4,6},{6,4},{8,10},{10,8},{12,14},{14,12},{16,18},{18,... | collective-permute-start | bytes 307208 | tf_op jit(solution)/shard_map/ppermute | solution.py:437
  5.1 1.5 %collective-permute-start.4 = (bf16[400,128]{1,0:T(8,128)(2,1)S(1)}, bf16[400,128]{1,0:T(8,128)(2,1)S(1)}, u32[]{:S(2)}, u32[]{:S(2)}) collective-permute-start(bf16[400,128]{1,0:T(8,128)(2,1)S(1)} %get-tuple-element.62), channel_id=1, source_target_pairs={{0,4},{2,6},{4,0},{6,2},{8,12},{10,14},{12,8},{14,10},{16,20},{18,... | collective-permute-start | bytes 307208 | tf_op jit(solution)/shard_map/ppermute | solution.py:437
  6.7 0.0 collective-permute-start.5
  6.7 2.0 %collective-permute-start.6 = (bf16[400,128]{1,0:T(8,128)(2,1)S(1)}, bf16[400,128]{1,0:T(8,128)(2,1)S(1)}, u32[]{:S(2)}, u32[]{:S(2)}) collective-permute-start(bf16[400,128]{1,0:T(8,128)(2,1)S(1)} %get-tuple-element.64), channel_id=1, source_target_pairs={{0,8},{2,10},{4,12},{6,14},{8,0},{10,2},{12,4},{14,6},{16,24},{18,... | collective-permute-start | bytes 307208 | tf_op jit(solution)/shard_map/ppermute | solution.py:437
  8.7 1.4 %collective-permute-start = (bf16[400,128]{1,0:T(8,128)(2,1)S(1)}, bf16[400,128]{1,0:T(8,128)(2,1)S(1)}, u32[]{:S(2)}, u32[]{:S(2)}) collective-permute-start(bf16[400,128]{1,0:T(8,128)(2,1)S(1)} %get-tuple-element.56), channel_id=1, source_target_pairs={{0,10},{2,8},{4,14},{6,12},{8,2},{10,0},{12,6},{14,4},{16,26},{18,... | collective-permute-start | bytes 307208 | tf_op jit(solution)/shard_map/ppermute | solution.py:437
  10.1 0.0 collective-permute-done.3.refs_1_
  10.1 2.5 %collective-permute-start.1 = (bf16[400,128]{1,0:T(8,128)(2,1)S(1)}, bf16[400,128]{1,0:T(8,128)(2,1)S(1)}, u32[]{:S(2)}, u32[]{:S(2)}) collective-permute-start(bf16[400,128]{1,0:T(8,128)(2,1)S(1)} %get-tuple-element.57), channel_id=1, source_target_pairs={{0,12},{2,14},{4,8},{6,10},{8,4},{10,6},{12,0},{14,2},{16,28},{18,... | collective-permute-start | bytes 307208 | tf_op jit(solution)/shard_map/ppermute | solution.py:437
  12.6 0.0 collective-permute-done.4.refs_2_
  12.6 1.1 %collective-permute-start.2 = (bf16[400,128]{1,0:T(8,128)(2,1)S(1)}, bf16[400,128]{1,0:T(8,128)(2,1)S(1)}, u32[]{:S(2)}, u32[]{:S(2)}) collective-permute-start(bf16[400,128]{1,0:T(8,128)(2,1)S(1)} %get-tuple-element.58), channel_id=1, source_target_pairs={{0,14},{2,12},{4,10},{6,8},{8,6},{10,4},{12,2},{14,0},{16,30},{18,... | collective-permute-start | bytes 307208 | tf_op jit(solution)/shard_map/ppermute | solution.py:437
  13.7 0.0 collective-permute-done.5.refs_3_
  13.8 0.0 collective-permute-done.6.refs_4_
  13.8 3.3 %own_half.1 = (f32[8,128,128]{2,1,0:T(8,128)S(1)}, bf16[8,128,128]{2,1,0:T(8,128)(2,1)S(1)}, f32[2,128,128]{2,1,0:T(8,128)S(1)}, f32[2,128,128]{2,1,0:T(8,128)S(...) custom-call(bf16[400,128]{1,0:T(8,128)(2,1)S(1)} %get-tuple-element.60.refs_0_, ...), custom_call_target="tpu_custom_call" | custom-call | flops 3500000000 | bytes 1048576 | tf_op jit(solution)/shard_map/own_half/pallas_call | solution.py:461
  17.1 2.1 %inside.2 = (bf16[4,128,128]{2,1,0:T(8,128)(2,1)S(1)}, bf16[4,128,128]{2,1,0:T(8,128)(2,1)S(1)}) custom-call(bf16[128,1024]{1,0:T(8,128)(2,1)S(1)} %copy-done.4, bf16[128,1024]{1,0:T(8,128)(2,1)S(1)} %copy-done.3, bf16[128,2048]{1,0:T(8,128)(2,1)S(1)} %copy-done.2, bf16[128,128]{1,0:T(8,128)(2,1)S(1)} %get-tuple-element.97.rows_ref), custom_call_target="tpu_custom_call" | custom-call | flops 2300000000 | bytes 1048576 | tf_op jit(solution)/shard_map/inside/pallas_call | solution.py:487
  19.2 0.0 collective-permute-done.refs_0_
  19.2 0.0 collective-permute-done.1.refs_1_
  19.2 0.3 collective-permute-done.2.refs_2_
  19.6 2.9 %other_half.1 = (f32[8,128,128]{2,1,0:T(8,128)S(1)}, bf16[8,128,128]{2,1,0:T(8,128)(2,1)S(1)}, f32[2,128,128]{2,1,0:T(8,128)S(1)}, f32[2,128,128]{2,1,0:T(8,128)S(1)}, bf16[2,128,128]{2,1,0:T(8,128)(2,1)S(1)}) custom-call(bf16[400,128]{1,0:T(8,128)(2,1)S(1)} %collective-permute-done.refs_0_, bf16[400,128]{1,0:T(8,128)(2,1)S(1)} %collective-permute-done.1.refs_1_, ...), custom_call_target="tpu_custom_call" | custom-call | flops 3500000000 | bytes 1048576 | tf_op jit(solution)/shard_map/other_half/pallas_call | solution.py:461
  22.5 0.0 slice-start
  22.5 0.0 slice-start.1
  22.5 0.0 copy-start
  22.6 0.0 copy-start.1
  22.6 2.7 %collective-permute-start.7 = (bf16[2,128,128]{2,1,0:T(8,128)(2,1)S(1)}, bf16[2,128,128]{2,1,0:T(8,128)(2,1)S(1)}, u32[]{:S(2)}, u32[]{:S(2)}) collective-permute-start(bf16[2,128,128]{2,1,0:T(8,128)(2,1)S(1)} %get-tuple-element.96), channel_id=1, source_target_pairs={{0,16},{2,18},{4,20},{6,22},{8,24},{10,26},{12,28},{14,30},{16,0},... | collective-permute-start | bytes 196616 | tf_op jit(solution)/shard_map/ppermute | solution.py:437
  25.2 4.1 %inside.3 = (bf16[12,128,128]{2,1,0:T(8,128)(2,1)S(1)}, bf16[12,128,128]{2,1,0:T(8,128)(2,1)S(1)}) custom-call(bf16[128,1024]{1,0:T(8,128)(2,1)S(1)} %copy-done.4, bf16[128,1024]{1,0:T(8,128)(2,1)S(1)} %copy-done.3, bf16[128,2048]{1,0:T(8,128)(2,1)S(1)} %copy-done.2, bf16[128,128]{1,0:T(8,128)(2,1)S(1)} %get-tuple-element.97.rows_ref), custom_call_target="tpu_custom_call" | custom-call | flops 5000000000 | bytes 1048576 | tf_op jit(solution)/shard_map/inside/pallas_call | solution.py:487
  29.3 0.5 %carry.1 = bf16[8,256,128]{2,1,0:T(8,128)(2,1)S(1)} custom-call(f32[8,128,128]{2,1,0:T(8,128)S(1)} %get-tuple-element.82.own_before, bf16[8,128,128]{2,1,0:T(8,128)(2,1)S(1)} %get-tuple-element.83.own_maps, f32[2,128,128]{2,1,0:T(8,128)S(1)} %get-tuple-element.84.refs_3_.own_end, f32[2,128,128]{2,1,0:T(8,128)S(1)} %get-tuple-element.85.refs_4_.own_map, ...), custom_call_target="tpu_custom_call" | custom-call | flops 600000000 | bytes 1048576 | tf_op jit(solution)/shard_map/carry/pallas_call | solution.py:523
  29.8 11.5 %all_to_all.5.state_ref = bf16[8,256,128]{2,1,0:T(8,128)(2,1)S(1)} all-to-all(bf16[8,256,128]{2,1,0:T(8,128)(2,1)S(1)} %carry.1), channel_id=1, replica_groups={{0,2,4,6,8,10,12,14},{16,18,20,22,24,26,28,30},{1,3,5,7,9,11,13,15},{17..., dimensions={0} | all-to-all | bytes 1048576 | tf_op jit(solution)/shard_map/all_to_all | solution.py:527
  41.3 1.2 %mixed.1 = (bf16[128,2048]{1,0:T(8,128)(2,1)S(1)}, bf16[128,1024]{1,0:T(8,128)(2,1)S(1)}) custom-call(bf16[8,256,128]{2,1,0:T(8,128)(2,1)S(1)} %all_to_all.5.state_ref, bf16[4,128,128]{2,1,0:T(8,128)(2,1)S(1)} %get-tuple-element.101.first_inside, bf16[4,128,128]{2,1,0:T(8,128)(2,1)S(1)} %get-tuple-element.102.first_window, ...), custom_call_target="tpu_custom_call" | custom-call | flops 2000000000 | bytes 1048576 | tf_op jit(solution)/shard_map/mixed/pallas_call | solution.py:529
  42.6 0.1 collective-permute-start.8
  42.7 0.8 %own_columns.1 = bf16[128,1024]{1,0:T(8,128)(2,1)S(1)} custom-call(bf16[128,2048]{1,0:T(8,128)(2,1)S(1)} %get-tuple-element.105.mixed_ref, bf16[2048,2048]{1,0:T(8,128)(2,1)S(1)} %bitcast.8), custom_call_target="tpu_custom_call" | custom-call | flops 1000000000 | bytes 1048576 | tf_op jit(solution)/shard_map/own_columns/pallas_call | solution.py:540
  43.4 0.8 %collective-permute-done.8 = bf16[128,1024]{1,0:T(8,128)(2,1)S(1)} collective-permute-done((bf16[128,1024]{1,0:T(8,128)(2,1)S(1)}, bf16[128,1024]{1,0:T(8,128)(2,1)S(1)}, u32[]{:S(2)}, u32[]{:S(2)}) %collective-permute-start.8) | collective-permute-done | bytes 262176 | tf_op jit(solution)/shard_map/ppermute | solution.py:537
  44.2 0.8 %add_convert_fusion = bf16[128,1024]{1,0:T(8,128)(2,1)} fusion(bf16[128,1024]{1,0:T(8,128)(2,1)S(1)} %collective-permute-done.8, bf16[128,1024]{1,0:T(8,128)(2,1)S(1)} %own_columns.1), kind=kLoop, calls=%fused_computation | loop fusion | flops 524288 | bytes 786432 | tf_op jit(solution)/shard_map/convert_element_type | solution.py:545
  (12 shorter events, 0.0 us)
Async XLA Ops:
  0.7 16.4 %copy-start.2 = (bf16[128,2048]{1,0:T(8,128)(2,1)S(1)}, bf16[128,2048]{1,0:T(8,128)(2,1)}, u32[]{:S(2)}) copy-start(bf16[128,2048]{1,0:T(8,128)(2,1)} %value_ref.3) | copy-start | bytes 1572868
  0.7 16.4 %copy-start.3 = (bf16[128,1024]{1,0:T(8,128)(2,1)S(1)}, bf16[128,1024]{1,0:T(8,128)(2,1)}, u32[]{:S(2)}) copy-start(bf16[128,1024]{1,0:T(8,128)(2,1)} %key_ref.3) | copy-start | bytes 786436
  0.7 16.4 %copy-start.4 = (bf16[128,1024]{1,0:T(8,128)(2,1)S(1)}, bf16[128,1024]{1,0:T(8,128)(2,1)}, u32[]{:S(2)}) copy-start(bf16[128,1024]{1,0:T(8,128)(2,1)} %query_ref.3) | copy-start | bytes 786436
  2.1 8.0 %collective-permute-start.3 = (bf16[400,128]{1,0:T(8,128)(2,1)S(1)}, bf16[400,128]{1,0:T(8,128)(2,1)S(1)}, u32[]{:S(2)}, u32[]{:S(2)}) collective-permute-start(bf16[400,128]{1,0:T(8,128)(2,1)S(1)} %get-tuple-element.61), channel_id=1, source_target_pairs={{0,2},{2,0},{4,6},{6,4},{8,10},{10,8},{12,14},{14,12},{16,18},{18,... | collective-permute-start | bytes 307208 | tf_op jit(solution)/shard_map/ppermute | solution.py:437
  5.1 7.5 %collective-permute-start.4 = (bf16[400,128]{1,0:T(8,128)(2,1)S(1)}, bf16[400,128]{1,0:T(8,128)(2,1)S(1)}, u32[]{:S(2)}, u32[]{:S(2)}) collective-permute-start(bf16[400,128]{1,0:T(8,128)(2,1)S(1)} %get-tuple-element.62), channel_id=1, source_target_pairs={{0,4},{2,6},{4,0},{6,2},{8,12},{10,14},{12,8},{14,10},{16,20},{18,... | collective-permute-start | bytes 307208 | tf_op jit(solution)/shard_map/ppermute | solution.py:437
  6.7 7.1 %collective-permute-start.5 = (bf16[400,128]{1,0:T(8,128)(2,1)S(1)}, bf16[400,128]{1,0:T(8,128)(2,1)S(1)}, u32[]{:S(2)}, u32[]{:S(2)}) collective-permute-start(bf16[400,128]{1,0:T(8,128)(2,1)S(1)} %get-tuple-element.63), channel_id=1, source_target_pairs={{0,6},{2,4},{4,2},{6,0},{8,14},{10,12},{12,10},{14,8},{16,22},{18,... | collective-permute-start | bytes 307208 | tf_op jit(solution)/shard_map/ppermute | solution.py:437
  6.7 7.1 %collective-permute-start.6 = (bf16[400,128]{1,0:T(8,128)(2,1)S(1)}, bf16[400,128]{1,0:T(8,128)(2,1)S(1)}, u32[]{:S(2)}, u32[]{:S(2)}) collective-permute-start(bf16[400,128]{1,0:T(8,128)(2,1)S(1)} %get-tuple-element.64), channel_id=1, source_target_pairs={{0,8},{2,10},{4,12},{6,14},{8,0},{10,2},{12,4},{14,6},{16,24},{18,... | collective-permute-start | bytes 307208 | tf_op jit(solution)/shard_map/ppermute | solution.py:437
  8.7 10.5 %collective-permute-start = (bf16[400,128]{1,0:T(8,128)(2,1)S(1)}, bf16[400,128]{1,0:T(8,128)(2,1)S(1)}, u32[]{:S(2)}, u32[]{:S(2)}) collective-permute-start(bf16[400,128]{1,0:T(8,128)(2,1)S(1)} %get-tuple-element.56), channel_id=1, source_target_pairs={{0,10},{2,8},{4,14},{6,12},{8,2},{10,0},{12,6},{14,4},{16,26},{18,... | collective-permute-start | bytes 307208 | tf_op jit(solution)/shard_map/ppermute | solution.py:437
  10.1 9.1 %collective-permute-start.1 = (bf16[400,128]{1,0:T(8,128)(2,1)S(1)}, bf16[400,128]{1,0:T(8,128)(2,1)S(1)}, u32[]{:S(2)}, u32[]{:S(2)}) collective-permute-start(bf16[400,128]{1,0:T(8,128)(2,1)S(1)} %get-tuple-element.57), channel_id=1, source_target_pairs={{0,12},{2,14},{4,8},{6,10},{8,4},{10,6},{12,0},{14,2},{16,28},{18,... | collective-permute-start | bytes 307208 | tf_op jit(solution)/shard_map/ppermute | solution.py:437
  12.6 6.9 %collective-permute-start.2 = (bf16[400,128]{1,0:T(8,128)(2,1)S(1)}, bf16[400,128]{1,0:T(8,128)(2,1)S(1)}, u32[]{:S(2)}, u32[]{:S(2)}) collective-permute-start(bf16[400,128]{1,0:T(8,128)(2,1)S(1)} %get-tuple-element.58), channel_id=1, source_target_pairs={{0,14},{2,12},{4,10},{6,8},{8,6},{10,4},{12,2},{14,0},{16,30},{18,... | collective-permute-start | bytes 307208 | tf_op jit(solution)/shard_map/ppermute | solution.py:437
  22.5 18.8 %slice-start = ((s8[8388608]{0:T(1024)(128)(4,1)}), s8[4194304]{0:T(1024)(128)(4,1)S(1)}, s32[]{:S(2)}) async-start(s8[8388608]{0:T(1024)(128)(4,1)} %bitcast.7), calls=%async_computation.1 | async-start | bytes 8388608
  22.5 18.8 %slice-start.1 = ((s8[8388608]{0:T(1024)(128)(4,1)}), s8[4194304]{0:T(1024)(128)(4,1)S(1)}, s32[]{:S(2)}) async-start(s8[8388608]{0:T(1024)(128)(4,1)} %bitcast.7), calls=%async_computation.2 | async-start | bytes 8388608
  22.5 18.8 %copy-start = (bf16[128,2048]{1,0:T(8,128)(2,1)S(1)}, bf16[128,2048]{1,0:T(8,128)(2,1)}, u32[]{:S(2)}) copy-start(bf16[128,2048]{1,0:T(8,128)(2,1)} %gate_ref.1) | copy-start | bytes 1572868
  22.6 18.8 %copy-start.1 = (f32[128]{0:T(128)S(1)}, f32[128]{0:T(128)}, u32[]{:S(2)}) copy-start(f32[128]{0:T(128)} %param.14) | copy-start | bytes 1540
  22.6 6.8 %collective-permute-start.7 = (bf16[2,128,128]{2,1,0:T(8,128)(2,1)S(1)}, bf16[2,128,128]{2,1,0:T(8,128)(2,1)S(1)}, u32[]{:S(2)}, u32[]{:S(2)}) collective-permute-start(bf16[2,128,128]{2,1,0:T(8,128)(2,1)S(1)} %get-tuple-element.96), channel_id=1, source_target_pairs={{0,16},{2,18},{4,20},{6,22},{8,24},{10,26},{12,28},{14,30},{16,0},... | collective-permute-start | bytes 196616 | tf_op jit(solution)/shard_map/ppermute | solution.py:437
  42.6 1.6 %collective-permute-start.8 = (bf16[128,1024]{1,0:T(8,128)(2,1)S(1)}, bf16[128,1024]{1,0:T(8,128)(2,1)S(1)}, u32[]{:S(2)}, u32[]{:S(2)}) collective-permute-start(bf16[128,1024]{1,0:T(8,128)(2,1)S(1)} %get-tuple-element.106), channel_id=1, source_target_pairs={{0,1},{1,0},{2,3},{3,2},{4,5},{5,4},{6,7},{7,6},{8,9},{9,8},{10,11... | collective-permute-start | bytes 786440 | tf_op jit(solution)/shard_map/ppermute | solution.py:537

commit v8 on v7

--- a/solution.py
+++ b/solution.py
@@ -104,6 +104,11 @@
     return lax.rem(lax.axis_index("ctx"), group)
 
 
+def partner(group, n):
+    half = group // 2
+    return n ^ (half - 1) if n >= half else n
+
+
 def pack_kernel(key_hbm, value_hbm, scalars_ref, *refs):
     group = len(refs) - 2
     out_refs, (rows_ref, in_sems) = refs[:group], refs[group:]
@@ -113,7 +118,7 @@
     base = (1 + REP) * tokens
     arrivals = []
     for s in range(group):
-        j = place ^ s
+        j = place ^ partner(group, s)
         sources = [key_hbm.at[:, pl.ds(pl.multiple_of(j * DK, DK), DK)]] + [
             value_hbm.at[:, pl.ds(pl.multiple_of((j * REP + r) * DV, DV), DV)] for r in range(REP)
         ]
@@ -139,7 +144,9 @@
                 pick = pick + jnp.where((at >= 0) & (at < REP) & (col == wanted), 1.0, 0.0)
         return pick.astype(BF16)
 
-    picks = picked(target ^ place), picked(target)
+    half = group // 2
+    sent_to = jnp.where(target >= half, target ^ (half - 1), target)
+    picks = picked(sent_to ^ place), picked(target)
     pieces = jnp.concatenate(
         two_pieces(scalars_ref[0]) + two_pieces(scalars_ref[1]), axis=0
     )
@@ -298,7 +305,7 @@
     for i in range(blocks):
         following = []
         for r in range(REP):
-            at = (low ^ i) * REP + r
+            at = (low ^ i if own else low ^ i ^ (blocks - 1)) * REP + r
             decay = decays[at][0:1, :]
             if i == 0:
                 map_ref[at] = eye.astype(BF16)
@@ -358,7 +365,7 @@
         for r in range(REP):
             at = (s % half) * REP + r
             start = starts[r][0] if s < half else starts[r][1]
-            out_ref[place ^ s, r * DK : (r + 1) * DK, :] = (
+            out_ref[place ^ partner(group, s), r * DK : (r + 1) * DK, :] = (
                 before[at] + nn(maps[at], start)
             ).astype(BF16)
 
@@ -447,7 +454,7 @@
         scratch=[pltpu.SemaphoreType.DMA((group, 1 + REP))],
         specs=[any_space, any_space, vmem],
     )(key_proj, value_proj, jnp.stack([write_strength.T, log_decay.T]))
-    taken = [packed[0]] + [swapped(packed[s], s) for s in range(1, group)]
+    taken = [packed[0]] + [swapped(packed[s], partner(group, s)) for s in range(1, group)]
 
     extra = 1 if half >= 4 else 0
 

time: 45.2 us -> 47.1 us (1.042)
  waiting for transfers between devices: 1.09 us -> 3.67 us
  blocking collectives: 11.5 us -> 10.6 us
    ppermute x8, waiting for transfers between devices: 0.34 us -> 2.92 us  [swapped(): return lax.ppermute(array, 'ctx', [(i, i ^ distance) for i in range(n_ctx)])]
    all_to_all x1, blocking collectives: 11.5 us -> 10.6 us  [local(): lax.all_to_all(states, 'ctx', 0, 0, axis_index_groups=groups, tiled=True)]
  transfers between devices with their start and end apart: 9 -> 9, of which waited for: 2 -> 2; matrix products, arithmetic and copies ran while one was open for 0% -> 0% of each run, Pallas kernels for 23% -> 22%
where the time goes in v8:
time: 47.1 us; the launch traced here: 46.8 us
  Pallas kernels  16.3 us (35%)
  starting transfers between devices  14.6 us (31%)
  blocking collectives  10.6 us (23%)
  waiting for transfers between devices  3.67 us (8%)
  other arithmetic  1.49 us (3%)
    ppermute x8, starting transfers between devices, swapped(): return lax.ppermute(array, 'ctx', [(i, i ^ distance) for i in range(n_ctx)])  14.5 us
    all_to_all x1, blocking collectives, local(): lax.all_to_all(states, 'ctx', 0, 0, axis_index_groups=groups, tiled=True)  10.6 us
    pallas_call x2, Pallas kernels, half_states(): kernel(functools.partial(half_kernel, blocks=half, extra=extra, group=gro...  6.23 us
    pallas_call x2, Pallas kernels, inside_part(): kernel(functools.partial(inside_kernel, first=start, base_bits=base_bits)...  6.21 us
    ppermute x8, waiting for transfers between devices, swapped(): return lax.ppermute(array, 'ctx', [(i, i ^ distance) for i in range(n_ctx)])  2.92 us
    pallas_call x1, Pallas kernels, local(): kernel(pack_kernel, (shape((packed_rows, DK), BF16),) * group + (shape((g...  1.42 us
    pallas_call x1, Pallas kernels, local(): kernel(functools.partial(mixed_kernel, shifts=n_head), (shape((tokens, he...  1.24 us
  transfers between devices with their start and end apart: 9, of which 2 were waited for; matrix products, arithmetic and copies ran while one was open for 0% of the time, Pallas kernels for 22%

profile of v8, /device:TPU:0, one launch (start us, length us, event | category | flops | bytes accessed | tf_op | source)
XLA Modules:
  0.0 46.8 jit_solution(15580039651944591357)
XLA Ops:
  0.0 0.7 %pad_maximum_fusion.scalars_ref = f32[2,16,128]{2,1,0:T(8,128)S(1)} fusion(f32[1,16,128]{2,1,0:T(8,128)} %bitcast.10, f32[1,16,128]{2,1,0:T(8,128)} %bitcast.11), kind=kLoop, calls=%fused_computation.1 | loop fusion | flops 4096 | bytes 32768 | tf_op jit(solution)/shard_map/stack | solution.py:456
  0.7 1.4 %pack.1 = (bf16[400,128]{1,0:T(8,128)(2,1)S(1)}, bf16[400,128]{1,0:T(8,128)(2,1)S(1)}, bf16[400,128]{1,0:T(8,128)(2,1)S(1)}, bf16[400,128]{1,0:T(8,128)(2,1)S(1)...) custom-call(bf16[128,1024]{1,0:T(8,128)(2,1)} %key_ref.3, ...), custom_call_target="tpu_custom_call" | custom-call | flops 2000000000 | bytes 1048576 | tf_op jit(solution)/shard_map/pack/pallas_call | solution.py:448
  2.1 3.0 %collective-permute-start.3 = (bf16[400,128]{1,0:T(8,128)(2,1)S(1)}, bf16[400,128]{1,0:T(8,128)(2,1)S(1)}, u32[]{:S(2)}, u32[]{:S(2)}) collective-permute-start(bf16[400,128]{1,0:T(8,128)(2,1)S(1)} %get-tuple-element.61), channel_id=1, source_target_pairs={{0,2},{2,0},{4,6},{6,4},{8,10},{10,8},{12,14},{14,12},{16,18},{18,... | collective-permute-start | bytes 307208 | tf_op jit(solution)/shard_map/ppermute | solution.py:444
  5.2 1.5 %collective-permute-start.4 = (bf16[400,128]{1,0:T(8,128)(2,1)S(1)}, bf16[400,128]{1,0:T(8,128)(2,1)S(1)}, u32[]{:S(2)}, u32[]{:S(2)}) collective-permute-start(bf16[400,128]{1,0:T(8,128)(2,1)S(1)} %get-tuple-element.62), channel_id=1, source_target_pairs={{0,4},{2,6},{4,0},{6,2},{8,12},{10,14},{12,8},{14,10},{16,20},{18,... | collective-permute-start | bytes 307208 | tf_op jit(solution)/shard_map/ppermute | solution.py:444
  6.7 0.0 collective-permute-start.5
  6.7 3.9 %collective-permute-start.6 = (bf16[400,128]{1,0:T(8,128)(2,1)S(1)}, bf16[400,128]{1,0:T(8,128)(2,1)S(1)}, u32[]{:S(2)}, u32[]{:S(2)}) collective-permute-start(bf16[400,128]{1,0:T(8,128)(2,1)S(1)} %get-tuple-element.64), channel_id=1, source_target_pairs={{0,14},{2,12},{4,10},{6,8},{8,6},{10,4},{12,2},{14,0},{16,30},{18,... | collective-permute-start | bytes 307208 | tf_op jit(solution)/shard_map/ppermute | solution.py:444
  10.6 0.4 collective-permute-start
  11.0 0.0 collective-permute-done.3.refs_1_
  11.0 1.5 %collective-permute-start.1 = (bf16[400,128]{1,0:T(8,128)(2,1)S(1)}, bf16[400,128]{1,0:T(8,128)(2,1)S(1)}, u32[]{:S(2)}, u32[]{:S(2)}) collective-permute-start(bf16[400,128]{1,0:T(8,128)(2,1)S(1)} %get-tuple-element.57), channel_id=1, source_target_pairs={{0,10},{2,8},{4,14},{6,12},{8,2},{10,0},{12,6},{14,4},{16,26},{18,... | collective-permute-start | bytes 307208 | tf_op jit(solution)/shard_map/ppermute | solution.py:444
  12.6 2.9 %collective-permute-done.4.refs_2_ = bf16[400,128]{1,0:T(8,128)(2,1)S(1)} collective-permute-done((bf16[400,128]{1,0:T(8,128)(2,1)S(1)}, bf16[400,128]{1,0:T(8,128)(2,1)S(1)}, u32[]{:S(2)}, u32[]{:S(2)}) %collective-permute-start.4) | collective-permute-done | bytes 102432 | tf_op jit(solution)/shard_map/ppermute | solution.py:444
  15.5 1.4 %collective-permute-start.2 = (bf16[400,128]{1,0:T(8,128)(2,1)S(1)}, bf16[400,128]{1,0:T(8,128)(2,1)S(1)}, u32[]{:S(2)}, u32[]{:S(2)}) collective-permute-start(bf16[400,128]{1,0:T(8,128)(2,1)S(1)} %get-tuple-element.58), channel_id=1, source_target_pairs={{0,8},{2,10},{4,12},{6,14},{8,0},{10,2},{12,4},{14,6},{16,24},{18,... | collective-permute-start | bytes 307208 | tf_op jit(solution)/shard_map/ppermute | solution.py:444
  16.9 0.0 collective-permute-done.5.refs_3_
  16.9 0.0 collective-permute-done.6.refs_4_
  16.9 3.3 %own_half.1 = (f32[8,128,128]{2,1,0:T(8,128)S(1)}, bf16[8,128,128]{2,1,0:T(8,128)(2,1)S(1)}, f32[2,128,128]{2,1,0:T(8,128)S(1)}, f32[2,128,128]{2,1,0:T(8,128)S(...) custom-call(bf16[400,128]{1,0:T(8,128)(2,1)S(1)} %get-tuple-element.60.refs_0_, ...), custom_call_target="tpu_custom_call" | custom-call | flops 3500000000 | bytes 1048576 | tf_op jit(solution)/shard_map/own_half/pallas_call | solution.py:468
  20.2 2.1 %inside.2 = (bf16[4,128,128]{2,1,0:T(8,128)(2,1)S(1)}, bf16[4,128,128]{2,1,0:T(8,128)(2,1)S(1)}) custom-call(bf16[128,1024]{1,0:T(8,128)(2,1)S(1)} %copy-done.4, bf16[128,1024]{1,0:T(8,128)(2,1)S(1)} %copy-done.3, bf16[128,2048]{1,0:T(8,128)(2,1)S(1)} %copy-done.2, bf16[128,128]{1,0:T(8,128)(2,1)S(1)} %get-tuple-element.97.rows_ref), custom_call_target="tpu_custom_call" | custom-call | flops 2300000000 | bytes 1048576 | tf_op jit(solution)/shard_map/inside/pallas_call | solution.py:494
  22.3 0.0 collective-permute-done.refs_0_
  22.4 0.0 collective-permute-done.1.refs_1_
  22.4 0.0 collective-permute-done.2.refs_2_
  22.4 2.9 %other_half.1 = (f32[8,128,128]{2,1,0:T(8,128)S(1)}, bf16[8,128,128]{2,1,0:T(8,128)(2,1)S(1)}, f32[2,128,128]{2,1,0:T(8,128)S(1)}, f32[2,128,128]{2,1,0:T(8,128)S(1)}, bf16[2,128,128]{2,1,0:T(8,128)(2,1)S(1)}) custom-call(bf16[400,128]{1,0:T(8,128)(2,1)S(1)} %collective-permute-done.refs_0_, bf16[400,128]{1,0:T(8,128)(2,1)S(1)} %collective-permute-done.1.refs_1_, ...), custom_call_target="tpu_custom_call" | custom-call | flops 3500000000 | bytes 1048576 | tf_op jit(solution)/shard_map/other_half/pallas_call | solution.py:468
  25.3 0.0 slice-start
  25.3 0.0 slice-start.1
  25.3 0.0 copy-start
  25.3 0.0 copy-start.1
  25.4 2.7 %collective-permute-start.7 = (bf16[2,128,128]{2,1,0:T(8,128)(2,1)S(1)}, bf16[2,128,128]{2,1,0:T(8,128)(2,1)S(1)}, u32[]{:S(2)}, u32[]{:S(2)}) collective-permute-start(bf16[2,128,128]{2,1,0:T(8,128)(2,1)S(1)} %get-tuple-element.96), channel_id=1, source_target_pairs={{0,16},{2,18},{4,20},{6,22},{8,24},{10,26},{12,28},{14,30},{16,0},... | collective-permute-start | bytes 196616 | tf_op jit(solution)/shard_map/ppermute | solution.py:444
  28.0 4.1 %inside.3 = (bf16[12,128,128]{2,1,0:T(8,128)(2,1)S(1)}, bf16[12,128,128]{2,1,0:T(8,128)(2,1)S(1)}) custom-call(bf16[128,1024]{1,0:T(8,128)(2,1)S(1)} %copy-done.4, bf16[128,1024]{1,0:T(8,128)(2,1)S(1)} %copy-done.3, bf16[128,2048]{1,0:T(8,128)(2,1)S(1)} %copy-done.2, bf16[128,128]{1,0:T(8,128)(2,1)S(1)} %get-tuple-element.97.rows_ref), custom_call_target="tpu_custom_call" | custom-call | flops 5000000000 | bytes 1048576 | tf_op jit(solution)/shard_map/inside/pallas_call | solution.py:494
  32.1 0.5 carry.1
  32.6 10.6 %all_to_all.5.state_ref = bf16[8,256,128]{2,1,0:T(8,128)(2,1)S(1)} all-to-all(bf16[8,256,128]{2,1,0:T(8,128)(2,1)S(1)} %carry.1), channel_id=1, replica_groups={{0,2,4,6,8,10,12,14},{16,18,20,22,24,26,28,30},{1,3,5,7,9,11,13,15},{17..., dimensions={0} | all-to-all | bytes 1048576 | tf_op jit(solution)/shard_map/all_to_all | solution.py:534
  43.2 1.2 %mixed.1 = (bf16[128,2048]{1,0:T(8,128)(2,1)S(1)}, bf16[128,1024]{1,0:T(8,128)(2,1)S(1)}) custom-call(bf16[8,256,128]{2,1,0:T(8,128)(2,1)S(1)} %all_to_all.5.state_ref, bf16[4,128,128]{2,1,0:T(8,128)(2,1)S(1)} %get-tuple-element.101.first_inside, bf16[4,128,128]{2,1,0:T(8,128)(2,1)S(1)} %get-tuple-element.102.first_window, ...), custom_call_target="tpu_custom_call" | custom-call | flops 2000000000 | bytes 1048576 | tf_op jit(solution)/shard_map/mixed/pallas_call | solution.py:536
  44.4 0.1 collective-permute-start.8
  44.5 0.8 %own_columns.1 = bf16[128,1024]{1,0:T(8,128)(2,1)S(1)} custom-call(bf16[128,2048]{1,0:T(8,128)(2,1)S(1)} %get-tuple-element.105.mixed_ref, bf16[2048,2048]{1,0:T(8,128)(2,1)S(1)} %bitcast.8), custom_call_target="tpu_custom_call" | custom-call | flops 1000000000 | bytes 1048576 | tf_op jit(solution)/shard_map/own_columns/pallas_call | solution.py:547
  45.3 0.8 %collective-permute-done.8 = bf16[128,1024]{1,0:T(8,128)(2,1)S(1)} collective-permute-done((bf16[128,1024]{1,0:T(8,128)(2,1)S(1)}, bf16[128,1024]{1,0:T(8,128)(2,1)S(1)}, u32[]{:S(2)}, u32[]{:S(2)}) %collective-permute-start.8) | collective-permute-done | bytes 262176 | tf_op jit(solution)/shard_map/ppermute | solution.py:544
  46.0 0.8 %add_convert_fusion = bf16[128,1024]{1,0:T(8,128)(2,1)} fusion(bf16[128,1024]{1,0:T(8,128)(2,1)S(1)} %collective-permute-done.8, bf16[128,1024]{1,0:T(8,128)(2,1)S(1)} %own_columns.1), kind=kLoop, calls=%fused_computation | loop fusion | flops 524288 | bytes 786432 | tf_op jit(solution)/shard_map/convert_element_type | solution.py:552
  (12 shorter events, 0.0 us)
Async XLA Ops:
  0.7 19.5 %copy-start.2 = (bf16[128,2048]{1,0:T(8,128)(2,1)S(1)}, bf16[128,2048]{1,0:T(8,128)(2,1)}, u32[]{:S(2)}) copy-start(bf16[128,2048]{1,0:T(8,128)(2,1)} %value_ref.3) | copy-start | bytes 1572868
  0.7 19.5 %copy-start.3 = (bf16[128,1024]{1,0:T(8,128)(2,1)S(1)}, bf16[128,1024]{1,0:T(8,128)(2,1)}, u32[]{:S(2)}) copy-start(bf16[128,1024]{1,0:T(8,128)(2,1)} %key_ref.3) | copy-start | bytes 786436
  0.7 19.5 %copy-start.4 = (bf16[128,1024]{1,0:T(8,128)(2,1)S(1)}, bf16[128,1024]{1,0:T(8,128)(2,1)}, u32[]{:S(2)}) copy-start(bf16[128,1024]{1,0:T(8,128)(2,1)} %query_ref.3) | copy-start | bytes 786436
  2.1 8.9 %collective-permute-start.3 = (bf16[400,128]{1,0:T(8,128)(2,1)S(1)}, bf16[400,128]{1,0:T(8,128)(2,1)S(1)}, u32[]{:S(2)}, u32[]{:S(2)}) collective-permute-start(bf16[400,128]{1,0:T(8,128)(2,1)S(1)} %get-tuple-element.61), channel_id=1, source_target_pairs={{0,2},{2,0},{4,6},{6,4},{8,10},{10,8},{12,14},{14,12},{16,18},{18,... | collective-permute-start | bytes 307208 | tf_op jit(solution)/shard_map/ppermute | solution.py:444
  5.2 10.3 %collective-permute-start.4 = (bf16[400,128]{1,0:T(8,128)(2,1)S(1)}, bf16[400,128]{1,0:T(8,128)(2,1)S(1)}, u32[]{:S(2)}, u32[]{:S(2)}) collective-permute-start(bf16[400,128]{1,0:T(8,128)(2,1)S(1)} %get-tuple-element.62), channel_id=1, source_target_pairs={{0,4},{2,6},{4,0},{6,2},{8,12},{10,14},{12,8},{14,10},{16,20},{18,... | collective-permute-start | bytes 307208 | tf_op jit(solution)/shard_map/ppermute | solution.py:444
  6.7 10.2 %collective-permute-start.5 = (bf16[400,128]{1,0:T(8,128)(2,1)S(1)}, bf16[400,128]{1,0:T(8,128)(2,1)S(1)}, u32[]{:S(2)}, u32[]{:S(2)}) collective-permute-start(bf16[400,128]{1,0:T(8,128)(2,1)S(1)} %get-tuple-element.63), channel_id=1, source_target_pairs={{0,6},{2,4},{4,2},{6,0},{8,14},{10,12},{12,10},{14,8},{16,22},{18,... | collective-permute-start | bytes 307208 | tf_op jit(solution)/shard_map/ppermute | solution.py:444
  6.7 10.2 %collective-permute-start.6 = (bf16[400,128]{1,0:T(8,128)(2,1)S(1)}, bf16[400,128]{1,0:T(8,128)(2,1)S(1)}, u32[]{:S(2)}, u32[]{:S(2)}) collective-permute-start(bf16[400,128]{1,0:T(8,128)(2,1)S(1)} %get-tuple-element.64), channel_id=1, source_target_pairs={{0,14},{2,12},{4,10},{6,8},{8,6},{10,4},{12,2},{14,0},{16,30},{18,... | collective-permute-start | bytes 307208 | tf_op jit(solution)/shard_map/ppermute | solution.py:444
  10.6 11.7 %collective-permute-start = (bf16[400,128]{1,0:T(8,128)(2,1)S(1)}, bf16[400,128]{1,0:T(8,128)(2,1)S(1)}, u32[]{:S(2)}, u32[]{:S(2)}) collective-permute-start(bf16[400,128]{1,0:T(8,128)(2,1)S(1)} %get-tuple-element.56), channel_id=1, source_target_pairs={{0,12},{2,14},{4,8},{6,10},{8,4},{10,6},{12,0},{14,2},{16,28},{18,... | collective-permute-start | bytes 307208 | tf_op jit(solution)/shard_map/ppermute | solution.py:444
  11.0 11.4 %collective-permute-start.1 = (bf16[400,128]{1,0:T(8,128)(2,1)S(1)}, bf16[400,128]{1,0:T(8,128)(2,1)S(1)}, u32[]{:S(2)}, u32[]{:S(2)}) collective-permute-start(bf16[400,128]{1,0:T(8,128)(2,1)S(1)} %get-tuple-element.57), channel_id=1, source_target_pairs={{0,10},{2,8},{4,14},{6,12},{8,2},{10,0},{12,6},{14,4},{16,26},{18,... | collective-permute-start | bytes 307208 | tf_op jit(solution)/shard_map/ppermute | solution.py:444
  15.5 6.9 %collective-permute-start.2 = (bf16[400,128]{1,0:T(8,128)(2,1)S(1)}, bf16[400,128]{1,0:T(8,128)(2,1)S(1)}, u32[]{:S(2)}, u32[]{:S(2)}) collective-permute-start(bf16[400,128]{1,0:T(8,128)(2,1)S(1)} %get-tuple-element.58), channel_id=1, source_target_pairs={{0,8},{2,10},{4,12},{6,14},{8,0},{10,2},{12,4},{14,6},{16,24},{18,... | collective-permute-start | bytes 307208 | tf_op jit(solution)/shard_map/ppermute | solution.py:444
  25.3 17.9 %slice-start = ((s8[8388608]{0:T(1024)(128)(4,1)}), s8[4194304]{0:T(1024)(128)(4,1)S(1)}, s32[]{:S(2)}) async-start(s8[8388608]{0:T(1024)(128)(4,1)} %bitcast.7), calls=%async_computation.1 | async-start | bytes 8388608
  25.3 17.9 %slice-start.1 = ((s8[8388608]{0:T(1024)(128)(4,1)}), s8[4194304]{0:T(1024)(128)(4,1)S(1)}, s32[]{:S(2)}) async-start(s8[8388608]{0:T(1024)(128)(4,1)} %bitcast.7), calls=%async_computation.2 | async-start | bytes 8388608
  25.3 17.8 %copy-start = (bf16[128,2048]{1,0:T(8,128)(2,1)S(1)}, bf16[128,2048]{1,0:T(8,128)(2,1)}, u32[]{:S(2)}) copy-start(bf16[128,2048]{1,0:T(8,128)(2,1)} %gate_ref.1) | copy-start | bytes 1572868
  25.3 17.8 %copy-start.1 = (f32[128]{0:T(128)S(1)}, f32[128]{0:T(128)}, u32[]{:S(2)}) copy-start(f32[128]{0:T(128)} %param.14) | copy-start | bytes 1540
  25.4 6.8 %collective-permute-start.7 = (bf16[2,128,128]{2,1,0:T(8,128)(2,1)S(1)}, bf16[2,128,128]{2,1,0:T(8,128)(2,1)S(1)}, u32[]{:S(2)}, u32[]{:S(2)}) collective-permute-start(bf16[2,128,128]{2,1,0:T(8,128)(2,1)S(1)} %get-tuple-element.96), channel_id=1, source_target_pairs={{0,16},{2,18},{4,20},{6,22},{8,24},{10,26},{12,28},{14,30},{16,0},... | collective-permute-start | bytes 196616 | tf_op jit(solution)/shard_map/ppermute | solution.py:444
  44.4 1.6 %collective-permute-start.8 = (bf16[128,1024]{1,0:T(8,128)(2,1)S(1)}, bf16[128,1024]{1,0:T(8,128)(2,1)S(1)}, u32[]{:S(2)}, u32[]{:S(2)}) collective-permute-start(bf16[128,1024]{1,0:T(8,128)(2,1)S(1)} %get-tuple-element.106), channel_id=1, source_target_pairs={{0,1},{1,0},{2,3},{3,2},{4,5},{5,4},{6,7},{7,6},{8,9},{9,8},{10,11... | collective-permute-start | bytes 786440 | tf_op jit(solution)/shard_map/ppermute | solution.py:544

commit v9 on v7

--- a/solution.py
+++ b/solution.py
@@ -518,7 +518,7 @@
         carried = jnp.zeros((REP, DK, DV), BF16)
 
     rows, end = lax.optimization_barrier((rows, end))
-    second = inside_part(early, group - early, rows, 5, 3)
+    second = inside_part(early, group - early, rows, 5, 4)
     carried, second = lax.optimization_barrier((carried, second))
     states = kernel(
         carry_kernel, shape((group, REP * DK, DV), BF16), "carry", 8, 0.6

time: 45.2 us -> 45.2 us (level)
  no operation moved by 1% of the time
where the time goes in v9:
time: 45.2 us; the launch traced here: 44.9 us
  Pallas kernels  16.3 us (36%)
  starting transfers between devices  14.3 us (32%)
  blocking collectives  11.5 us (25%)
  other arithmetic  1.49 us (3%)
  waiting for transfers between devices  1.09 us (2%)
    ppermute x8, starting transfers between devices, swapped(): return lax.ppermute(array, 'ctx', [(i, i ^ distance) for i in range(n_ctx)])  14.3 us
    all_to_all x1, blocking collectives, local(): lax.all_to_all(states, 'ctx', 0, 0, axis_index_groups=groups, tiled=True)  11.5 us
    pallas_call x2, Pallas kernels, half_states(): kernel(functools.partial(half_kernel, blocks=half, extra=extra, group=gro...  6.26 us
    pallas_call x2, Pallas kernels, inside_part(): kernel(functools.partial(inside_kernel, first=start, base_bits=base_bits)...  6.14 us
    pallas_call x1, Pallas kernels, local(): kernel(pack_kernel, (shape((packed_rows, DK), BF16),) * group + (shape((g...  1.41 us
    pallas_call x1, Pallas kernels, local(): kernel(functools.partial(mixed_kernel, shifts=n_head), (shape((tokens, he...  1.24 us
  transfers between devices with their start and end apart: 9, of which 2 were waited for; matrix products, arithmetic and copies ran while one was open for 0% of the time, Pallas kernels for 23%

profile of v9, /device:TPU:0, one launch (start us, length us, event | category | flops | bytes accessed | tf_op | source)
XLA Modules:
  0.0 44.9 jit_solution(12094463640810076862)
XLA Ops:
  0.0 0.7 %pad_maximum_fusion.scalars_ref = f32[2,16,128]{2,1,0:T(8,128)S(1)} fusion(f32[1,16,128]{2,1,0:T(8,128)} %bitcast.10, f32[1,16,128]{2,1,0:T(8,128)} %bitcast.11), kind=kLoop, calls=%fused_computation.1 | loop fusion | flops 4096 | bytes 32768 | tf_op jit(solution)/shard_map/stack | solution.py:449
  0.7 1.4 %pack.1 = (bf16[400,128]{1,0:T(8,128)(2,1)S(1)}, bf16[400,128]{1,0:T(8,128)(2,1)S(1)}, bf16[400,128]{1,0:T(8,128)(2,1)S(1)}, bf16[400,128]{1,0:T(8,128)(2,1)S(1)...) custom-call(bf16[128,1024]{1,0:T(8,128)(2,1)} %key_ref.3, ...), custom_call_target="tpu_custom_call" | custom-call | flops 2000000000 | bytes 1048576 | tf_op jit(solution)/shard_map/pack/pallas_call | solution.py:441
  2.1 3.0 %collective-permute-start.3 = (bf16[400,128]{1,0:T(8,128)(2,1)S(1)}, bf16[400,128]{1,0:T(8,128)(2,1)S(1)}, u32[]{:S(2)}, u32[]{:S(2)}) collective-permute-start(bf16[400,128]{1,0:T(8,128)(2,1)S(1)} %get-tuple-element.61), channel_id=1, source_target_pairs={{0,2},{2,0},{4,6},{6,4},{8,10},{10,8},{12,14},{14,12},{16,18},{18,... | collective-permute-start | bytes 307208 | tf_op jit(solution)/shard_map/ppermute | solution.py:437
  5.1 1.5 %collective-permute-start.4 = (bf16[400,128]{1,0:T(8,128)(2,1)S(1)}, bf16[400,128]{1,0:T(8,128)(2,1)S(1)}, u32[]{:S(2)}, u32[]{:S(2)}) collective-permute-start(bf16[400,128]{1,0:T(8,128)(2,1)S(1)} %get-tuple-element.62), channel_id=1, source_target_pairs={{0,4},{2,6},{4,0},{6,2},{8,12},{10,14},{12,8},{14,10},{16,20},{18,... | collective-permute-start | bytes 307208 | tf_op jit(solution)/shard_map/ppermute | solution.py:437
  6.7 0.0 collective-permute-start.5
  6.7 2.0 %collective-permute-start.6 = (bf16[400,128]{1,0:T(8,128)(2,1)S(1)}, bf16[400,128]{1,0:T(8,128)(2,1)S(1)}, u32[]{:S(2)}, u32[]{:S(2)}) collective-permute-start(bf16[400,128]{1,0:T(8,128)(2,1)S(1)} %get-tuple-element.64), channel_id=1, source_target_pairs={{0,8},{2,10},{4,12},{6,14},{8,0},{10,2},{12,4},{14,6},{16,24},{18,... | collective-permute-start | bytes 307208 | tf_op jit(solution)/shard_map/ppermute | solution.py:437
  8.7 1.4 %collective-permute-start = (bf16[400,128]{1,0:T(8,128)(2,1)S(1)}, bf16[400,128]{1,0:T(8,128)(2,1)S(1)}, u32[]{:S(2)}, u32[]{:S(2)}) collective-permute-start(bf16[400,128]{1,0:T(8,128)(2,1)S(1)} %get-tuple-element.56), channel_id=1, source_target_pairs={{0,10},{2,8},{4,14},{6,12},{8,2},{10,0},{12,6},{14,4},{16,26},{18,... | collective-permute-start | bytes 307208 | tf_op jit(solution)/shard_map/ppermute | solution.py:437
  10.1 0.0 collective-permute-done.3.refs_1_
  10.1 2.5 %collective-permute-start.1 = (bf16[400,128]{1,0:T(8,128)(2,1)S(1)}, bf16[400,128]{1,0:T(8,128)(2,1)S(1)}, u32[]{:S(2)}, u32[]{:S(2)}) collective-permute-start(bf16[400,128]{1,0:T(8,128)(2,1)S(1)} %get-tuple-element.57), channel_id=1, source_target_pairs={{0,12},{2,14},{4,8},{6,10},{8,4},{10,6},{12,0},{14,2},{16,28},{18,... | collective-permute-start | bytes 307208 | tf_op jit(solution)/shard_map/ppermute | solution.py:437
  12.6 0.0 collective-permute-done.4.refs_2_
  12.6 1.1 %collective-permute-start.2 = (bf16[400,128]{1,0:T(8,128)(2,1)S(1)}, bf16[400,128]{1,0:T(8,128)(2,1)S(1)}, u32[]{:S(2)}, u32[]{:S(2)}) collective-permute-start(bf16[400,128]{1,0:T(8,128)(2,1)S(1)} %get-tuple-element.58), channel_id=1, source_target_pairs={{0,14},{2,12},{4,10},{6,8},{8,6},{10,4},{12,2},{14,0},{16,30},{18,... | collective-permute-start | bytes 307208 | tf_op jit(solution)/shard_map/ppermute | solution.py:437
  13.7 0.0 collective-permute-done.5.refs_3_
  13.8 0.0 collective-permute-done.6.refs_4_
  13.8 3.3 %own_half.1 = (f32[8,128,128]{2,1,0:T(8,128)S(1)}, bf16[8,128,128]{2,1,0:T(8,128)(2,1)S(1)}, f32[2,128,128]{2,1,0:T(8,128)S(1)}, f32[2,128,128]{2,1,0:T(8,128)S(...) custom-call(bf16[400,128]{1,0:T(8,128)(2,1)S(1)} %get-tuple-element.60.refs_0_, ...), custom_call_target="tpu_custom_call" | custom-call | flops 3500000000 | bytes 1048576 | tf_op jit(solution)/shard_map/own_half/pallas_call | solution.py:461
  17.1 2.1 %inside.2 = (bf16[4,128,128]{2,1,0:T(8,128)(2,1)S(1)}, bf16[4,128,128]{2,1,0:T(8,128)(2,1)S(1)}) custom-call(bf16[128,1024]{1,0:T(8,128)(2,1)S(1)} %copy-done.4, bf16[128,1024]{1,0:T(8,128)(2,1)S(1)} %copy-done.3, bf16[128,2048]{1,0:T(8,128)(2,1)S(1)} %copy-done.2, bf16[128,128]{1,0:T(8,128)(2,1)S(1)} %get-tuple-element.97.rows_ref), custom_call_target="tpu_custom_call" | custom-call | flops 2300000000 | bytes 1048576 | tf_op jit(solution)/shard_map/inside/pallas_call | solution.py:487
  19.2 0.0 collective-permute-done.refs_0_
  19.2 0.0 collective-permute-done.1.refs_1_
  19.2 0.3 collective-permute-done.2.refs_2_
  19.6 2.9 %other_half.1 = (f32[8,128,128]{2,1,0:T(8,128)S(1)}, bf16[8,128,128]{2,1,0:T(8,128)(2,1)S(1)}, f32[2,128,128]{2,1,0:T(8,128)S(1)}, f32[2,128,128]{2,1,0:T(8,128)S(1)}, bf16[2,128,128]{2,1,0:T(8,128)(2,1)S(1)}) custom-call(bf16[400,128]{1,0:T(8,128)(2,1)S(1)} %collective-permute-done.refs_0_, bf16[400,128]{1,0:T(8,128)(2,1)S(1)} %collective-permute-done.1.refs_1_, ...), custom_call_target="tpu_custom_call" | custom-call | flops 3500000000 | bytes 1048576 | tf_op jit(solution)/shard_map/other_half/pallas_call | solution.py:461
  22.5 0.0 slice-start
  22.5 0.0 slice-start.1
  22.5 0.0 copy-start
  22.6 0.0 copy-start.1
  22.6 2.7 %collective-permute-start.7 = (bf16[2,128,128]{2,1,0:T(8,128)(2,1)S(1)}, bf16[2,128,128]{2,1,0:T(8,128)(2,1)S(1)}, u32[]{:S(2)}, u32[]{:S(2)}) collective-permute-start(bf16[2,128,128]{2,1,0:T(8,128)(2,1)S(1)} %get-tuple-element.96), channel_id=1, source_target_pairs={{0,16},{2,18},{4,20},{6,22},{8,24},{10,26},{12,28},{14,30},{16,0},... | collective-permute-start | bytes 196616 | tf_op jit(solution)/shard_map/ppermute | solution.py:437
  25.2 4.0 %inside.3 = (bf16[12,128,128]{2,1,0:T(8,128)(2,1)S(1)}, bf16[12,128,128]{2,1,0:T(8,128)(2,1)S(1)}) custom-call(bf16[128,1024]{1,0:T(8,128)(2,1)S(1)} %copy-done.4, bf16[128,1024]{1,0:T(8,128)(2,1)S(1)} %copy-done.3, bf16[128,2048]{1,0:T(8,128)(2,1)S(1)} %copy-done.2, bf16[128,128]{1,0:T(8,128)(2,1)S(1)} %get-tuple-element.97.rows_ref), custom_call_target="tpu_custom_call" | custom-call | flops 5000000000 | bytes 1048576 | tf_op jit(solution)/shard_map/inside/pallas_call | solution.py:487
  29.3 0.5 %carry.1 = bf16[8,256,128]{2,1,0:T(8,128)(2,1)S(1)} custom-call(f32[8,128,128]{2,1,0:T(8,128)S(1)} %get-tuple-element.82.own_before, bf16[8,128,128]{2,1,0:T(8,128)(2,1)S(1)} %get-tuple-element.83.own_maps, f32[2,128,128]{2,1,0:T(8,128)S(1)} %get-tuple-element.84.refs_3_.own_end, f32[2,128,128]{2,1,0:T(8,128)S(1)} %get-tuple-element.85.refs_4_.own_map, ...), custom_call_target="tpu_custom_call" | custom-call | flops 600000000 | bytes 1048576 | tf_op jit(solution)/shard_map/carry/pallas_call | solution.py:523
  29.7 11.5 %all_to_all.5.state_ref = bf16[8,256,128]{2,1,0:T(8,128)(2,1)S(1)} all-to-all(bf16[8,256,128]{2,1,0:T(8,128)(2,1)S(1)} %carry.1), channel_id=1, replica_groups={{0,2,4,6,8,10,12,14},{16,18,20,22,24,26,28,30},{1,3,5,7,9,11,13,15},{17..., dimensions={0} | all-to-all | bytes 1048576 | tf_op jit(solution)/shard_map/all_to_all | solution.py:527
  41.3 1.2 %mixed.1 = (bf16[128,2048]{1,0:T(8,128)(2,1)S(1)}, bf16[128,1024]{1,0:T(8,128)(2,1)S(1)}) custom-call(bf16[8,256,128]{2,1,0:T(8,128)(2,1)S(1)} %all_to_all.5.state_ref, bf16[4,128,128]{2,1,0:T(8,128)(2,1)S(1)} %get-tuple-element.101.first_inside, bf16[4,128,128]{2,1,0:T(8,128)(2,1)S(1)} %get-tuple-element.102.first_window, ...), custom_call_target="tpu_custom_call" | custom-call | flops 2000000000 | bytes 1048576 | tf_op jit(solution)/shard_map/mixed/pallas_call | solution.py:529
  42.5 0.1 collective-permute-start.8
  42.6 0.8 %own_columns.1 = bf16[128,1024]{1,0:T(8,128)(2,1)S(1)} custom-call(bf16[128,2048]{1,0:T(8,128)(2,1)S(1)} %get-tuple-element.105.mixed_ref, bf16[2048,2048]{1,0:T(8,128)(2,1)S(1)} %bitcast.8), custom_call_target="tpu_custom_call" | custom-call | flops 1000000000 | bytes 1048576 | tf_op jit(solution)/shard_map/own_columns/pallas_call | solution.py:540
  43.4 0.8 %collective-permute-done.8 = bf16[128,1024]{1,0:T(8,128)(2,1)S(1)} collective-permute-done((bf16[128,1024]{1,0:T(8,128)(2,1)S(1)}, bf16[128,1024]{1,0:T(8,128)(2,1)S(1)}, u32[]{:S(2)}, u32[]{:S(2)}) %collective-permute-start.8) | collective-permute-done | bytes 262176 | tf_op jit(solution)/shard_map/ppermute | solution.py:537
  44.1 0.8 %add_convert_fusion = bf16[128,1024]{1,0:T(8,128)(2,1)} fusion(bf16[128,1024]{1,0:T(8,128)(2,1)S(1)} %collective-permute-done.8, bf16[128,1024]{1,0:T(8,128)(2,1)S(1)} %own_columns.1), kind=kLoop, calls=%fused_computation | loop fusion | flops 524288 | bytes 786432 | tf_op jit(solution)/shard_map/convert_element_type | solution.py:545
  (12 shorter events, 0.0 us)
Async XLA Ops:
  0.7 16.4 %copy-start.2 = (bf16[128,2048]{1,0:T(8,128)(2,1)S(1)}, bf16[128,2048]{1,0:T(8,128)(2,1)}, u32[]{:S(2)}) copy-start(bf16[128,2048]{1,0:T(8,128)(2,1)} %value_ref.3) | copy-start | bytes 1572868
  0.7 16.4 %copy-start.3 = (bf16[128,1024]{1,0:T(8,128)(2,1)S(1)}, bf16[128,1024]{1,0:T(8,128)(2,1)}, u32[]{:S(2)}) copy-start(bf16[128,1024]{1,0:T(8,128)(2,1)} %key_ref.3) | copy-start | bytes 786436
  0.7 16.4 %copy-start.4 = (bf16[128,1024]{1,0:T(8,128)(2,1)S(1)}, bf16[128,1024]{1,0:T(8,128)(2,1)}, u32[]{:S(2)}) copy-start(bf16[128,1024]{1,0:T(8,128)(2,1)} %query_ref.3) | copy-start | bytes 786436
  2.1 8.0 %collective-permute-start.3 = (bf16[400,128]{1,0:T(8,128)(2,1)S(1)}, bf16[400,128]{1,0:T(8,128)(2,1)S(1)}, u32[]{:S(2)}, u32[]{:S(2)}) collective-permute-start(bf16[400,128]{1,0:T(8,128)(2,1)S(1)} %get-tuple-element.61), channel_id=1, source_target_pairs={{0,2},{2,0},{4,6},{6,4},{8,10},{10,8},{12,14},{14,12},{16,18},{18,... | collective-permute-start | bytes 307208 | tf_op jit(solution)/shard_map/ppermute | solution.py:437
  5.1 7.5 %collective-permute-start.4 = (bf16[400,128]{1,0:T(8,128)(2,1)S(1)}, bf16[400,128]{1,0:T(8,128)(2,1)S(1)}, u32[]{:S(2)}, u32[]{:S(2)}) collective-permute-start(bf16[400,128]{1,0:T(8,128)(2,1)S(1)} %get-tuple-element.62), channel_id=1, source_target_pairs={{0,4},{2,6},{4,0},{6,2},{8,12},{10,14},{12,8},{14,10},{16,20},{18,... | collective-permute-start | bytes 307208 | tf_op jit(solution)/shard_map/ppermute | solution.py:437
  6.7 7.1 %collective-permute-start.5 = (bf16[400,128]{1,0:T(8,128)(2,1)S(1)}, bf16[400,128]{1,0:T(8,128)(2,1)S(1)}, u32[]{:S(2)}, u32[]{:S(2)}) collective-permute-start(bf16[400,128]{1,0:T(8,128)(2,1)S(1)} %get-tuple-element.63), channel_id=1, source_target_pairs={{0,6},{2,4},{4,2},{6,0},{8,14},{10,12},{12,10},{14,8},{16,22},{18,... | collective-permute-start | bytes 307208 | tf_op jit(solution)/shard_map/ppermute | solution.py:437
  6.7 7.1 %collective-permute-start.6 = (bf16[400,128]{1,0:T(8,128)(2,1)S(1)}, bf16[400,128]{1,0:T(8,128)(2,1)S(1)}, u32[]{:S(2)}, u32[]{:S(2)}) collective-permute-start(bf16[400,128]{1,0:T(8,128)(2,1)S(1)} %get-tuple-element.64), channel_id=1, source_target_pairs={{0,8},{2,10},{4,12},{6,14},{8,0},{10,2},{12,4},{14,6},{16,24},{18,... | collective-permute-start | bytes 307208 | tf_op jit(solution)/shard_map/ppermute | solution.py:437
  8.7 10.5 %collective-permute-start = (bf16[400,128]{1,0:T(8,128)(2,1)S(1)}, bf16[400,128]{1,0:T(8,128)(2,1)S(1)}, u32[]{:S(2)}, u32[]{:S(2)}) collective-permute-start(bf16[400,128]{1,0:T(8,128)(2,1)S(1)} %get-tuple-element.56), channel_id=1, source_target_pairs={{0,10},{2,8},{4,14},{6,12},{8,2},{10,0},{12,6},{14,4},{16,26},{18,... | collective-permute-start | bytes 307208 | tf_op jit(solution)/shard_map/ppermute | solution.py:437
  10.1 9.1 %collective-permute-start.1 = (bf16[400,128]{1,0:T(8,128)(2,1)S(1)}, bf16[400,128]{1,0:T(8,128)(2,1)S(1)}, u32[]{:S(2)}, u32[]{:S(2)}) collective-permute-start(bf16[400,128]{1,0:T(8,128)(2,1)S(1)} %get-tuple-element.57), channel_id=1, source_target_pairs={{0,12},{2,14},{4,8},{6,10},{8,4},{10,6},{12,0},{14,2},{16,28},{18,... | collective-permute-start | bytes 307208 | tf_op jit(solution)/shard_map/ppermute | solution.py:437
  12.6 6.9 %collective-permute-start.2 = (bf16[400,128]{1,0:T(8,128)(2,1)S(1)}, bf16[400,128]{1,0:T(8,128)(2,1)S(1)}, u32[]{:S(2)}, u32[]{:S(2)}) collective-permute-start(bf16[400,128]{1,0:T(8,128)(2,1)S(1)} %get-tuple-element.58), channel_id=1, source_target_pairs={{0,14},{2,12},{4,10},{6,8},{8,6},{10,4},{12,2},{14,0},{16,30},{18,... | collective-permute-start | bytes 307208 | tf_op jit(solution)/shard_map/ppermute | solution.py:437
  22.5 18.7 %slice-start = ((s8[8388608]{0:T(1024)(128)(4,1)}), s8[4194304]{0:T(1024)(128)(4,1)S(1)}, s32[]{:S(2)}) async-start(s8[8388608]{0:T(1024)(128)(4,1)} %bitcast.7), calls=%async_computation.1 | async-start | bytes 8388608
  22.5 18.7 %slice-start.1 = ((s8[8388608]{0:T(1024)(128)(4,1)}), s8[4194304]{0:T(1024)(128)(4,1)S(1)}, s32[]{:S(2)}) async-start(s8[8388608]{0:T(1024)(128)(4,1)} %bitcast.7), calls=%async_computation.2 | async-start | bytes 8388608
  22.5 18.7 %copy-start = (bf16[128,2048]{1,0:T(8,128)(2,1)S(1)}, bf16[128,2048]{1,0:T(8,128)(2,1)}, u32[]{:S(2)}) copy-start(bf16[128,2048]{1,0:T(8,128)(2,1)} %gate_ref.1) | copy-start | bytes 1572868
  22.6 18.7 %copy-start.1 = (f32[128]{0:T(128)S(1)}, f32[128]{0:T(128)}, u32[]{:S(2)}) copy-start(f32[128]{0:T(128)} %param.14) | copy-start | bytes 1540
  22.6 6.7 %collective-permute-start.7 = (bf16[2,128,128]{2,1,0:T(8,128)(2,1)S(1)}, bf16[2,128,128]{2,1,0:T(8,128)(2,1)S(1)}, u32[]{:S(2)}, u32[]{:S(2)}) collective-permute-start(bf16[2,128,128]{2,1,0:T(8,128)(2,1)S(1)} %get-tuple-element.96), channel_id=1, source_target_pairs={{0,16},{2,18},{4,20},{6,22},{8,24},{10,26},{12,28},{14,30},{16,0},... | collective-permute-start | bytes 196616 | tf_op jit(solution)/shard_map/ppermute | solution.py:437
  42.5 1.6 %collective-permute-start.8 = (bf16[128,1024]{1,0:T(8,128)(2,1)S(1)}, bf16[128,1024]{1,0:T(8,128)(2,1)S(1)}, u32[]{:S(2)}, u32[]{:S(2)}) collective-permute-start(bf16[128,1024]{1,0:T(8,128)(2,1)S(1)} %get-tuple-element.106), channel_id=1, source_target_pairs={{0,1},{1,0},{2,3},{3,2},{4,5},{5,4},{6,7},{7,6},{8,9},{9,8},{10,11... | collective-permute-start | bytes 786440 | tf_op jit(solution)/shard_map/ppermute | solution.py:537
